TPU v7x, 32 devices: a whole 2x2x4 slice. The times are simulated.
32 devices in a mesh: ctx: 16 (over z, y, core), ch: 2 (over x).
Axes of the slice: x: 2, y: 2, z: 4, core: 2. Of those that a mesh axis runs over, the one named last changes fastest.
Arguments:
- streams: bfloat16 [8192, 3, 2048], P('ctx', None, 'ch'), may hold values from -6 to 6
- short_taps: float32 [3, 3, 2048], P(None, None, 'ch'), may hold values from -3 to 3
- filters: bfloat16 [8192, 2048], P('ctx', 'ch'), may hold values from -1 to 1, as said below
- skip_gain: float32 [2048], P('ch'), may hold values from 0.2 to 0.6
- out_weight: bfloat16 [2048, 4096], P('ch'), may hold values from -0.1875 to 0.1875
Outputs:
- output: bfloat16 [8192, 4096], P('ctx', 'ch')
Inputs may be any that keep to these rules, and one draw needn't show every extreme that they name: `filters`: filter taps of every channel and lag.
All inputs are finite; a program needn't handle non-finite values.
Results may differ from a plain program's by a relative error of at most 0.017.
Values may be sent and summed in bfloat16 or wider, within the bound.
No kernel may reach another device: no remote copies, remote signals or barrier semaphores. Data moves between devices by JAX's collectives and lax.ppermute only.
A program may use at most 192 MiB of HBM per device.

v0:
```python
import functools

import jax
import jax.numpy as jnp
import ml_dtypes
import numpy as np
from jax import lax
from jax.experimental import pallas as pl
from jax.experimental.pallas import tpu as pltpu
from jax.sharding import PartitionSpec as P

LANES = 128


def passed_along(value, axis, steps):
    count = lax.axis_size(axis)
    initial, last = (max(0, -steps), min(count, count - steps))
    return lax.ppermute(value, axis, [(source, source + steps) for source in range(initial, last)])


def paired_columns(half):
    order = np.arange(2 * half).reshape(2, half // LANES, LANES)
    return order.transpose(1, 0, 2).reshape(-1)


def head_table(size):
    half = size // 2
    rows = np.arange(half)[:, None]
    cols = np.arange(size)[None, :]
    freq = np.where(cols < half, cols, cols - half)
    angle = (rows * freq % size) * (2.0 * np.pi / size)
    nyquist = np.where(rows % 2 == 0, 1.0, -1.0)
    table = np.where(cols < half, np.cos(angle), np.where(cols == half, nyquist, -np.sin(angle)))
    return table[:, paired_columns(half)].astype(ml_dtypes.bfloat16)


def inverse_table(size):
    half = size // 2
    rows = np.arange(size)[:, None]
    places = half + np.arange(half)[None, :]
    freq = np.where(rows < half, rows, rows - half)
    angle = (places * freq % size) * (2.0 * np.pi / size)
    weight = np.where(freq == 0, 1.0, 2.0) / size
    nyquist = np.where(places % 2 == 0, 1.0, -1.0) / size
    table = np.where(
        rows < half, weight * np.cos(angle), np.where(rows == half, nyquist, -weight * np.sin(angle))
    )
    return table[paired_columns(half)].astype(ml_dtypes.bfloat16)


def call(kernel, in_specs, out_specs, outs, grid=(), scratch=(), megabytes=16, flops=0, moved=0, scalars=0):
    inner = pl.pallas_call(
        kernel,
        grid_spec=pltpu.PrefetchScalarGridSpec(
            num_scalar_prefetch=scalars,
            grid=grid,
            in_specs=in_specs,
            out_specs=out_specs,
            scratch_shapes=list(scratch),
        ),
        out_shape=[pltpu.HBM(shape, dtype) for shape, dtype in outs],
        compiler_params=pltpu.CompilerParams(vmem_limit_bytes=megabytes * 1024 * 1024),
        cost_estimate=pl.CostEstimate(flops=flops, bytes_accessed=moved, transcendentals=0),
    )

    def run(*args, free=()):
        pinned = [
            a if k < scalars or k in free else pltpu.with_memory_space_constraint(a, pltpu.HBM)
            for k, a in enumerate(args)
        ]
        return inner(*pinned)

    return run


def store_turned(value, o_ref, parts):
    count, held, rows = o_ref.shape
    step = held // parts
    tile = value.shape[1] // parts
    value = value.T
    for p in range(parts):
        piece = value[p * tile : (p + 1) * tile].reshape(count, step, rows)
        o_ref[:, p * step : (p + 1) * step] = piece.astype(o_ref.dtype)


def turn_kernel(parts, x_ref, s_ref, o_ref, tail_ref):
    tail_ref[...] = s_ref[:, s_ref.shape[1] - 2 :]
    store_turned(x_ref[...].astype(jnp.float32), o_ref, parts)


def turned(x, streams, count, parts):
    rows, chan = x.shape
    own = chan // count
    grid = min(parts, 2)
    last = min(rows, 16)
    tile = chan // grid
    return call(
        functools.partial(turn_kernel, parts // grid),
        [
            pl.BlockSpec((rows, tile), lambda p: (0, p)),
            pl.BlockSpec((3, last, tile), lambda p: (0, rows // last - 1, p)),
        ],
        [
            pl.BlockSpec((count, own // grid, rows), lambda p: (0, p, 0)),
            pl.BlockSpec((3, 2, tile), lambda p: (0, 0, p)),
        ],
        [((count, own, rows), x.dtype), ((3, 2, chan), streams.dtype)],
        grid=(grid,),
        moved=4 * rows * chan,
    )(x, streams)


def mix_kernel(parts, s_ref, e_ref, t_ref, turned_ref, outer_ref):
    rows, width = s_ref.shape[1:]
    place = lax.broadcasted_iota(jnp.int32, (rows, width), 0)

    def mixed(q):
        now = s_ref[q].astype(jnp.float32)
        edge = e_ref[q].astype(jnp.float32)
        one = jnp.where(place == 0, edge[1:2], pltpu.roll(now, 1, 0))
        two = jnp.where(
            place == 0, edge[0:1], jnp.where(place == 1, edge[1:2], pltpu.roll(now, 2, 0))
        )
        return t_ref[0, q : q + 1] * now + t_ref[1, q : q + 1] * one + t_ref[2, q : q + 1] * two

    outer_ref[...] = mixed(2).astype(outer_ref.dtype)
    store_turned(mixed(0) * mixed(1), turned_ref, parts)


def mix(streams, edges, taps, count, parts):
    _, rows, chan = streams.shape
    own = chan // count
    grid = min(parts, 2)
    tile = chan // grid
    return call(
        functools.partial(mix_kernel, parts // grid),
        [
            pl.BlockSpec((3, rows, tile), lambda p: (0, 0, p)),
            pl.BlockSpec((3, 2, tile), lambda p: (0, 0, p)),
            pl.BlockSpec((3, 3, tile), lambda p: (0, 0, p)),
        ],
        [
            pl.BlockSpec((count, own // grid, rows), lambda p: (0, p, 0)),
            pl.BlockSpec((rows, tile), lambda p: (0, p)),
        ],
        [((count, own, rows), jnp.bfloat16), ((rows, chan), jnp.bfloat16)],
        grid=(grid,),
        megabytes=32,
        moved=10 * rows * chan,
    )(streams, edges, taps)


def filter_kernel(own, f_ref, table_ref, real_ref, imag_ref):
    spectrum = jnp.dot(f_ref[...], table_ref[...], preferred_element_type=jnp.float32)
    lane = lax.broadcasted_iota(jnp.int32, spectrum.shape, 1)
    nyquist = (pl.program_id(0) == 0) & (lane == LANES)
    signed = jnp.where((lane % 2 == 0) | nyquist, spectrum, -spectrum)
    earlier = jnp.concatenate([jnp.zeros((own, 2 * LANES), jnp.float32), spectrum[:-own]], axis=0)
    window = (earlier + signed).astype(jnp.bfloat16).astype(jnp.float32)
    real_ref[...] = window[:, :LANES]
    imag_ref[...] = window[:, LANES:]


def filter_spectra(blocks, table):
    count, own, rows = blocks.shape
    height = count * own
    plane = ((height, rows), jnp.float32)
    spec = pl.BlockSpec((height, LANES), lambda f: (0, f))
    return call(
        functools.partial(filter_kernel, own),
        [
            pl.BlockSpec((height, rows), lambda f: (0, 0)),
            pl.BlockSpec((rows, 2 * LANES), lambda f: (0, f)),
        ],
        [spec, spec],
        [plane, plane],
        grid=(rows // LANES,),
        flops=4 * height * rows * rows,
        moved=height * rows * 10,
    )(blocks.reshape(height, rows), table)


def conv_kernel(low, x_ref, head_ref, real_ref, imag_ref, back_ref, skip_ref, o_ref, *scratch):
    head_buf, real_buf, imag_buf, back_buf, spec_ref, low_ref, sems = scratch
    count, _, part, rows = o_ref.shape
    high = min(part, 16)
    group = 2
    some = pl.ds(low, part)
    pairs = [
        (head_ref, head_buf),
        (real_ref.at[:, some], real_buf),
        (imag_ref.at[:, some], imag_buf),
        (back_ref, back_buf),
    ]
    copies = [pltpu.make_async_copy(a, b, sems.at[i]) for i, (a, b) in enumerate(pairs)]
    for copy in copies:
        copy.start()
    copies[0].wait()
    x = x_ref[:, low : low + part]
    blocks = x.reshape(count * part, rows)
    spec_ref[...] = jnp.dot(blocks, head_buf[...], preferred_element_type=jnp.float32)
    for copy in copies[1:]:
        copy.wait()
    lane = lax.broadcasted_iota(jnp.int32, (high, LANES), 1)
    slabs = part // high

    def one_slab(turn, carry):
        tile = turn // slabs
        base = pl.multiple_of((turn % slabs) * high, high)
        column = pl.ds(pl.multiple_of(tile * LANES, LANES), LANES)
        reals = pl.ds(pl.multiple_of(tile * 2 * LANES, LANES), LANES)
        imags = pl.ds(pl.multiple_of(tile * 2 * LANES + LANES, LANES), LANES)
        first = (lane == 0) & (tile == 0)
        for start in range(0, count, group):
            sums = [[None] * 3 for _ in range(group)]
            factors = {}
            for source in range(start + group):
                place = pl.ds(base + source * part, high)
                real, imag = (spec_ref[place, reals], spec_ref[place, imags])
                for g in range(group):
                    lag = start + g - source
                    if lag < 0:
                        continue
                    if lag not in factors:
                        place = pl.ds(base, high)
                        factors[lag] = (real_buf[lag, place, column], imag_buf[lag, place, column])
                    a, b = factors[lag]
                    terms = (real * a, imag * b, real * b + imag * a)
                    before = sums[g]
                    sums[g] = [t if p is None else p + t for p, t in zip(before, terms)]
            for g in range(group):
                rr, ii, ri = sums[g]
                place = pl.ds(base + (start + g) * part, high)
                low_ref[place, reals] = jnp.where(first, rr, rr - ii).astype(low_ref.dtype)
                low_ref[place, imags] = jnp.where(first, ii, ri).astype(low_ref.dtype)
        return carry

    lax.fori_loop(0, slabs * (rows // LANES), one_slab, 0)
    back = jnp.dot(
        low_ref[...].astype(jnp.bfloat16), back_buf[...], preferred_element_type=jnp.float32
    )
    value = back.reshape(count, part, rows)
    value = value + skip_ref[low : low + part, :1][None] * x_ref[:, low : low + part].astype(jnp.float32)
    for copy in range(o_ref.shape[1]):
        o_ref[:, copy] = value.astype(o_ref.dtype)


def long_conv(blocks, head, planes, back, skip, low, part, copies=1):
    count, own, rows = blocks.shape
    height = count * part
    return call(
        functools.partial(conv_kernel, low),
        [pl.BlockSpec(memory_space=pltpu.VMEM)]
        + [pl.BlockSpec(memory_space=pl.ANY)] * 4
        + [pl.BlockSpec(memory_space=pltpu.VMEM)],
        [pl.BlockSpec(memory_space=pltpu.VMEM)],
        [((count, copies, part, rows), jnp.bfloat16)],
        scratch=[
            pltpu.VMEM(head.shape, jnp.bfloat16),
            pltpu.VMEM((count, part, rows), jnp.float32),
            pltpu.VMEM((count, part, rows), jnp.float32),
            pltpu.VMEM(back.shape, jnp.bfloat16),
            pltpu.VMEM((height, 2 * rows), jnp.float32),
            pltpu.VMEM((height, 2 * rows), jnp.float32 if part % 16 else jnp.bfloat16),
            pltpu.SemaphoreType.DMA((4,)),
        ],
        megabytes=28,
        flops=8 * height * rows * rows,
        moved=height * rows * 16,
    )(blocks, head, *[p.reshape(count, own, rows) for p in planes], back, skip, free=(0,))[0]


def gated_part(long, outer, p):
    count, step, rows = long.shape
    value = long.reshape(count * step, rows).T.astype(jnp.float32)
    tile = count * step
    return (outer[:, p * tile : (p + 1) * tile].astype(jnp.float32) * value).astype(jnp.bfloat16)


def gate_kernel(long_ref, outer_ref, o_ref):
    step = long_ref.shape[1] // 2
    tile = o_ref.shape[1] // 2
    for p in range(2):
        long = long_ref[:, p * step : (p + 1) * step]
        o_ref[:, p * tile : (p + 1) * tile] = gated_part(long, outer_ref, p)


def gate(long, outer):
    rows = outer.shape[0]
    width = long.shape[0] * long.shape[1]
    return call(
        gate_kernel,
        [
            pl.BlockSpec(long.shape, lambda n: (0, 0, 0)),
            pl.BlockSpec((rows, width), lambda n: (0, 0)),
        ],
        [pl.BlockSpec((rows, width), lambda n: (0, 0))],
        [((rows, width), jnp.bfloat16)],
        grid=(1,),
        moved=6 * rows * width,
    )(long, outer, free=(0,))[0]


def own_kernel(here_ref, gated_ref, weight_ref, o_ref):
    value = jnp.dot(gated_ref[...], weight_ref[...], preferred_element_type=jnp.float32)
    o_ref[...] = value.astype(o_ref.dtype)


def own_term(here, gated, out_weight, cols):
    rows, used = gated.shape
    wide = cols // 2
    return call(
        own_kernel,
        [
            pl.BlockSpec((rows, used), lambda n, h: (0, 0)),
            pl.BlockSpec((used, wide), lambda n, h: (0, h[0] * 2 + n)),
        ],
        [pl.BlockSpec((rows, wide), lambda n, h: (0, n))],
        [((rows, cols), jnp.bfloat16)],
        grid=(2,),
        flops=2 * rows * used * cols,
        moved=rows * cols * 2 + used * cols * 2,
        scalars=1,
    )(here, gated, out_weight)[0]


def last_kernel(
    place_ref, sent_ref, dealt_ref, sum_ref, mine_ref, theirs_ref, near_ref, far_ref, weight_ref, o_ref, *scratch
):
    outer_buf, weight_buf, block_buf, sum_buf, out_buf, gated_ref, sems = scratch
    here, core = (place_ref[0], place_ref[1])
    rows, used = outer_buf.shape[1:]
    wide = out_buf.shape[2]
    cols = 4 * wide
    pairs = [(mine_ref.at[:, pl.ds(used, used)], outer_buf.at[0]), (theirs_ref, outer_buf.at[1])]
    gates = [pltpu.make_async_copy(a, b, sems.at[g]) for g, (a, b) in enumerate(pairs)]
    for copy in gates:
        copy.start()
    places, inputs = ([], [])
    for k in range(4):
        source, side = ((near_ref, core), (far_ref, 1 - core))[k // 2]
        inside = k % 2 * wide
        column = pl.multiple_of(side * 2 * wide + inside, wide)
        places.append(pl.ds(column, wide))
        ours = pl.multiple_of(here * cols + column, wide)
        pairs = [
            (source.at[:, pl.ds(inside, wide)], block_buf.at[k]),
            (weight_ref.at[pl.ds(used, used), pl.ds(ours, wide)], weight_buf.at[k]),
            (sum_ref.at[:, places[k]], sum_buf.at[k]),
        ]
        inputs.append(
            [pltpu.make_async_copy(a, b, sems.at[2 + 3 * k + i]) for i, (a, b) in enumerate(pairs)]
        )
        for copy in inputs[k]:
            copy.start()
    tile = used // 2
    step = dealt_ref.shape[2] // 2
    for g in range(2):
        gates[g].wait()
        long = dealt_ref[:, here if g == 0 else 1 - here]
        for p in range(2):
            gated_ref[g, :, p * tile : (p + 1) * tile] = gated_part(
                long[:, p * step : (p + 1) * step], outer_buf.at[g], p
            )
    outputs = []
    for k in range(4):
        for copy in inputs[k]:
            copy.wait()
        value = sum_buf[k].astype(jnp.float32)
        for left, right in (
            (sent_ref[...], block_buf[k, :used]),
            (gated_ref[1], block_buf[k, used:]),
            (gated_ref[0], weight_buf[k]),
        ):
            value = value + jnp.dot(left, right, preferred_element_type=jnp.float32)
        out_buf[k] = value.astype(out_buf.dtype)
        outputs.append(pltpu.make_async_copy(out_buf.at[k], o_ref.at[:, places[k]], sems.at[14 + k]))
        outputs[k].start()
    for copy in outputs:
        copy.wait()


def last_term(place, sent, dealt, total, mine, theirs, near, far, out_weight):
    rows, cols = total.shape
    chan = near.shape[0]
    wide = cols // 4
    used = chan // 2
    vmem, anywhere = (pl.BlockSpec(memory_space=pltpu.VMEM), pl.BlockSpec(memory_space=pl.ANY))
    bf16 = jnp.bfloat16
    return call(
        last_kernel,
        [pl.BlockSpec(memory_space=pltpu.SMEM), vmem, vmem] + [anywhere] * 6,
        [anywhere],
        [((rows, cols), bf16)],
        scratch=[
            pltpu.VMEM((2, rows, used), bf16),
            pltpu.VMEM((4, used, wide), bf16),
            pltpu.VMEM((4, chan, wide), bf16),
            pltpu.VMEM((4, rows, wide), bf16),
            pltpu.VMEM((4, rows, wide), bf16),
            pltpu.VMEM((2, rows, used), bf16),
            pltpu.SemaphoreType.DMA((18,)),
        ],
        megabytes=32,
        flops=24 * rows * used * wide,
        moved=rows * wide * 16 + used * wide * 24,
    )(place, sent, dealt, total, mine, theirs, near, far, out_weight, free=(0, 1, 2))[0]


def exchanged(value):
    return lax.all_to_all(value, "ctx", 0, 0, tiled=True)


def to_groups(values):
    groups = lax.axis_size("ch")
    return [
        lax.ppermute(value, "ch", [(g, (g + s) % groups) for g in range(groups)])
        for s, value in enumerate(values, 1)
    ]


def any_groups(long, outer, out_weight):
    rows, chan = outer.shape
    groups = lax.axis_size("ch")
    here = lax.axis_index("ch")
    cols = out_weight.shape[1] // groups
    gated = gated_part(long, outer, 0)
    total = jnp.zeros((rows, cols), jnp.float32)
    weights = [
        lax.dynamic_slice(out_weight, (0, (here + s) % groups * cols), (chan, cols))
        for s in range(groups)
    ]
    values = [gated] + to_groups([gated] * (groups - 1))
    for value, weight in zip(values, weights[:1] + to_groups(weights[1:])):
        total = total + jnp.dot(value, weight, preferred_element_type=jnp.float32)
    return total.astype(jnp.bfloat16)


def local(streams, short_taps, filters, skip_gain, out_weight):
    rows, _, chan = streams.shape
    count = lax.axis_size("ctx")
    groups = lax.axis_size("ch")
    own = chan // count
    fast = groups == 2 and count % 2 == 0 and own % 64 == 0
    parts = 4 if fast else 1
    step = own // parts
    after = lax.optimization_barrier
    position, here = (lax.axis_index("ctx"), lax.axis_index("ch"))
    head = jnp.asarray(head_table(2 * rows))
    back = jnp.asarray(inverse_table(2 * rows))
    skip = lax.dynamic_index_in_dim(skip_gain.reshape(parts, count, step), position, 1, False)
    skip = jnp.broadcast_to(skip.reshape(own, 1), (own, LANES))
    streams = streams.transpose(1, 0, 2)
    turned_filters, tail = turned(filters, streams, count, parts)
    edges = passed_along(tail, "ctx", 1)
    turned_filters, edges = after((turned_filters, edges))
    filter_blocks = exchanged(turned_filters)
    cols = out_weight.shape[1] // groups
    if fast:
        half = cols // 2
        columns = (1 - here) * cols + position % 2 * half
        near = lax.dynamic_slice(out_weight, (0, columns), (chan, half))
        near, edges = after((near, edges))
    edges, skip = after((edges, skip))
    turned_inner, outer = mix(streams, edges, short_taps, count, parts)
    turned_inner, filter_blocks = after((turned_inner, filter_blocks))
    inner_blocks = exchanged(turned_inner)
    planes = filter_spectra(filter_blocks, head)
    if not fast:
        long = exchanged(long_conv(inner_blocks, head, planes, back, skip, 0, own)[:, 0])
        return any_groups(long, outer, out_weight)
    near, theirs = to_groups([near])[0], to_groups([outer[:, chan // 2 :]])[0]
    planes, near = after((planes, near))
    inner_blocks, near = after((inner_blocks, near))
    far = lax.ppermute(near, "ctx", [(i, i ^ 1) for i in range(count)])
    early = long_conv(inner_blocks, head, planes, back, skip, 0, 2 * step)[:, 0]
    inner_blocks, early = after((inner_blocks, early))
    late = long_conv(inner_blocks, head, planes, back, skip, 2 * step, 2 * step, copies=groups)
    early, late, far, theirs = after((exchanged(early), late, far, theirs))
    gated = gate(early, outer)
    sent = to_groups([gated])[0]
    dealt = lax.all_to_all(
        late.reshape(count * groups, 2 * step, rows), ("ctx", "ch"), 0, 0, tiled=True
    )
    dealt = dealt.reshape(count, groups, 2 * step, rows)
    total = own_term(here[None], gated, out_weight, cols)
    place = jnp.stack([here, position % 2])
    return last_term(place, sent, dealt, total, outer, theirs, near, far, out_weight)


def solution(mesh):
    return jax.shard_map(
        local,
        mesh=mesh,
        in_specs=(
            P("ctx", None, "ch"),
            P(None, None, "ch"),
            P("ctx", "ch"),
            P("ch"),
            P("ch", None),
        ),
        out_specs=P("ctx", "ch"),
        check_vma=False,
    )
```

profile of v0, /device:TPU:0, one launch (start us, length us, event | category | flops | bytes accessed | tf_op | source)
XLA Modules:
  0.0 136.9 jit_solution(8220453095871776127)
XLA Ops:
  0.0 2.3 %shard_map.73 = (bf16[16,64,512]{2,1,0:T(8,128)(2,1)}, bf16[3,2,1024]{2,1,0:T(2,128)(2,1)}) custom-call(bf16[512,1024]{1,0:T(8,128)(2,1)} %x_ref.1, bf16[3,512,1024]{2,1,0:T(8,128)(2,1)} %bitcast.10), custom_call_target="tpu_custom_call" | custom-call | bytes 2097152 | tf_op jit(solution)/shard_map/pallas_call | solution.py:71
  2.3 2.3 %collective-permute-start = (bf16[3,2,1024]{2,1,0:T(2,128)(2,1)}, bf16[3,2,1024]{2,1,0:T(2,128)(2,1)S(1)}, u32[]{:S(2)}, u32[]{:S(2)}) collective-permute-start(bf16[3,2,1024]{2,1,0:T(2,128)(2,1)} %get-tuple-element.31), channel_id=1, source_target_pairs={{0,2},{2,4},{4,6},{6,8},{8,10},{10,12},{12,14},{14,16},{16,18},{18... | collective-permute-start | bytes 36872 | tf_op jit(solution)/shard_map/ppermute | solution.py:18
  4.6 1.0 collective-permute-done.e_ref
  5.7 9.2 %all-to-all-start = ((bf16[16,64,512]{2,1,0:T(8,128)(2,1)}), bf16[16,64,512]{2,1,0:T(8,128)(2,1)S(1)}, u32[]{:S(2)}, u32[]{:S(2)}) async-start(bf16[16,64,512]{2,1,0:T(8,128)(2,1)} %get-tuple-element.36), calls=%async_computation | async-start | bytes 2097152 | tf_op jit(solution)/shard_map/all_to_all | solution.py:411
  14.9 0.0 copy-start.4
  14.9 1.8 %constant_dynamic-slice_fusion = bf16[1024,1024]{1,0:T(8,128)(2,1)S(1)} fusion(bf16[1024,4096]{1,0:T(8,128)(2,1)} %weight_ref.3, s32[]{:T(128)S(6)} %select_n.17), kind=kLoop, calls=%fused_computation.2 | loop fusion | bytes 4194308 | tf_op jit(solution)/shard_map/dynamic_slice | solution.py:462
  16.7 1.6 %collective-permute-start.1 = (bf16[1024,1024]{1,0:T(8,128)(2,1)S(1)}, bf16[1024,1024]{1,0:T(8,128)(2,1)}, u32[]{:S(2)}, u32[]{:S(2)}) collective-permute-start(bf16[1024,1024]{1,0:T(8,128)(2,1)S(1)} %constant_dynamic-slice_fusion), channel_id=1, source_target_pairs={{0,1},{1,0},{2,3},{3,2},{4,5},{5,4},{6,7},{7,6},{8,9},{9,8},{10,11... | collective-permute-start | bytes 6291464 | tf_op jit(solution)/shard_map/ppermute | solution.py:417
  18.3 0.1 reshape.23
  18.4 0.1 broadcast_in_dim.8
  18.5 0.7 broadcast_in_dim.9.skip_ref
  19.2 5.8 %shard_map.74 = (bf16[16,64,512]{2,1,0:T(8,128)(2,1)}, bf16[512,1024]{1,0:T(8,128)(2,1)}) custom-call(bf16[3,512,1024]{2,1,0:T(8,128)(2,1)} %bitcast.11, bf16[3,2,1024]{2,1,0:T(2,128)(2,1)} %copy-done.3, f32[3,3,1024]{2,1,0:T(4,128)} %t_ref.1), custom_call_target="tpu_custom_call" | custom-call | bytes 5242880 | tf_op jit(solution)/shard_map/pallas_call | solution.py:71
  25.0 12.9 %all-to-all-done = bf16[16,64,512]{2,1,0:T(8,128)(2,1)S(1)} async-done(((bf16[16,64,512]{2,1,0:T(8,128)(2,1)}), bf16[16,64,512]{2,1,0:T(8,128)(2,1)S(1)}, u32[]{:S(2)}, u32[]{:S(2)}) %all-to-all-start) | async-done | bytes 1048608 | tf_op jit(solution)/shard_map/all_to_all | solution.py:411
  37.8 1.0 copy-done.1
  38.8 6.9 %all-to-all-start.1 = ((bf16[16,64,512]{2,1,0:T(8,128)(2,1)}), bf16[16,64,512]{2,1,0:T(8,128)(2,1)S(1)}, u32[]{:S(2)}, u32[]{:S(2)}) async-start(bf16[16,64,512]{2,1,0:T(8,128)(2,1)} %get-tuple-element.37), calls=%async_computation.1 | async-start | bytes 2097152 | tf_op jit(solution)/shard_map/all_to_all | solution.py:411
  45.7 5.2 %shard_map.75 = (f32[1024,512]{1,0:T(8,128)}, f32[1024,512]{1,0:T(8,128)}) custom-call(bf16[1024,512]{1,0:T(8,128)(2,1)} %bitcast.18, bf16[512,1024]{1,0:T(8,128)(2,1)} %constant.40.clone.table_ref.head_ref), custom_call_target="tpu_custom_call" | custom-call | flops 1073741824 | bytes 5242880 | tf_op jit(solution)/shard_map/pallas_call | solution.py:71
  51.0 13.8 %collective-permute-done.1.near_ref = bf16[1024,1024]{1,0:T(8,128)(2,1)} collective-permute-done((bf16[1024,1024]{1,0:T(8,128)(2,1)S(1)}, bf16[1024,1024]{1,0:T(8,128)(2,1)}, u32[]{:S(2)}, u32[]{:S(2)}) %collective-permute-start.1) | collective-permute-done | bytes 2097184 | tf_op jit(solution)/shard_map/ppermute | solution.py:417
  64.8 3.9 %all-to-all-done.1.x_ref = bf16[16,64,512]{2,1,0:T(8,128)(2,1)S(1)} async-done(((bf16[16,64,512]{2,1,0:T(8,128)(2,1)}), bf16[16,64,512]{2,1,0:T(8,128)(2,1)S(1)}, u32[]{:S(2)}, u32[]{:S(2)}) %all-to-all-start.1) | async-done | bytes 1048608 | tf_op jit(solution)/shard_map/all_to_all | solution.py:411
  68.6 0.6 collective-permute-start.2
  69.3 7.5 %shard_map.76 = bf16[16,1,32,512]{3,2,1,0:T(8,128)(2,1)} custom-call(bf16[16,64,512]{2,1,0:T(8,128)(2,1)S(1)} %all-to-all-done.1.x_ref, bf16[512,1024]{1,0:T(8,128)(2,1)} %constant.40.clone.table_ref.head_ref, f32[16,64,512]{2,1,0:T(8,128)} %bitcast.12, f32[16,64,512]{2,1,0:T(8,128)} %bitcast.14, bf16[1024,512]{1,0:T(8,128)(2,1)} %constant.41.clone.back_ref, ...), custom_call_target="tpu_custom_call" | custom-call | flops 1073741824 | bytes 4194304 | tf_op jit(solution)/shard_map/pallas_call | solution.py:71
  76.8 6.6 %all-to-all-start.2 = ((bf16[16,32,512]{2,1,0:T(8,128)(2,1)}), bf16[16,32,512]{2,1,0:T(8,128)(2,1)S(1)}, u32[]{:S(2)}, u32[]{:S(2)}) async-start(bf16[16,32,512]{2,1,0:T(8,128)(2,1)} %bitcast.17), calls=%async_computation.2 | async-start | bytes 1048576 | tf_op jit(solution)/shard_map/all_to_all | solution.py:411
  83.4 1.6 %collective-permute-start.3 = (bf16[512,512]{1,0:T(8,128)(2,1)S(1)}, bf16[512,512]{1,0:T(8,128)(2,1)S(1)}, u32[]{:S(2)}, u32[]{:S(2)}) collective-permute-start(bf16[512,512]{1,0:T(8,128)(2,1)S(1)} %slice.3), channel_id=1, source_target_pairs={{0,1},{1,0},{2,3},{3,2},{4,5},{5,4},{6,7},{7,6},{8,9},{9,8},{10,11... | collective-permute-start | bytes 1572872 | tf_op jit(solution)/shard_map/ppermute | solution.py:417
  85.0 7.6 %shard_map.77 = bf16[16,2,32,512]{3,2,1,0:T(8,128)(2,1)} custom-call(bf16[16,64,512]{2,1,0:T(8,128)(2,1)S(1)} %all-to-all-done.1.x_ref, bf16[512,1024]{1,0:T(8,128)(2,1)} %constant.40.clone.table_ref.head_ref, f32[16,64,512]{2,1,0:T(8,128)} %bitcast.13, f32[16,64,512]{2,1,0:T(8,128)} %bitcast.15, bf16[1024,512]{1,0:T(8,128)(2,1)} %constant.41.clone.back_ref, ...), custom_call_target="tpu_custom_call" | custom-call | flops 1073741824 | bytes 4194304 | tf_op jit(solution)/shard_map/pallas_call | solution.py:71
  92.6 5.1 %collective-permute-done.3.theirs_ref = bf16[512,512]{1,0:T(8,128)(2,1)S(1)} collective-permute-done((bf16[512,512]{1,0:T(8,128)(2,1)S(1)}, bf16[512,512]{1,0:T(8,128)(2,1)S(1)}, u32[]{:S(2)}, u32[]{:S(2)}) %collective-permute-start.3) | collective-permute-done | bytes 524320 | tf_op jit(solution)/shard_map/ppermute | solution.py:417
  97.7 0.1 all-to-all-done.2.long_ref
  97.8 5.6 %all-to-all-start.3 = ((bf16[32,32,512]{2,1,0:T(8,128)(2,1)}), bf16[32,32,512]{2,1,0:T(8,128)(2,1)S(1)}, u32[]{:S(2)}, u32[]{:S(2)}) async-start(bf16[32,32,512]{2,1,0:T(8,128)(2,1)} %bitcast.16), calls=%async_computation.3 | async-start | bytes 2097152 | tf_op jit(solution)/shard_map/all_to_all | solution.py:482
  103.4 2.1 %shard_map.78.gated_ref = bf16[512,512]{1,0:T(8,128)(2,1)} custom-call(bf16[16,32,512]{2,1,0:T(8,128)(2,1)S(1)} %all-to-all-done.2.long_ref, bf16[512,1024]{1,0:T(8,128)(2,1)} %get-tuple-element.50.outer_ref.mine_ref), custom_call_target="tpu_custom_call" | custom-call | bytes 1572864 | tf_op jit(solution)/shard_map/pallas_call | solution.py:71
  105.5 1.8 %collective-permute-start.4 = (bf16[512,512]{1,0:T(8,128)(2,1)}, bf16[512,512]{1,0:T(8,128)(2,1)S(1)}, u32[]{:S(2)}, u32[]{:S(2)}) collective-permute-start(bf16[512,512]{1,0:T(8,128)(2,1)} %shard_map.78.gated_ref), channel_id=1, source_target_pairs={{0,1},{1,0},{2,3},{3,2},{4,5},{5,4},{6,7},{7,6},{8,9},{9,8},{10,11... | collective-permute-start | bytes 1572872 | tf_op jit(solution)/shard_map/ppermute | solution.py:417
  107.2 0.1 pad_add_fusion.place_ref
  107.3 3.8 %shard_map.79.sum_ref = bf16[512,2048]{1,0:T(8,128)(2,1)} custom-call(s32[1]{0:T(128)} %bitcast.here_ref, bf16[512,512]{1,0:T(8,128)(2,1)} %shard_map.78.gated_ref, bf16[1024,4096]{1,0:T(8,128)(2,1)} %weight_ref.3), custom_call_target="tpu_custom_call" | custom-call | flops 1073741824 | bytes 4194304 | tf_op jit(solution)/shard_map/pallas_call | solution.py:71
  111.1 17.2 %collective-permute-done.4.sent_ref = bf16[512,512]{1,0:T(8,128)(2,1)S(1)} collective-permute-done((bf16[512,512]{1,0:T(8,128)(2,1)}, bf16[512,512]{1,0:T(8,128)(2,1)S(1)}, u32[]{:S(2)}, u32[]{:S(2)}) %collective-permute-start.4) | collective-permute-done | bytes 524320 | tf_op jit(solution)/shard_map/ppermute | solution.py:417
  128.4 1.3 all-to-all-done.3
  129.6 7.3 %shard_map.80 = bf16[512,2048]{1,0:T(8,128)(2,1)} custom-call(s32[2]{0:T(128)S(1)} %pad_add_fusion.place_ref, bf16[512,512]{1,0:T(8,128)(2,1)S(1)} %collective-permute-done.4.sent_ref, bf16[16,2,32,512]{3,2,1,0:T(8,128)(2,1)S(1)} %bitcast.9, bf16[512,2048]{1,0:T(8,128)(2,1)} %shard_map.79.sum_ref, bf16[512,1024]{1,0:T(8,128)(2,1)} %get-tuple-element.50.outer_ref.mine_ref, ...), custom_call_target="tpu_custom_call" | custom-call | flops 3221225472 | bytes 10485760 | tf_op jit(solution)/shard_map/pallas_call | solution.py:71
  (11 shorter events, 0.1 us)
Async XLA Ops:
  2.3 3.4 %collective-permute-start = (bf16[3,2,1024]{2,1,0:T(2,128)(2,1)}, bf16[3,2,1024]{2,1,0:T(2,128)(2,1)S(1)}, u32[]{:S(2)}, u32[]{:S(2)}) collective-permute-start(bf16[3,2,1024]{2,1,0:T(2,128)(2,1)} %get-tuple-element.31), channel_id=1, source_target_pairs={{0,2},{2,4},{4,6},{6,8},{8,10},{10,12},{12,14},{14,16},{16,18},{18... | collective-permute-start | bytes 36872 | tf_op jit(solution)/shard_map/ppermute | solution.py:18
  5.7 11.0 %copy-start.3 = (bf16[3,2,1024]{2,1,0:T(2,128)(2,1)}, bf16[3,2,1024]{2,1,0:T(2,128)(2,1)S(1)}, u32[]{:S(2)}) copy-start(bf16[3,2,1024]{2,1,0:T(2,128)(2,1)S(1)} %collective-permute-done.e_ref) | copy-start | bytes 36868
  5.7 32.2 %all-to-all-start = ((bf16[16,64,512]{2,1,0:T(8,128)(2,1)}), bf16[16,64,512]{2,1,0:T(8,128)(2,1)S(1)}, u32[]{:S(2)}, u32[]{:S(2)}) async-start(bf16[16,64,512]{2,1,0:T(8,128)(2,1)} %get-tuple-element.36), calls=%async_computation | async-start | bytes 2097152 | tf_op jit(solution)/shard_map/all_to_all | solution.py:411
  14.9 3.4 %copy-start.4 = (f32[1024]{0:T(1024)S(1)}, f32[1024]{0:T(1024)}, u32[]{:S(2)}) copy-start(f32[1024]{0:T(1024)} %param.10) | copy-start | bytes 12292
  16.7 48.1 %collective-permute-start.1 = (bf16[1024,1024]{1,0:T(8,128)(2,1)S(1)}, bf16[1024,1024]{1,0:T(8,128)(2,1)}, u32[]{:S(2)}, u32[]{:S(2)}) collective-permute-start(bf16[1024,1024]{1,0:T(8,128)(2,1)S(1)} %constant_dynamic-slice_fusion), channel_id=1, source_target_pairs={{0,1},{1,0},{2,3},{3,2},{4,5},{5,4},{6,7},{7,6},{8,9},{9,8},{10,11... | collective-permute-start | bytes 6291464 | tf_op jit(solution)/shard_map/ppermute | solution.py:417
  37.8 1.0 copy-start.1
  38.8 29.8 %all-to-all-start.1 = ((bf16[16,64,512]{2,1,0:T(8,128)(2,1)}), bf16[16,64,512]{2,1,0:T(8,128)(2,1)S(1)}, u32[]{:S(2)}, u32[]{:S(2)}) async-start(bf16[16,64,512]{2,1,0:T(8,128)(2,1)} %get-tuple-element.37), calls=%async_computation.1 | async-start | bytes 2097152 | tf_op jit(solution)/shard_map/all_to_all | solution.py:411
  68.6 29.2 %collective-permute-start.2 = (bf16[1024,1024]{1,0:T(8,128)(2,1)}, bf16[1024,1024]{1,0:T(8,128)(2,1)}, u32[]{:S(2)}, u32[]{:S(2)}) collective-permute-start(bf16[1024,1024]{1,0:T(8,128)(2,1)} %collective-permute-done.1.near_ref), channel_id=1, source_target_pairs={{0,2},{2,0},{4,6},{6,4},{8,10},{10,8},{12,14},{14,12},{16,18},{18,... | collective-permute-start | bytes 6291464 | tf_op jit(solution)/shard_map/ppermute | solution.py:475
  69.3 14.1 %copy-start = (bf16[512,1024]{1,0:T(8,128)(2,1)S(1)}, bf16[512,1024]{1,0:T(8,128)(2,1)}, u32[]{:S(2)}) copy-start(bf16[512,1024]{1,0:T(8,128)(2,1)} %get-tuple-element.50.outer_ref.mine_ref) | copy-start | bytes 3145732
  76.8 21.0 %all-to-all-start.2 = ((bf16[16,32,512]{2,1,0:T(8,128)(2,1)}), bf16[16,32,512]{2,1,0:T(8,128)(2,1)S(1)}, u32[]{:S(2)}, u32[]{:S(2)}) async-start(bf16[16,32,512]{2,1,0:T(8,128)(2,1)} %bitcast.17), calls=%async_computation.2 | async-start | bytes 1048576 | tf_op jit(solution)/shard_map/all_to_all | solution.py:411
  83.4 14.3 %collective-permute-start.3 = (bf16[512,512]{1,0:T(8,128)(2,1)S(1)}, bf16[512,512]{1,0:T(8,128)(2,1)S(1)}, u32[]{:S(2)}, u32[]{:S(2)}) collective-permute-start(bf16[512,512]{1,0:T(8,128)(2,1)S(1)} %slice.3), channel_id=1, source_target_pairs={{0,1},{1,0},{2,3},{3,2},{4,5},{5,4},{6,7},{7,6},{8,9},{9,8},{10,11... | collective-permute-start | bytes 1572872 | tf_op jit(solution)/shard_map/ppermute | solution.py:417
  97.7 7.7 %copy-start.2 = (bf16[512,512]{1,0:T(8,128)(2,1)}, bf16[512,512]{1,0:T(8,128)(2,1)S(1)}, u32[]{:S(2)}) copy-start(bf16[512,512]{1,0:T(8,128)(2,1)S(1)} %collective-permute-done.3.theirs_ref) | copy-start | bytes 1572868
  97.8 31.8 %all-to-all-start.3 = ((bf16[32,32,512]{2,1,0:T(8,128)(2,1)}), bf16[32,32,512]{2,1,0:T(8,128)(2,1)S(1)}, u32[]{:S(2)}, u32[]{:S(2)}) async-start(bf16[32,32,512]{2,1,0:T(8,128)(2,1)} %bitcast.16), calls=%async_computation.3 | async-start | bytes 2097152 | tf_op jit(solution)/shard_map/all_to_all | solution.py:482
  105.5 22.9 %collective-permute-start.4 = (bf16[512,512]{1,0:T(8,128)(2,1)}, bf16[512,512]{1,0:T(8,128)(2,1)S(1)}, u32[]{:S(2)}, u32[]{:S(2)}) collective-permute-start(bf16[512,512]{1,0:T(8,128)(2,1)} %shard_map.78.gated_ref), channel_id=1, source_target_pairs={{0,1},{1,0},{2,3},{3,2},{4,5},{5,4},{6,7},{7,6},{8,9},{9,8},{10,11... | collective-permute-start | bytes 1572872 | tf_op jit(solution)/shard_map/ppermute | solution.py:417
where the time goes:
time: 138 us; the launch traced here: 137 us
  waiting for transfers between devices  55.3 us (40%)
  Pallas kernels  41.7 us (30%)
  starting transfers between devices  36.1 us (26%)
  local copies, waits for them, and re-layouts  3.7 us (3%)
    pallas_call x8, Pallas kernels, run(): return inner(*pinned)  41.7 us
    ppermute x3, waiting for transfers between devices, to_groups(): lax.ppermute(value, 'ch', [(g, (g + s) % groups) for g in range(groups)])  36.2 us
    all_to_all x3, starting transfers between devices, exchanged(): return lax.all_to_all(value, 'ctx', 0, 0, tiled=True)  22.7 us
    all_to_all x3, waiting for transfers between devices, exchanged(): return lax.all_to_all(value, 'ctx', 0, 0, tiled=True)  16.8 us
    all_to_all x1, starting transfers between devices, local(): lax.all_to_all(late.reshape(count * groups, 2 * step, rows), ('ctx', 'ch'...  5.56 us
    ppermute x3, starting transfers between devices, to_groups(): lax.ppermute(value, 'ch', [(g, (g + s) % groups) for g in range(groups)])  4.9 us
  transfers between devices with their start and end apart: 9, of which 8 were waited for; matrix products, arithmetic and copies ran while one was open for 2% of the time, Pallas kernels for 23%

commit v1 on v0

v1 whole, which is shorter than its diff:
```python
import functools

import jax
import jax.numpy as jnp
import ml_dtypes
import numpy as np
from jax import lax
from jax.experimental import pallas as pl
from jax.experimental.pallas import tpu as pltpu
from jax.sharding import PartitionSpec as P

LANES = 128


def passed_along(value, axis, steps):
    count = lax.axis_size(axis)
    initial, last = (max(0, -steps), min(count, count - steps))
    return lax.ppermute(value, axis, [(source, source + steps) for source in range(initial, last)])


def paired_columns(half):
    order = np.arange(2 * half).reshape(2, half // LANES, LANES)
    return order.transpose(1, 0, 2).reshape(-1)


def head_table(size):
    half = size // 2
    rows = np.arange(half)[:, None]
    cols = np.arange(size)[None, :]
    freq = np.where(cols < half, cols, cols - half)
    angle = (rows * freq % size) * (2.0 * np.pi / size)
    nyquist = np.where(rows % 2 == 0, 1.0, -1.0)
    table = np.where(cols < half, np.cos(angle), np.where(cols == half, nyquist, -np.sin(angle)))
    return table[:, paired_columns(half)].astype(ml_dtypes.bfloat16)


def inverse_table(size):
    half = size // 2
    rows = np.arange(size)[:, None]
    places = half + np.arange(half)[None, :]
    freq = np.where(rows < half, rows, rows - half)
    angle = (places * freq % size) * (2.0 * np.pi / size)
    weight = np.where(freq == 0, 1.0, 2.0) / size
    nyquist = np.where(places % 2 == 0, 1.0, -1.0) / size
    table = np.where(
        rows < half, weight * np.cos(angle), np.where(rows == half, nyquist, -weight * np.sin(angle))
    )
    return table[paired_columns(half)].astype(ml_dtypes.bfloat16)


def call(kernel, in_specs, out_specs, outs, grid=(), scratch=(), megabytes=16, flops=0, moved=0, scalars=0, aliases=None):
    inner = pl.pallas_call(
        kernel,
        grid_spec=pltpu.PrefetchScalarGridSpec(
            num_scalar_prefetch=scalars,
            grid=grid,
            in_specs=in_specs,
            out_specs=out_specs,
            scratch_shapes=list(scratch),
        ),
        out_shape=[pltpu.HBM(shape, dtype) for shape, dtype in outs],
        input_output_aliases=aliases or {},
        compiler_params=pltpu.CompilerParams(vmem_limit_bytes=megabytes * 1024 * 1024),
        cost_estimate=pl.CostEstimate(flops=flops, bytes_accessed=moved, transcendentals=0),
    )

    def run(*args, free=()):
        pinned = [
            a if k < scalars or k in free else pltpu.with_memory_space_constraint(a, pltpu.HBM)
            for k, a in enumerate(args)
        ]
        return inner(*pinned)

    return run


def store_turned(value, o_ref):
    o_ref[...] = value.T.reshape(o_ref.shape).astype(o_ref.dtype)


def turn_kernel(x_ref, s_ref, o_ref, tail_ref):
    tail_ref[...] = s_ref[:, s_ref.shape[1] - 2 :]
    store_turned(x_ref[...].astype(jnp.float32), o_ref)


def turned(x, streams, count, parts):
    rows, chan = x.shape
    own = chan // count
    last = min(rows, 16)
    tile = chan // parts
    return call(
        turn_kernel,
        [
            pl.BlockSpec((rows, tile), lambda p: (0, p)),
            pl.BlockSpec((3, last, tile), lambda p: (0, rows // last - 1, p)),
        ],
        [
            pl.BlockSpec((count, 1, own // parts, rows), lambda p: (0, 0, p, 0)),
            pl.BlockSpec((3, 2, tile), lambda p: (0, 0, p)),
        ],
        [((count, 2, own, rows), x.dtype), ((3, 2, chan), streams.dtype)],
        grid=(parts,),
        moved=4 * rows * chan,
    )(x, streams)


def mixed(s_ref, e_ref, t_ref, q):
    rows, width = s_ref.shape[1:]
    place = lax.broadcasted_iota(jnp.int32, (8, width), 0)
    now = s_ref[q].astype(jnp.float32)
    edge = e_ref[q].astype(jnp.float32)
    one, two = (pltpu.roll(now, 1, 0), pltpu.roll(now, 2, 0))
    one_top = jnp.where(place == 0, edge[1:2], one[:8])
    two_top = jnp.where(place == 0, edge[0:1], jnp.where(place == 1, edge[1:2], two[:8]))
    one = jnp.concatenate([one_top, one[8:]], axis=0)
    two = jnp.concatenate([two_top, two[8:]], axis=0)
    return t_ref[0, q : q + 1] * now + t_ref[1, q : q + 1] * one + t_ref[2, q : q + 1] * two


def inner_kernel(s_ref, e_ref, t_ref, _, o_ref):
    store_turned(mixed(s_ref, e_ref, t_ref, 0) * mixed(s_ref, e_ref, t_ref, 1), o_ref)


def with_inner(both, streams, edges, taps, parts):
    count, _, own, rows = both.shape
    chan = count * own
    tile = chan // parts
    return call(
        inner_kernel,
        [
            pl.BlockSpec((2, rows, tile), lambda p: (0, 0, p)),
            pl.BlockSpec((3, 2, tile), lambda p: (0, 0, p)),
            pl.BlockSpec((3, 3, tile), lambda p: (0, 0, p)),
            pl.BlockSpec(memory_space=pl.ANY),
        ],
        [pl.BlockSpec((count, 1, own // parts, rows), lambda p: (0, 1, p, 0))],
        [(both.shape, both.dtype)],
        grid=(parts,),
        megabytes=32,
        moved=6 * rows * chan,
        aliases={3: 0},
    )(streams, edges, taps, both)[0]


def outer_kernel(s_ref, e_ref, t_ref, o_ref):
    o_ref[...] = mixed(s_ref, e_ref, t_ref, 0).astype(o_ref.dtype)


def outer_gate(streams, which, edges, taps, parts):
    _, rows, chan = streams.shape
    tile = chan // parts
    return call(
        outer_kernel,
        [
            pl.BlockSpec((1, rows, tile), lambda p: (which, 0, p)),
            pl.BlockSpec((1, 2, tile), lambda p: (0, 0, p)),
            pl.BlockSpec((3, 1, tile), lambda p: (0, 0, p)),
        ],
        [pl.BlockSpec((rows, tile), lambda p: (0, p))],
        [((rows, chan), jnp.bfloat16)],
        grid=(parts,),
        megabytes=32,
        moved=4 * rows * chan,
    )(streams, edges, taps)[0]


def deal_kernel(f_ref, s_ref, t_ref, o_ref, f_buf, s_buf, tail_buf, sems):
    count, height, rows = o_ref.shape
    step = (height - 8) // 4
    chan = f_ref.shape[1]
    tile = chan // 2
    last = tail_buf.shape[0]
    per = LANES // step
    copies = [
        pltpu.make_async_copy(f_ref.at[:, pl.ds(p * tile, tile)], f_buf.at[p], sems.at[2 * p])
        for p in range(2)
    ] + [
        pltpu.make_async_copy(
            s_ref.at[pl.ds(0, 2), :, pl.ds(p * tile, tile)], s_buf.at[p], sems.at[2 * p + 1]
        )
        for p in range(2)
    ]
    copies.append(
        pltpu.make_async_copy(s_ref.at[2, pl.ds(rows - last, last)], tail_buf, sems.at[4])
    )
    for k in (0, 2, 1, 3, 4):
        copies[k].start()
    for p in range(2):
        start = p * 2 * step
        lanes = slice(p * tile, (p + 1) * tile)
        copies[p].wait()
        value = f_buf[p].astype(jnp.float32).T.reshape(count, step, rows)
        o_ref[:, start : start + step] = value.astype(o_ref.dtype)
        copies[2 + p].wait()
        both = []
        for q in range(2):
            now = s_buf[p, q].astype(jnp.float32)
            value = t_ref[0, q : q + 1, lanes] * now
            value = value + t_ref[1, q : q + 1, lanes] * pltpu.roll(now, 1, 0)
            both.append(value + t_ref[2, q : q + 1, lanes] * pltpu.roll(now, 2, 0))
        value = (both[0] * both[1]).T.reshape(count, step, rows)
        o_ref[:, start + step : start + 2 * step] = value.astype(o_ref.dtype)
        ends = [s_buf[p, q, a : a + 2].astype(jnp.float32) for a in (0, rows - 2) for q in range(2)]
        ends = jnp.concatenate(ends, axis=0).astype(o_ref.dtype)
        for g in range(tile // LANES):
            value = ends[:, g * LANES : (g + 1) * LANES]
            o_ref[g * per : (g + 1) * per, 4 * step :, p * LANES : (p + 1) * LANES] = (
                jnp.broadcast_to(value[None], (per, 8, LANES))
            )
    copies[4].wait()
    tail = tail_buf[last - 2 :].astype(jnp.float32)
    wide = chan // 4
    tail = jnp.concatenate(
        [tail[t : t + 1, q * wide : (q + 1) * wide] for t in range(2) for q in range(4)], axis=0
    ).astype(o_ref.dtype)
    o_ref[:, 4 * step :, 2 * LANES : 2 * LANES + wide] = jnp.broadcast_to(
        tail[None], (count, 8, wide)
    )


def deal(filters, streams, taps, count):
    rows, chan = filters.shape
    height = 2 * chan // count + 8
    anywhere, vmem = (pl.BlockSpec(memory_space=pl.ANY), pl.BlockSpec(memory_space=pltpu.VMEM))
    bf16 = jnp.bfloat16
    return call(
        deal_kernel,
        [anywhere, anywhere, vmem],
        [vmem],
        [((count, height, rows), bf16)],
        scratch=[
            pltpu.VMEM((2, rows, chan // 2), bf16),
            pltpu.VMEM((2, 2, rows, chan // 2), bf16),
            pltpu.VMEM((16, chan), bf16),
            pltpu.SemaphoreType.DMA((5,)),
        ],
        megabytes=32,
        moved=10 * rows * chan,
    )(filters, streams, taps)[0]


def first_tokens(ends, taps, place):
    count = ends.shape[0]

    def at(row):
        return ends[:, row].astype(jnp.float32)

    block = lax.broadcasted_iota(jnp.int32, (count, LANES), 0)

    def before(row):
        return jnp.where(block == 0, 0.0, pltpu.roll(at(row), 1, 0))

    values = [1.0, 1.0]
    for q in range(2):
        t0, t1, t2 = (taps[2 * m + q : 2 * m + q + 1] for m in range(3))
        one, two = (at(2 * q), at(2 * q + 1))
        far, near = (before(4 + 2 * q), before(5 + 2 * q))
        values[0] = values[0] * (t0 * one + t1 * near + t2 * far)
        values[1] = values[1] * (t0 * two + t1 * one + t2 * near)
    rest = jnp.zeros((LANES - 2 * count, LANES), jnp.float32)
    return jnp.concatenate(values + [rest], axis=0).T


def conv_kernel(split, place_ref, both_ref, head_ref, back_ref, skip_ref, taps_ref, o_ref, *scratch):
    head_buf, back_buf, spec_ref, factor_ref, low_ref, x_buf, fix_ref, sems = scratch
    count, _, part, rows = o_ref.shape
    high = min(part, 16)
    group = 2
    low = 2 * part * (split or 0)
    pairs = [(head_ref, head_buf), (back_ref, back_buf)]
    copies = [pltpu.make_async_copy(a, b, sems.at[i]) for i, (a, b) in enumerate(pairs)]
    for copy in copies:
        copy.start()
    x_buf[...] = both_ref[:, low + part : low + 2 * part]
    if split is not None:
        ends = both_ref[:, 4 * part :, split * LANES : (split + 1) * LANES]
        fix_ref[...] = first_tokens(ends, taps_ref[split], place_ref[0])
        mine = fix_ref[pl.ds(pl.multiple_of(place_ref[0] * part, part), part), :]
        lane = lax.broadcasted_iota(jnp.int32, (part, LANES), 1)
        for block in range(count):
            one = pltpu.roll(mine, (LANES - block) % LANES, 1)
            two = pltpu.roll(mine, (LANES - block - count + 1) % LANES, 1)
            value = x_buf[block, :, :LANES].astype(jnp.float32)
            value = jnp.where(lane == 0, one, jnp.where(lane == 1, two, value))
            x_buf[block, :, :LANES] = value.astype(x_buf.dtype)
    copies[0].wait()
    for ref, blocks in ((factor_ref, both_ref[:, low : low + part]), (spec_ref, x_buf[...])):
        blocks = blocks.reshape(count * part, rows)
        ref[...] = jnp.dot(blocks, head_buf[...], preferred_element_type=jnp.float32)
    column = lax.broadcasted_iota(jnp.int32, (part, 2 * rows), 1)
    sign = jnp.where(column % 2 == 0, 1.0, -1.0)

    def one_window(turn, carry):
        block = count - 1 - turn
        place = pl.ds(pl.multiple_of(block * part, part), part)
        before = pl.ds(pl.multiple_of(jnp.maximum(block - 1, 0) * part, part), part)
        earlier = jnp.where(block > 0, factor_ref[before, :], 0.0)
        factor_ref[place, :] = earlier + sign * factor_ref[place, :]
        return carry

    lax.fori_loop(0, count, one_window, 0)
    lane = lax.broadcasted_iota(jnp.int32, (high, LANES), 1)
    slabs = part // high

    def one_slab(turn, carry):
        tile = turn // slabs
        base = pl.multiple_of((turn % slabs) * high, high)
        reals = pl.ds(pl.multiple_of(tile * 2 * LANES, LANES), LANES)
        imags = pl.ds(pl.multiple_of(tile * 2 * LANES + LANES, LANES), LANES)
        first = (lane == 0) & (tile == 0)
        for start in range(0, count, group):
            sums = [[None] * 3 for _ in range(group)]
            factors = {}
            for source in range(start + group):
                place = pl.ds(base + source * part, high)
                real, imag = (spec_ref[place, reals], spec_ref[place, imags])
                for g in range(group):
                    lag = start + g - source
                    if lag < 0:
                        continue
                    if lag not in factors:
                        place = pl.ds(base + lag * part, high)
                        factors[lag] = (factor_ref[place, reals], factor_ref[place, imags])
                    a, b = factors[lag]
                    terms = (real * a, imag * b, real * b + imag * a)
                    before = sums[g]
                    sums[g] = [t if p is None else p + t for p, t in zip(before, terms)]
            for g in range(group):
                rr, ii, ri = sums[g]
                place = pl.ds(base + (start + g) * part, high)
                low_ref[place, reals] = jnp.where(first, rr, rr - ii).astype(low_ref.dtype)
                low_ref[place, imags] = jnp.where(first, ii, ri).astype(low_ref.dtype)
        return carry

    lax.fori_loop(0, slabs * (rows // LANES), one_slab, 0)
    copies[1].wait()
    back = jnp.dot(
        low_ref[...].astype(jnp.bfloat16), back_buf[...], preferred_element_type=jnp.float32
    )
    value = back.reshape(count, part, rows)
    skip = skip_ref[low // 2 : low // 2 + part, :1][None]
    value = value + skip * x_buf[...].astype(jnp.float32)
    for copy in range(o_ref.shape[1]):
        o_ref[:, copy] = value.astype(o_ref.dtype)


def long_conv(both, head, back, skip, taps, place, split, copies=1):
    count, _, rows = both.shape
    own = skip.shape[0]
    part = own if split is None else own // 2
    height = count * part
    vmem, anywhere = (pl.BlockSpec(memory_space=pltpu.VMEM), pl.BlockSpec(memory_space=pl.ANY))
    return call(
        functools.partial(conv_kernel, split),
        [pl.BlockSpec(memory_space=pltpu.SMEM), vmem, anywhere, anywhere, vmem, vmem],
        [vmem],
        [((count, copies, part, rows), jnp.bfloat16)],
        scratch=[
            pltpu.VMEM(head.shape, jnp.bfloat16),
            pltpu.VMEM(back.shape, jnp.bfloat16),
            pltpu.VMEM((height, 2 * rows), jnp.float32),
            pltpu.VMEM((height, 2 * rows), jnp.float32),
            pltpu.VMEM((height, 2 * rows), jnp.float32 if part % 16 else jnp.bfloat16),
            pltpu.VMEM((count, part, rows), jnp.bfloat16),
            pltpu.VMEM((LANES, LANES), jnp.float32),
            pltpu.SemaphoreType.DMA((2,)),
        ],
        megabytes=28,
        flops=12 * height * rows * rows,
        moved=height * rows * 8,
    )(place, both, head, back, skip, taps, free=(0, 1))[0]


def gated_part(long, outer, first):
    count, step, rows = long.shape
    value = long.reshape(count * step, rows).T.astype(jnp.float32)
    outer = outer.astype(jnp.float32)
    outer = jnp.concatenate([outer[:8] + first, outer[8:]], axis=0)
    return (outer * value).astype(jnp.bfloat16)


def gate_kernel(long_ref, outer_ref, first_ref, o_ref):
    o_ref[...] = gated_part(long_ref[...], outer_ref[...], first_ref[...])


def gate(long, outer, first):
    rows = outer.shape[0]
    width = long.shape[0] * long.shape[1]
    return call(
        gate_kernel,
        [
            pl.BlockSpec(long.shape, lambda n: (0, 0, 0)),
            pl.BlockSpec((rows, width), lambda n: (0, 0)),
            pl.BlockSpec((8, width), lambda n: (0, 0)),
        ],
        [pl.BlockSpec((rows, width), lambda n: (0, 0))],
        [((rows, width), jnp.bfloat16)],
        grid=(1,),
        moved=6 * rows * width,
    )(long, outer, first, free=(0,))[0]


def own_kernel(here_ref, gated_ref, weight_ref, o_ref):
    value = jnp.dot(gated_ref[...], weight_ref[...], preferred_element_type=jnp.float32)
    o_ref[...] = value.astype(o_ref.dtype)


def own_term(here, gated, out_weight, cols):
    rows, used = gated.shape
    wide = cols // 2
    return call(
        own_kernel,
        [
            pl.BlockSpec((rows, used), lambda n, h: (0, 0)),
            pl.BlockSpec((used, wide), lambda n, h: (0, h[0] * 2 + n)),
        ],
        [pl.BlockSpec((rows, wide), lambda n, h: (0, n))],
        [((rows, cols), jnp.bfloat16)],
        grid=(2,),
        flops=2 * rows * used * cols,
        moved=rows * cols * 2 + used * cols * 2,
        scalars=1,
    )(here, gated, out_weight)[0]


def last_kernel(
    place_ref, sent_ref, dealt_ref, first_ref, sum_ref, mine_ref, theirs_ref, *refs
):
    blocks, (weight_ref, o_ref, *scratch) = (refs[:4], refs[4:])
    outer_buf, weight_buf, block_buf, sum_buf, out_buf, gated_ref, sems = scratch
    here, quarter = (place_ref[0], place_ref[1])
    rows, used = outer_buf.shape[1:]
    wide = out_buf.shape[2]
    cols = 4 * wide
    pairs = [(mine_ref.at[:, pl.ds(used, used)], outer_buf.at[0]), (theirs_ref, outer_buf.at[1])]
    gates = [pltpu.make_async_copy(a, b, sems.at[g]) for g, (a, b) in enumerate(pairs)]
    for copy in gates:
        copy.start()
    places, inputs = ([], [])
    for k in range(4):
        column = pl.multiple_of((quarter ^ k) * wide, wide)
        places.append(pl.ds(column, wide))
        ours = pl.multiple_of(here * cols + column, wide)
        pairs = [
            (blocks[k], block_buf.at[k]),
            (weight_ref.at[pl.ds(used, used), pl.ds(ours, wide)], weight_buf.at[k]),
            (sum_ref.at[:, places[k]], sum_buf.at[k]),
        ]
        inputs.append(
            [pltpu.make_async_copy(a, b, sems.at[2 + 3 * k + i]) for i, (a, b) in enumerate(pairs)]
        )
        for copy in inputs[k]:
            copy.start()
    for g in range(2):
        gates[g].wait()
        long = dealt_ref[:, here if g == 0 else 1 - here]
        gated_ref[g] = gated_part(long, outer_buf[g], first_ref[g])
    outputs = []
    for k in range(4):
        for copy in inputs[k]:
            copy.wait()
        value = sum_buf[k].astype(jnp.float32)
        for left, right in (
            (sent_ref[...], block_buf[k, :used]),
            (gated_ref[1], block_buf[k, used:]),
            (gated_ref[0], weight_buf[k]),
        ):
            value = value + jnp.dot(left, right, preferred_element_type=jnp.float32)
        out_buf[k] = value.astype(out_buf.dtype)
        outputs.append(pltpu.make_async_copy(out_buf.at[k], o_ref.at[:, places[k]], sems.at[14 + k]))
        outputs[k].start()
    for copy in outputs:
        copy.wait()


def last_term(place, sent, dealt, first, total, mine, theirs, blocks, out_weight):
    rows, cols = total.shape
    chan = mine.shape[1]
    wide = cols // 4
    used = chan // 2
    vmem, anywhere = (pl.BlockSpec(memory_space=pltpu.VMEM), pl.BlockSpec(memory_space=pl.ANY))
    bf16 = jnp.bfloat16
    return call(
        last_kernel,
        [pl.BlockSpec(memory_space=pltpu.SMEM), vmem, vmem, vmem] + [anywhere] * 8,
        [anywhere],
        [((rows, cols), bf16)],
        scratch=[
            pltpu.VMEM((2, rows, used), bf16),
            pltpu.VMEM((4, used, wide), bf16),
            pltpu.VMEM((4, chan, wide), bf16),
            pltpu.VMEM((4, rows, wide), bf16),
            pltpu.VMEM((4, rows, wide), bf16),
            pltpu.VMEM((2, rows, used), bf16),
            pltpu.SemaphoreType.DMA((18,)),
        ],
        megabytes=32,
        flops=24 * rows * used * wide,
        moved=rows * wide * 16 + used * wide * 24,
    )(place, sent, dealt, first, total, mine, theirs, *blocks, out_weight, free=(0, 1, 2, 3))[0]


def exchanged(value):
    return lax.all_to_all(value, "ctx", 0, 0, tiled=True)


def to_groups(values):
    groups = lax.axis_size("ch")
    return [
        lax.ppermute(value, "ch", [(g, (g + s) % groups) for g in range(groups)])
        for s, value in enumerate(values, 1)
    ]


def any_groups(long, outer, out_weight):
    rows, chan = outer.shape
    groups = lax.axis_size("ch")
    here = lax.axis_index("ch")
    cols = out_weight.shape[1] // groups
    gated = gated_part(long, outer, jnp.zeros((8, chan), jnp.float32))
    total = jnp.zeros((rows, cols), jnp.float32)
    weights = [
        lax.dynamic_slice(out_weight, (0, (here + s) % groups * cols), (chan, cols))
        for s in range(groups)
    ]
    values = [gated] + to_groups([gated] * (groups - 1))
    for value, weight in zip(values, weights[:1] + to_groups(weights[1:])):
        total = total + jnp.dot(value, weight, preferred_element_type=jnp.float32)
    return total.astype(jnp.bfloat16)


def local(streams, short_taps, filters, skip_gain, out_weight):
    rows, _, chan = streams.shape
    count = lax.axis_size("ctx")
    groups = lax.axis_size("ch")
    own = chan // count
    step = own // 2
    fast = groups == 2 and count % 4 == 0 and own % 32 == 0 and LANES % step == 0
    fast = fast and chan // 4 + 2 * LANES <= rows and 2 * count <= LANES
    after = lax.optimization_barrier
    position, here = (lax.axis_index("ctx"), lax.axis_index("ch"))
    head = jnp.asarray(head_table(2 * rows))
    back = jnp.asarray(inverse_table(2 * rows))
    streams = streams.transpose(1, 0, 2)
    parts = 2 if fast else 1
    skip = skip_gain.reshape(parts, count, own // parts)
    skip = lax.dynamic_index_in_dim(skip, position, 1, False)
    skip = jnp.broadcast_to(skip.reshape(own, 1), (own, LANES))
    if not fast:
        both, tail = turned(filters, streams, count, parts)
        edges = passed_along(tail, "ctx", 1)
        both = exchanged(with_inner(both, streams, edges, short_taps, parts))
        both = both.reshape(count, 2 * own, rows)
        outer = outer_gate(streams, 2, edges[2:], short_taps[:, 2:], parts)
        none = jnp.zeros((2, 8, LANES), jnp.float32)
        long = long_conv(both, head, back, skip, none, jnp.zeros((1,), jnp.int32), None)
        return any_groups(exchanged(long[:, 0]), outer, out_weight)
    per = LANES // step
    place = (position % per)[None]
    taps = short_taps[:, :2].reshape(6, 2, chan // 2)
    taps = lax.dynamic_slice(taps, (0, 0, position // per * LANES), (6, 2, LANES))
    taps = jnp.pad(taps.transpose(1, 0, 2), ((0, 0), (0, 2), (0, 0)))
    both = exchanged(deal(filters, streams, short_taps, count))
    cols = out_weight.shape[1] // groups
    wide = cols // 4
    columns = (1 - here) * cols + position % 4 * wide
    near = lax.dynamic_slice(out_weight, (0, columns), (chan, wide))
    near, skip, taps = after((near, skip, taps))
    near = to_groups([near])[0]
    none = jnp.zeros((1, 2, chan), jnp.float32)
    none, near = after((none, near))
    outer = outer_gate(streams, 2, none, short_taps[:, 2:], 2)
    theirs = to_groups([outer[:, chan // 2 :]])[0]

    def swapped(value, bit):
        return lax.ppermute(value, "ctx", [(i, i ^ bit) for i in range(count)])

    across = swapped(near, 2)
    early = long_conv(both, head, back, skip, taps, place, 0)[:, 0]
    edges = lax.dynamic_slice(
        both, (jnp.maximum(position - 1, 0), 4 * step, 2 * LANES), (1, 8, chan // 4)
    )
    edges = jnp.where(position == 0, 0.0, edges.reshape(2, chan).astype(jnp.float32))
    first = jnp.stack(
        [short_taps[1, 2] * edges[1] + short_taps[2, 2] * edges[0], short_taps[2, 2] * edges[1]]
    )
    first = jnp.pad(first, ((0, 6), (0, 0)))
    other = to_groups([first[:, chan // 2 :]])[0]
    both, across, theirs, _ = after((both, across, theirs, early))
    blocks = [near, swapped(near, 1), across, swapped(across, 1)]
    late = long_conv(both, head, back, skip, taps, place, 1, copies=groups)
    early, late, blocks, other, first = after((exchanged(early), late, blocks, other, first))
    gated = gate(early, outer, first)
    sent = to_groups([gated])[0]
    dealt = lax.all_to_all(
        late.reshape(count * groups, step, rows), ("ctx", "ch"), 0, 0, tiled=True
    )
    dealt = dealt.reshape(count, groups, step, rows)
    total = own_term(here[None], gated, out_weight, cols)
    place = jnp.stack([here, position % 4])
    first = jnp.stack([first[:, chan // 2 :], other])
    return last_term(place, sent, dealt, first, total, outer, theirs, blocks, out_weight)


def solution(mesh):
    return jax.shard_map(
        local,
        mesh=mesh,
        in_specs=(
            P("ctx", None, "ch"),
            P(None, None, "ch"),
            P("ctx", "ch"),
            P("ch"),
            P("ch", None),
        ),
        out_specs=P("ctx", "ch"),
        check_vma=False,
    )
```

time: 138 us -> 132 us (0.957)
  starting transfers between devices: 36.1 us -> 26 us
  waiting for transfers between devices: 55.3 us -> 60.2 us
  Pallas kernels: 41.7 us -> 39.4 us
  local copies, waits for them, and re-layouts: 3.7 us -> 5.13 us
    all_to_all x3 -> x2, starting transfers between devices: 22.7 us -> 14 us  [exchanged(): return lax.all_to_all(value, 'ctx', 0, 0, tiled=True)]
    all_to_all x3 -> x2, waiting for transfers between devices: 16.8 us -> 10.6 us  [exchanged(): return lax.all_to_all(value, 'ctx', 0, 0, tiled=True)]
    ppermute x2 -> x3, waiting for transfers between devices: 1.03 us -> 7.08 us  [swapped(): return lax.ppermute(value, 'ctx', [(i, i ^ bit) for i in range(count)])]
    ppermute x3 -> x4, waiting for transfers between devices: 36.2 us -> 41.3 us  [to_groups(): lax.ppermute(value, 'ch', [(g, (g + s) % groups) for g in range(groups)])]
    pallas_call x8 -> x7, Pallas kernels: 41.7 us -> 39.4 us  [run(): return inner(*pinned)]
    slice x1 -> x5, local copies, waits for them, and re-layouts: 0.04 us -> 1.7 us  [the longest x1 1.08 us: local(): theirs = to_groups([outer[:, chan // 2:]])[0]]
    all_to_all x1, starting transfers between devices: 5.56 us -> 4.01 us  [local(): lax.all_to_all(late.reshape(count * groups, step, rows), ('ctx', 'ch'), 0...]
    ppermute x3 -> x4, starting transfers between devices: 4.9 us -> 6.37 us  [to_groups(): lax.ppermute(value, 'ch', [(g, (g + s) % groups) for g in range(groups)])]
  transfers between devices with their start and end apart: 9 -> 10, of which waited for: 8 -> 6; matrix products, arithmetic and copies ran while one was open for 2% -> 4% of each run, Pallas kernels for 23% -> 20%
where the time goes in v1:
time: 132 us; the launch traced here: 131 us
  waiting for transfers between devices  60.2 us (46%)
  Pallas kernels  39.4 us (30%)
  starting transfers between devices  26 us (20%)
  local copies, waits for them, and re-layouts  5.13 us (4%)
    ppermute x4, waiting for transfers between devices, to_groups(): lax.ppermute(value, 'ch', [(g, (g + s) % groups) for g in range(groups)])  41.3 us
    pallas_call x7, Pallas kernels, run(): return inner(*pinned)  39.4 us
    all_to_all x2, starting transfers between devices, exchanged(): return lax.all_to_all(value, 'ctx', 0, 0, tiled=True)  14 us
    all_to_all x2, waiting for transfers between devices, exchanged(): return lax.all_to_all(value, 'ctx', 0, 0, tiled=True)  10.6 us
    ppermute x3, waiting for transfers between devices, swapped(): return lax.ppermute(value, 'ctx', [(i, i ^ bit) for i in range(count)])  7.08 us
    ppermute x4, starting transfers between devices, to_groups(): lax.ppermute(value, 'ch', [(g, (g + s) % groups) for g in range(groups)])  6.37 us
    all_to_all x1, starting transfers between devices, local(): lax.all_to_all(late.reshape(count * groups, step, rows), ('ctx', 'ch'), 0...  4.01 us
  transfers between devices with their start and end apart: 10, of which 6 were waited for; matrix products, arithmetic and copies ran while one was open for 4% of the time, Pallas kernels for 20%

profile of v1, /device:TPU:0, one launch (start us, length us, event | category | flops | bytes accessed | tf_op | source)
XLA Modules:
  0.0 131.2 jit_solution(16107847473373663325)
XLA Ops:
  0.0 5.7 %shard_map.73 = bf16[16,136,512]{2,1,0:T(8,128)(2,1)} custom-call(bf16[512,1024]{1,0:T(8,128)(2,1)} %f_ref.1, bf16[3,512,1024]{2,1,0:T(8,128)(2,1)} %bitcast.28, f32[3,3,1024]{2,1,0:T(4,128)} %t_ref.1), custom_call_target="tpu_custom_call" | custom-call | bytes 5242880 | tf_op jit(solution)/shard_map/pallas_call | solution.py:72
  5.7 0.0 copy-start.4
  5.7 0.0 slice-start
  5.7 7.4 %all-to-all-start = ((bf16[16,136,512]{2,1,0:T(8,128)(2,1)}), bf16[16,136,512]{2,1,0:T(8,128)(2,1)S(1)}, u32[]{:S(2)}, u32[]{:S(2)}) async-start(bf16[16,136,512]{2,1,0:T(8,128)(2,1)} %shard_map.73), calls=%async_computation | async-start | bytes 4456448 | tf_op jit(solution)/shard_map/all_to_all | solution.py:504
  13.2 0.1 reshape.25
  13.3 0.1 broadcast_in_dim.16
  13.5 0.6 pad.8.taps_ref
  14.1 1.3 constant_dynamic-slice_fusion.1
  15.4 0.7 broadcast_in_dim.17.skip_ref
  16.0 1.5 %collective-permute-start = (bf16[1024,512]{1,0:T(8,128)(2,1)S(1)}, bf16[1024,512]{1,0:T(8,128)(2,1)}, u32[]{:S(2)}, u32[]{:S(2)}) collective-permute-start(bf16[1024,512]{1,0:T(8,128)(2,1)S(1)} %constant_dynamic-slice_fusion.1), channel_id=1, source_target_pairs={{0,1},{1,0},{2,3},{3,2},{4,5},{5,4},{6,7},{7,6},{8,9},{9,8},{10,11... | collective-permute-start | bytes 3145736 | tf_op jit(solution)/shard_map/ppermute | solution.py:510
  17.5 24.1 %collective-permute-done.refs_0_ = bf16[1024,512]{1,0:T(8,128)(2,1)} collective-permute-done((bf16[1024,512]{1,0:T(8,128)(2,1)S(1)}, bf16[1024,512]{1,0:T(8,128)(2,1)}, u32[]{:S(2)}, u32[]{:S(2)}) %collective-permute-start) | collective-permute-done | bytes 1048608 | tf_op jit(solution)/shard_map/ppermute | solution.py:510
  41.6 1.6 %collective-permute-start.1 = (bf16[1024,512]{1,0:T(8,128)(2,1)}, bf16[1024,512]{1,0:T(8,128)(2,1)}, u32[]{:S(2)}, u32[]{:S(2)}) collective-permute-start(bf16[1024,512]{1,0:T(8,128)(2,1)} %collective-permute-done.refs_0_), channel_id=1, source_target_pairs={{0,4},{2,6},{4,0},{6,2},{8,12},{10,14},{12,8},{14,10},{16,20},{18,... | collective-permute-start | bytes 3145736 | tf_op jit(solution)/shard_map/ppermute | solution.py:576
  43.3 0.6 slice.36.t_ref
  43.9 0.6 broadcast_in_dim.18.e_ref
  44.5 2.6 %shard_map.75.outer_ref.mine_ref = bf16[512,1024]{1,0:T(8,128)(2,1)} custom-call(bf16[3,512,1024]{2,1,0:T(8,128)(2,1)} %bitcast.29, f32[1,2,1024]{2,1,0:T(2,128)} %broadcast_in_dim.18.e_ref, f32[3,1,1024]{2,1,0:T(1,128)} %slice.36.t_ref), custom_call_target="tpu_custom_call" | custom-call | bytes 2097152 | tf_op jit(solution)/shard_map/pallas_call | solution.py:72
  47.1 1.1 slice.46
  48.2 1.6 %collective-permute-start.2 = (bf16[512,512]{1,0:T(8,128)(2,1)S(1)}, bf16[512,512]{1,0:T(8,128)(2,1)S(1)}, u32[]{:S(2)}, u32[]{:S(2)}) collective-permute-start(bf16[512,512]{1,0:T(8,128)(2,1)S(1)} %slice.46), channel_id=1, source_target_pairs={{0,1},{1,0},{2,3},{3,2},{4,5},{5,4},{6,7},{7,6},{8,9},{9,8},{10,11... | collective-permute-start | bytes 1572872 | tf_op jit(solution)/shard_map/ppermute | solution.py:510
  49.8 6.9 %all-to-all-done.both_ref = bf16[16,136,512]{2,1,0:T(8,128)(2,1)S(1)} async-done(((bf16[16,136,512]{2,1,0:T(8,128)(2,1)}), bf16[16,136,512]{2,1,0:T(8,128)(2,1)S(1)}, u32[]{:S(2)}, u32[]{:S(2)}) %all-to-all-start) | async-done | bytes 2228256 | tf_op jit(solution)/shard_map/all_to_all | solution.py:504
  56.7 8.8 %shard_map.74 = bf16[16,1,32,512]{3,2,1,0:T(8,128)(2,1)} custom-call(s32[1]{0:T(128)} %bitcast.1.place_ref, bf16[16,136,512]{2,1,0:T(8,128)(2,1)S(1)} %all-to-all-done.both_ref, bf16[512,1024]{1,0:T(8,128)(2,1)} %constant.66.clone.head_ref, bf16[1024,512]{1,0:T(8,128)(2,1)} %constant.67.clone.back_ref, f32[64,128]{1,0:T(8,128)} %broadcast_in_dim.17.skip_ref, ...), custom_call_target="tpu_custom_call" | custom-call | flops 1610612736 | bytes 2097152 | tf_op jit(solution)/shard_map/pallas_call | solution.py:72
  65.5 7.1 %collective-permute-done.1.refs_2_ = bf16[1024,512]{1,0:T(8,128)(2,1)} collective-permute-done((bf16[1024,512]{1,0:T(8,128)(2,1)}, bf16[1024,512]{1,0:T(8,128)(2,1)}, u32[]{:S(2)}, u32[]{:S(2)}) %collective-permute-start.1) | collective-permute-done | bytes 1048608 | tf_op jit(solution)/shard_map/ppermute | solution.py:576
  72.6 6.6 %all-to-all-start.1 = ((bf16[16,32,512]{2,1,0:T(8,128)(2,1)}), bf16[16,32,512]{2,1,0:T(8,128)(2,1)S(1)}, u32[]{:S(2)}, u32[]{:S(2)}) async-start(bf16[16,32,512]{2,1,0:T(8,128)(2,1)} %bitcast.31), calls=%async_computation.1 | async-start | bytes 1048576 | tf_op jit(solution)/shard_map/all_to_all | solution.py:504
  79.4 1.6 %collective-permute-start.5 = (f32[8,512]{1,0:T(8,128)S(1)}, f32[8,512]{1,0:T(8,128)S(1)}, u32[]{:S(2)}, u32[]{:S(2)}) collective-permute-start(f32[8,512]{1,0:T(8,128)S(1)} %slice.49), channel_id=1, source_target_pairs={{0,1},{1,0},{2,3},{3,2},{4,5},{5,4},{6,7},{7,6},{8,9},{9,8},{10,11... | collective-permute-start | bytes 49160 | tf_op jit(solution)/shard_map/ppermute | solution.py:510
  80.9 9.0 %shard_map.76 = bf16[16,2,32,512]{3,2,1,0:T(8,128)(2,1)} custom-call(s32[1]{0:T(128)} %bitcast.1.place_ref, bf16[16,136,512]{2,1,0:T(8,128)(2,1)S(1)} %all-to-all-done.both_ref, bf16[512,1024]{1,0:T(8,128)(2,1)} %constant.66.clone.head_ref, bf16[1024,512]{1,0:T(8,128)(2,1)} %constant.67.clone.back_ref, f32[64,128]{1,0:T(8,128)} %broadcast_in_dim.17.skip_ref, ...), custom_call_target="tpu_custom_call" | custom-call | flops 1610612736 | bytes 2097152 | tf_op jit(solution)/shard_map/pallas_call | solution.py:72
  90.0 3.7 %all-to-all-done.1.long_ref = bf16[16,32,512]{2,1,0:T(8,128)(2,1)S(1)} async-done(((bf16[16,32,512]{2,1,0:T(8,128)(2,1)}), bf16[16,32,512]{2,1,0:T(8,128)(2,1)S(1)}, u32[]{:S(2)}, u32[]{:S(2)}) %all-to-all-start.1) | async-done | bytes 524320 | tf_op jit(solution)/shard_map/all_to_all | solution.py:504
  93.7 4.0 %all-to-all-start.2 = ((bf16[32,32,512]{2,1,0:T(8,128)(2,1)}), bf16[32,32,512]{2,1,0:T(8,128)(2,1)S(1)}, u32[]{:S(2)}, u32[]{:S(2)}) async-start(bf16[32,32,512]{2,1,0:T(8,128)(2,1)} %bitcast.30), calls=%async_computation.2 | async-start | bytes 2097152 | tf_op jit(solution)/shard_map/all_to_all | solution.py:595
  97.7 2.1 %shard_map.77.gated_ref = bf16[512,512]{1,0:T(8,128)(2,1)} custom-call(bf16[16,32,512]{2,1,0:T(8,128)(2,1)S(1)} %all-to-all-done.1.long_ref, bf16[512,1024]{1,0:T(8,128)(2,1)} %shard_map.75.outer_ref.mine_ref, f32[8,1024]{1,0:T(8,128)} %copy-done.1), custom_call_target="tpu_custom_call" | custom-call | bytes 1572864 | tf_op jit(solution)/shard_map/pallas_call | solution.py:72
  99.9 1.8 %collective-permute-start.6 = (bf16[512,512]{1,0:T(8,128)(2,1)}, bf16[512,512]{1,0:T(8,128)(2,1)S(1)}, u32[]{:S(2)}, u32[]{:S(2)}) collective-permute-start(bf16[512,512]{1,0:T(8,128)(2,1)} %shard_map.77.gated_ref), channel_id=1, source_target_pairs={{0,1},{1,0},{2,3},{3,2},{4,5},{5,4},{6,7},{7,6},{8,9},{9,8},{10,11... | collective-permute-start | bytes 1572872 | tf_op jit(solution)/shard_map/ppermute | solution.py:510
  101.6 0.1 pad_add_fusion.place_ref
  101.7 3.9 %shard_map.78.sum_ref = bf16[512,2048]{1,0:T(8,128)(2,1)} custom-call(s32[1]{0:T(128)} %bitcast.here_ref, bf16[512,512]{1,0:T(8,128)(2,1)} %shard_map.77.gated_ref, bf16[1024,4096]{1,0:T(8,128)(2,1)} %refs_4_.1), custom_call_target="tpu_custom_call" | custom-call | flops 1073741824 | bytes 4194304 | tf_op jit(solution)/shard_map/pallas_call | solution.py:72
  105.6 17.1 %collective-permute-done.6.sent_ref = bf16[512,512]{1,0:T(8,128)(2,1)S(1)} collective-permute-done((bf16[512,512]{1,0:T(8,128)(2,1)}, bf16[512,512]{1,0:T(8,128)(2,1)S(1)}, u32[]{:S(2)}, u32[]{:S(2)}) %collective-permute-start.6) | collective-permute-done | bytes 524320 | tf_op jit(solution)/shard_map/ppermute | solution.py:510
  122.7 1.3 all-to-all-done.2
  124.0 7.3 %shard_map.79 = bf16[512,2048]{1,0:T(8,128)(2,1)} custom-call(s32[2]{0:T(128)S(1)} %pad_add_fusion.place_ref, bf16[512,512]{1,0:T(8,128)(2,1)S(1)} %collective-permute-done.6.sent_ref, bf16[16,2,32,512]{3,2,1,0:T(8,128)(2,1)S(1)} %bitcast.27, f32[2,8,512]{2,1,0:T(8,128)S(1)} %pad_maximum_fusion.first_ref, bf16[512,2048]{1,0:T(8,128)(2,1)} %shard_map.78.sum_ref, ...), custom_call_target="tpu_custom_call" | custom-call | flops 3221225472 | bytes 10485760 | tf_op jit(solution)/shard_map/pallas_call | solution.py:72
  (29 shorter events, 0.2 us)
Async XLA Ops:
  5.7 7.5 %copy-start.4 = (f32[1024]{0:T(1024)S(1)}, f32[1024]{0:T(1024)}, u32[]{:S(2)}) copy-start(f32[1024]{0:T(1024)} %param.10) | copy-start | bytes 12292
  5.7 7.7 %slice-start = ((f32[3,3,1024]{2,1,0:T(4,128)}), f32[3,2,1024]{2,1,0:T(2,128)S(1)}, s32[]{:S(2)}) async-start(f32[3,3,1024]{2,1,0:T(4,128)} %t_ref.1), calls=%async_computation.3 | async-start | bytes 49152 | tf_op jit(solution)/shard_map/slice | solution.py:560
  5.7 50.9 %all-to-all-start = ((bf16[16,136,512]{2,1,0:T(8,128)(2,1)}), bf16[16,136,512]{2,1,0:T(8,128)(2,1)S(1)}, u32[]{:S(2)}, u32[]{:S(2)}) async-start(bf16[16,136,512]{2,1,0:T(8,128)(2,1)} %shard_map.73), calls=%async_computation | async-start | bytes 4456448 | tf_op jit(solution)/shard_map/all_to_all | solution.py:504
  13.1 30.1 %copy-start.3 = (f32[3,3,1024]{2,1,0:T(4,128)S(1)}, f32[3,3,1024]{2,1,0:T(4,128)}, u32[]{:S(2)}) copy-start(f32[3,3,1024]{2,1,0:T(4,128)} %t_ref.1) | copy-start | bytes 110596
  16.0 25.6 %collective-permute-start = (bf16[1024,512]{1,0:T(8,128)(2,1)S(1)}, bf16[1024,512]{1,0:T(8,128)(2,1)}, u32[]{:S(2)}, u32[]{:S(2)}) collective-permute-start(bf16[1024,512]{1,0:T(8,128)(2,1)S(1)} %constant_dynamic-slice_fusion.1), channel_id=1, source_target_pairs={{0,1},{1,0},{2,3},{3,2},{4,5},{5,4},{6,7},{7,6},{8,9},{9,8},{10,11... | collective-permute-start | bytes 3145736 | tf_op jit(solution)/shard_map/ppermute | solution.py:510
  41.6 31.0 %collective-permute-start.1 = (bf16[1024,512]{1,0:T(8,128)(2,1)}, bf16[1024,512]{1,0:T(8,128)(2,1)}, u32[]{:S(2)}, u32[]{:S(2)}) collective-permute-start(bf16[1024,512]{1,0:T(8,128)(2,1)} %collective-permute-done.refs_0_), channel_id=1, source_target_pairs={{0,4},{2,6},{4,0},{6,2},{8,12},{10,14},{12,8},{14,10},{16,20},{18,... | collective-permute-start | bytes 3145736 | tf_op jit(solution)/shard_map/ppermute | solution.py:576
  48.2 17.3 %collective-permute-start.2 = (bf16[512,512]{1,0:T(8,128)(2,1)S(1)}, bf16[512,512]{1,0:T(8,128)(2,1)S(1)}, u32[]{:S(2)}, u32[]{:S(2)}) collective-permute-start(bf16[512,512]{1,0:T(8,128)(2,1)S(1)} %slice.46), channel_id=1, source_target_pairs={{0,1},{1,0},{2,3},{3,2},{4,5},{5,4},{6,7},{7,6},{8,9},{9,8},{10,11... | collective-permute-start | bytes 1572872 | tf_op jit(solution)/shard_map/ppermute | solution.py:510
  49.8 40.2 %collective-permute-start.3 = (bf16[1024,512]{1,0:T(8,128)(2,1)}, bf16[1024,512]{1,0:T(8,128)(2,1)}, u32[]{:S(2)}, u32[]{:S(2)}) collective-permute-start(bf16[1024,512]{1,0:T(8,128)(2,1)} %collective-permute-done.refs_0_), channel_id=1, source_target_pairs={{0,2},{2,0},{4,6},{6,4},{8,10},{10,8},{12,14},{14,12},{16,18},{18,... | collective-permute-start | bytes 3145736 | tf_op jit(solution)/shard_map/ppermute | solution.py:576
  65.5 24.4 %copy-start = (bf16[512,512]{1,0:T(8,128)(2,1)}, bf16[512,512]{1,0:T(8,128)(2,1)S(1)}, u32[]{:S(2)}) copy-start(bf16[512,512]{1,0:T(8,128)(2,1)S(1)} %collective-permute-done.2.theirs_ref) | copy-start | bytes 1572868
  72.6 21.1 %collective-permute-start.4 = (bf16[1024,512]{1,0:T(8,128)(2,1)}, bf16[1024,512]{1,0:T(8,128)(2,1)}, u32[]{:S(2)}, u32[]{:S(2)}) collective-permute-start(bf16[1024,512]{1,0:T(8,128)(2,1)} %collective-permute-done.1.refs_2_), channel_id=1, source_target_pairs={{0,2},{2,0},{4,6},{6,4},{8,10},{10,8},{12,14},{14,12},{16,18},{18,... | collective-permute-start | bytes 3145736 | tf_op jit(solution)/shard_map/ppermute | solution.py:576
  72.6 21.1 %all-to-all-start.1 = ((bf16[16,32,512]{2,1,0:T(8,128)(2,1)}), bf16[16,32,512]{2,1,0:T(8,128)(2,1)S(1)}, u32[]{:S(2)}, u32[]{:S(2)}) async-start(bf16[16,32,512]{2,1,0:T(8,128)(2,1)} %bitcast.31), calls=%async_computation.1 | async-start | bytes 1048576 | tf_op jit(solution)/shard_map/all_to_all | solution.py:504
  79.4 10.6 %copy-start.1 = (f32[8,1024]{1,0:T(8,128)}, f32[8,1024]{1,0:T(8,128)S(1)}, u32[]{:S(2)}) copy-start(f32[8,1024]{1,0:T(8,128)S(1)} %select_maximum_fusion.first_ref) | copy-start | bytes 98308
  79.4 10.6 %collective-permute-start.5 = (f32[8,512]{1,0:T(8,128)S(1)}, f32[8,512]{1,0:T(8,128)S(1)}, u32[]{:S(2)}, u32[]{:S(2)}) collective-permute-start(f32[8,512]{1,0:T(8,128)S(1)} %slice.49), channel_id=1, source_target_pairs={{0,1},{1,0},{2,3},{3,2},{4,5},{5,4},{6,7},{7,6},{8,9},{9,8},{10,11... | collective-permute-start | bytes 49160 | tf_op jit(solution)/shard_map/ppermute | solution.py:510
  93.7 30.3 %all-to-all-start.2 = ((bf16[32,32,512]{2,1,0:T(8,128)(2,1)}), bf16[32,32,512]{2,1,0:T(8,128)(2,1)S(1)}, u32[]{:S(2)}, u32[]{:S(2)}) async-start(bf16[32,32,512]{2,1,0:T(8,128)(2,1)} %bitcast.30), calls=%async_computation.2 | async-start | bytes 2097152 | tf_op jit(solution)/shard_map/all_to_all | solution.py:595
  99.9 22.9 %collective-permute-start.6 = (bf16[512,512]{1,0:T(8,128)(2,1)}, bf16[512,512]{1,0:T(8,128)(2,1)S(1)}, u32[]{:S(2)}, u32[]{:S(2)}) collective-permute-start(bf16[512,512]{1,0:T(8,128)(2,1)} %shard_map.77.gated_ref), channel_id=1, source_target_pairs={{0,1},{1,0},{2,3},{3,2},{4,5},{5,4},{6,7},{7,6},{8,9},{9,8},{10,11... | collective-permute-start | bytes 1572872 | tf_op jit(solution)/shard_map/ppermute | solution.py:510
  101.7 3.9 %copy-start.2 = (f32[8,1024]{1,0:T(8,128)S(1)}, f32[8,1024]{1,0:T(8,128)}, u32[]{:S(2)}) copy-start(f32[8,1024]{1,0:T(8,128)} %copy-done.1) | copy-start | bytes 98308

commit v2 on v1

--- a/solution.py
+++ b/solution.py
@@ -264,11 +264,17 @@
 def conv_kernel(split, place_ref, both_ref, head_ref, back_ref, skip_ref, taps_ref, o_ref, *scratch):
     head_buf, back_buf, spec_ref, factor_ref, low_ref, x_buf, fix_ref, sems = scratch
     count, _, part, rows = o_ref.shape
+    tiles = rows // LANES
     high = min(part, 16)
     group = 2
     low = 2 * part * (split or 0)
-    pairs = [(head_ref, head_buf), (back_ref, back_buf)]
-    copies = [pltpu.make_async_copy(a, b, sems.at[i]) for i, (a, b) in enumerate(pairs)]
+    copies = [
+        pltpu.make_async_copy(
+            head_ref.at[:, pl.ds(t * 2 * LANES, 2 * LANES)], head_buf.at[t], sems.at[t]
+        )
+        for t in range(tiles)
+    ]
+    copies.append(pltpu.make_async_copy(back_ref, back_buf, sems.at[tiles]))
     for copy in copies:
         copy.start()
     x_buf[...] = both_ref[:, low + part : low + 2 * part]
@@ -283,57 +289,63 @@
             value = x_buf[block, :, :LANES].astype(jnp.float32)
             value = jnp.where(lane == 0, one, jnp.where(lane == 1, two, value))
             x_buf[block, :, :LANES] = value.astype(x_buf.dtype)
-    copies[0].wait()
-    for ref, blocks in ((factor_ref, both_ref[:, low : low + part]), (spec_ref, x_buf[...])):
-        blocks = blocks.reshape(count * part, rows)
-        ref[...] = jnp.dot(blocks, head_buf[...], preferred_element_type=jnp.float32)
-    column = lax.broadcasted_iota(jnp.int32, (part, 2 * rows), 1)
-    sign = jnp.where(column % 2 == 0, 1.0, -1.0)
-
-    def one_window(turn, carry):
-        block = count - 1 - turn
-        place = pl.ds(pl.multiple_of(block * part, part), part)
-        before = pl.ds(pl.multiple_of(jnp.maximum(block - 1, 0) * part, part), part)
-        earlier = jnp.where(block > 0, factor_ref[before, :], 0.0)
-        factor_ref[place, :] = earlier + sign * factor_ref[place, :]
-        return carry
-
-    lax.fori_loop(0, count, one_window, 0)
+    height = count * part
+    filters = both_ref[:, low : low + part].reshape(height, rows)
+    odd = lax.broadcasted_iota(jnp.int32, (height, 2 * LANES), 1) % 2 == 1
     lane = lax.broadcasted_iota(jnp.int32, (high, LANES), 1)
-    slabs = part // high
-
-    def one_slab(turn, carry):
-        tile = turn // slabs
-        base = pl.multiple_of((turn % slabs) * high, high)
-        reals = pl.ds(pl.multiple_of(tile * 2 * LANES, LANES), LANES)
-        imags = pl.ds(pl.multiple_of(tile * 2 * LANES + LANES, LANES), LANES)
-        first = (lane == 0) & (tile == 0)
+
+    def spectra(t):
+        copies[t].wait()
+        value = jnp.dot(filters, head_buf[t], preferred_element_type=jnp.float32)
+        earlier = jnp.concatenate([jnp.zeros_like(value[:part]), value[:-part]], axis=0)
+        factor_ref[t] = earlier + jnp.where(odd, -value, value)
+        spec_ref[t] = jnp.dot(
+            x_buf[...].reshape(height, rows), head_buf[t], preferred_element_type=jnp.float32
+        )
+
+    def products(t, slab):
+        base = slab * high
+        if not isinstance(base, int):
+            base = pl.multiple_of(base, high)
         for start in range(0, count, group):
             sums = [[None] * 3 for _ in range(group)]
             factors = {}
             for source in range(start + group):
                 place = pl.ds(base + source * part, high)
-                real, imag = (spec_ref[place, reals], spec_ref[place, imags])
+                real, imag = (spec_ref[t, place, :LANES], spec_ref[t, place, LANES:])
                 for g in range(group):
                     lag = start + g - source
                     if lag < 0:
                         continue
                     if lag not in factors:
                         place = pl.ds(base + lag * part, high)
-                        factors[lag] = (factor_ref[place, reals], factor_ref[place, imags])
+                        factors[lag] = (factor_ref[t, place, :LANES], factor_ref[t, place, LANES:])
                     a, b = factors[lag]
                     terms = (real * a, imag * b, real * b + imag * a)
                     before = sums[g]
-                    sums[g] = [t if p is None else p + t for p, t in zip(before, terms)]
+                    sums[g] = [u if p is None else p + u for p, u in zip(before, terms)]
             for g in range(group):
                 rr, ii, ri = sums[g]
                 place = pl.ds(base + (start + g) * part, high)
-                low_ref[place, reals] = jnp.where(first, rr, rr - ii).astype(low_ref.dtype)
-                low_ref[place, imags] = jnp.where(first, ii, ri).astype(low_ref.dtype)
-        return carry
-
-    lax.fori_loop(0, slabs * (rows // LANES), one_slab, 0)
-    copies[1].wait()
+                re, im = (rr - ii, ri)
+                if t == 0:
+                    re, im = (jnp.where(lane == 0, rr, re), jnp.where(lane == 0, ii, im))
+                low_ref[place, t * 2 * LANES : t * 2 * LANES + LANES] = re.astype(low_ref.dtype)
+                low_ref[place, t * 2 * LANES + LANES : (t + 1) * 2 * LANES] = im.astype(low_ref.dtype)
+
+    for t in range(tiles):
+        spectra(t)
+        if split is not None:
+            for slab in range(part // high):
+                products(t, slab)
+        else:
+
+            def one_slab(slab, carry, t=t):
+                products(t, slab)
+                return carry
+
+            lax.fori_loop(0, part // high, one_slab, 0)
+    copies[tiles].wait()
     back = jnp.dot(
         low_ref[...].astype(jnp.bfloat16), back_buf[...], preferred_element_type=jnp.float32
     )
@@ -356,14 +368,14 @@
         [vmem],
         [((count, copies, part, rows), jnp.bfloat16)],
         scratch=[
-            pltpu.VMEM(head.shape, jnp.bfloat16),
+            pltpu.VMEM((rows // LANES, rows, 2 * LANES), jnp.bfloat16),
             pltpu.VMEM(back.shape, jnp.bfloat16),
-            pltpu.VMEM((height, 2 * rows), jnp.float32),
-            pltpu.VMEM((height, 2 * rows), jnp.float32),
+            pltpu.VMEM((rows // LANES, height, 2 * LANES), jnp.float32),
+            pltpu.VMEM((rows // LANES, height, 2 * LANES), jnp.float32),
             pltpu.VMEM((height, 2 * rows), jnp.float32 if part % 16 else jnp.bfloat16),
             pltpu.VMEM((count, part, rows), jnp.bfloat16),
             pltpu.VMEM((LANES, LANES), jnp.float32),
-            pltpu.SemaphoreType.DMA((2,)),
+            pltpu.SemaphoreType.DMA((rows // LANES + 1,)),
         ],
         megabytes=28,
         flops=12 * height * rows * rows,
@@ -576,6 +588,7 @@
         return lax.ppermute(value, "ctx", [(i, i ^ bit) for i in range(count)])
 
     across = swapped(near, 2)
+    both, outer, theirs = after((both, outer, theirs))
     early = long_conv(both, head, back, skip, taps, place, 0)[:, 0]
     edges = lax.dynamic_slice(
         both, (jnp.maximum(position - 1, 0), 4 * step, 2 * LANES), (1, 8, chan // 4)
@@ -586,10 +599,11 @@
     )
     first = jnp.pad(first, ((0, 6), (0, 0)))
     other = to_groups([first[:, chan // 2 :]])[0]
-    both, across, theirs, _ = after((both, across, theirs, early))
+    both, _ = after((both, early))
+    late = long_conv(both, head, back, skip, taps, place, 1, copies=groups)
+    late, across = after((late, across))
     blocks = [near, swapped(near, 1), across, swapped(across, 1)]
-    late = long_conv(both, head, back, skip, taps, place, 1, copies=groups)
-    early, late, blocks, other, first = after((exchanged(early), late, blocks, other, first))
+    early, late, other, first = after((exchanged(early), late, other, first))
     gated = gate(early, outer, first)
     sent = to_groups([gated])[0]
     dealt = lax.all_to_all(

time: 132 us -> 129 us (0.977)
  waiting for transfers between devices: 60.2 us -> 54.9 us
  Pallas kernels: 39.4 us -> 36.4 us
  starting transfers between devices: 26 us -> 28.9 us
  local copies, waits for them, and re-layouts: 5.13 us -> 7.08 us
    ppermute x4, waiting for transfers between devices: 41.3 us -> 48.4 us  [to_groups(): lax.ppermute(value, 'ch', [(g, (g + s) % groups) for g in range(groups)])]
    ppermute x3, waiting for transfers between devices: 7.08 us -> 0.01 us  [swapped(): return lax.ppermute(value, 'ctx', [(i, i ^ bit) for i in range(count)])]
    all_to_all x2, waiting for transfers between devices: 10.6 us -> 5.25 us  [exchanged(): return lax.all_to_all(value, 'ctx', 0, 0, tiled=True)]
    pallas_call x7, Pallas kernels: 39.4 us -> 36.4 us  [run(): return inner(*pinned)]
    all_to_all x2, starting transfers between devices: 14 us -> 16.3 us  [exchanged(): return lax.all_to_all(value, 'ctx', 0, 0, tiled=True)]
    unnamed x14 -> x18, local copies, waits for them, and re-layouts: 0.04 us -> 1.99 us
  transfers between devices with their start and end apart: 10 -> 10, of which waited for: 6 -> 5; matrix products, arithmetic and copies ran while one was open for 4% -> 4% of each run, Pallas kernels for 20% -> 18%
where the time goes in v2:
time: 129 us; the launch traced here: 128 us
  waiting for transfers between devices  54.9 us (43%)
  Pallas kernels  36.4 us (28%)
  starting transfers between devices  28.9 us (22%)
  local copies, waits for them, and re-layouts  7.08 us (5%)
    ppermute x4, waiting for transfers between devices, to_groups(): lax.ppermute(value, 'ch', [(g, (g + s) % groups) for g in range(groups)])  48.4 us
    pallas_call x7, Pallas kernels, run(): return inner(*pinned)  36.4 us
    all_to_all x2, starting transfers between devices, exchanged(): return lax.all_to_all(value, 'ctx', 0, 0, tiled=True)  16.3 us
    ppermute x4, starting transfers between devices, to_groups(): lax.ppermute(value, 'ch', [(g, (g + s) % groups) for g in range(groups)])  6.4 us
    all_to_all x2, waiting for transfers between devices, exchanged(): return lax.all_to_all(value, 'ctx', 0, 0, tiled=True)  5.25 us
    all_to_all x1, starting transfers between devices, local(): lax.all_to_all(late.reshape(count * groups, step, rows), ('ctx', 'ch'), 0...  4.01 us
  transfers between devices with their start and end apart: 10, of which 5 were waited for; matrix products, arithmetic and copies ran while one was open for 4% of the time, Pallas kernels for 18%

profile of v2, /device:TPU:0, one launch (start us, length us, event | category | flops | bytes accessed | tf_op | source)
XLA Modules:
  0.0 127.9 jit_solution(16634882410785227238)
XLA Ops:
  0.0 5.7 %shard_map.73 = bf16[16,136,512]{2,1,0:T(8,128)(2,1)} custom-call(bf16[512,1024]{1,0:T(8,128)(2,1)} %f_ref.1, bf16[3,512,1024]{2,1,0:T(8,128)(2,1)} %bitcast.28, f32[3,3,1024]{2,1,0:T(4,128)} %t_ref.1), custom_call_target="tpu_custom_call" | custom-call | bytes 5242880 | tf_op jit(solution)/shard_map/pallas_call | solution.py:72
  5.7 7.4 %all-to-all-start = ((bf16[16,136,512]{2,1,0:T(8,128)(2,1)}), bf16[16,136,512]{2,1,0:T(8,128)(2,1)S(1)}, u32[]{:S(2)}, u32[]{:S(2)}) async-start(bf16[16,136,512]{2,1,0:T(8,128)(2,1)} %shard_map.73), calls=%async_computation | async-start | bytes 4456448 | tf_op jit(solution)/shard_map/all_to_all | solution.py:516
  13.3 0.1 broadcast_in_dim.17
  13.5 0.6 pad.8.taps_ref
  14.1 1.3 %constant_dynamic-slice_fusion.1 = bf16[1024,512]{1,0:T(8,128)(2,1)S(1)} fusion(bf16[1024,4096]{1,0:T(8,128)(2,1)} %refs_4_.1, s32[]{:T(128)S(6)} %select_n.36), kind=kLoop, calls=%fused_computation.14 | loop fusion | bytes 2097156 | tf_op jit(solution)/shard_map/dynamic_slice | solution.py:579
  15.4 0.7 broadcast_in_dim.18.skip_ref
  16.0 1.5 %collective-permute-start = (bf16[1024,512]{1,0:T(8,128)(2,1)S(1)}, bf16[1024,512]{1,0:T(8,128)(2,1)}, u32[]{:S(2)}, u32[]{:S(2)}) collective-permute-start(bf16[1024,512]{1,0:T(8,128)(2,1)S(1)} %constant_dynamic-slice_fusion.1), channel_id=1, source_target_pairs={{0,1},{1,0},{2,3},{3,2},{4,5},{5,4},{6,7},{7,6},{8,9},{9,8},{10,11... | collective-permute-start | bytes 3145736 | tf_op jit(solution)/shard_map/ppermute | solution.py:522
  17.5 0.6 slice.36.t_ref
  18.1 23.5 %collective-permute-done.refs_0_ = bf16[1024,512]{1,0:T(8,128)(2,1)} collective-permute-done((bf16[1024,512]{1,0:T(8,128)(2,1)S(1)}, bf16[1024,512]{1,0:T(8,128)(2,1)}, u32[]{:S(2)}, u32[]{:S(2)}) %collective-permute-start) | collective-permute-done | bytes 1048608 | tf_op jit(solution)/shard_map/ppermute | solution.py:522
  41.6 0.6 broadcast_in_dim.16.e_ref
  42.2 2.6 %shard_map.74.outer_ref.mine_ref = bf16[512,1024]{1,0:T(8,128)(2,1)} custom-call(bf16[3,512,1024]{2,1,0:T(8,128)(2,1)} %bitcast.29, f32[1,2,1024]{2,1,0:T(2,128)} %broadcast_in_dim.16.e_ref, f32[3,1,1024]{2,1,0:T(1,128)} %slice.36.t_ref), custom_call_target="tpu_custom_call" | custom-call | bytes 2097152 | tf_op jit(solution)/shard_map/pallas_call | solution.py:72
  44.9 1.1 slice.46
  46.0 1.6 %collective-permute-start.1 = (bf16[512,512]{1,0:T(8,128)(2,1)S(1)}, bf16[512,512]{1,0:T(8,128)(2,1)S(1)}, u32[]{:S(2)}, u32[]{:S(2)}) collective-permute-start(bf16[512,512]{1,0:T(8,128)(2,1)S(1)} %slice.46), channel_id=1, source_target_pairs={{0,1},{1,0},{2,3},{3,2},{4,5},{5,4},{6,7},{7,6},{8,9},{9,8},{10,11... | collective-permute-start | bytes 1572872 | tf_op jit(solution)/shard_map/ppermute | solution.py:522
  47.5 1.6 %collective-permute-start.2 = (bf16[1024,512]{1,0:T(8,128)(2,1)}, bf16[1024,512]{1,0:T(8,128)(2,1)}, u32[]{:S(2)}, u32[]{:S(2)}) collective-permute-start(bf16[1024,512]{1,0:T(8,128)(2,1)} %collective-permute-done.refs_0_), channel_id=1, source_target_pairs={{0,4},{2,6},{4,0},{6,2},{8,12},{10,14},{12,8},{14,10},{16,20},{18,... | collective-permute-start | bytes 3145736 | tf_op jit(solution)/shard_map/ppermute | solution.py:588
  49.2 10.3 %collective-permute-done.1.theirs_ref = bf16[512,512]{1,0:T(8,128)(2,1)S(1)} collective-permute-done((bf16[512,512]{1,0:T(8,128)(2,1)S(1)}, bf16[512,512]{1,0:T(8,128)(2,1)S(1)}, u32[]{:S(2)}, u32[]{:S(2)}) %collective-permute-start.1) | collective-permute-done | bytes 524320 | tf_op jit(solution)/shard_map/ppermute | solution.py:522
  59.5 7.3 %shard_map.75 = bf16[16,1,32,512]{3,2,1,0:T(8,128)(2,1)} custom-call(s32[1]{0:T(128)} %bitcast.1.place_ref, bf16[16,136,512]{2,1,0:T(8,128)(2,1)S(1)} %all-to-all-done.both_ref, bf16[512,1024]{1,0:T(8,128)(2,1)} %constant.66.clone.head_ref, bf16[1024,512]{1,0:T(8,128)(2,1)} %constant.67.clone.back_ref, f32[64,128]{1,0:T(8,128)} %broadcast_in_dim.18.skip_ref, ...), custom_call_target="tpu_custom_call" | custom-call | flops 1610612736 | bytes 2097152 | tf_op jit(solution)/shard_map/pallas_call | solution.py:72
  66.8 8.9 %all-to-all-start.1 = ((bf16[16,32,512]{2,1,0:T(8,128)(2,1)}), bf16[16,32,512]{2,1,0:T(8,128)(2,1)S(1)}, u32[]{:S(2)}, u32[]{:S(2)}) async-start(bf16[16,32,512]{2,1,0:T(8,128)(2,1)} %bitcast.31), calls=%async_computation.1 | async-start | bytes 1048576 | tf_op jit(solution)/shard_map/all_to_all | solution.py:516
  75.9 1.6 %collective-permute-start.3 = (f32[8,512]{1,0:T(8,128)S(1)}, f32[8,512]{1,0:T(8,128)S(1)}, u32[]{:S(2)}, u32[]{:S(2)}) collective-permute-start(f32[8,512]{1,0:T(8,128)S(1)} %slice.49), channel_id=1, source_target_pairs={{0,1},{1,0},{2,3},{3,2},{4,5},{5,4},{6,7},{7,6},{8,9},{9,8},{10,11... | collective-permute-start | bytes 49160 | tf_op jit(solution)/shard_map/ppermute | solution.py:522
  77.5 7.5 %shard_map.76 = bf16[16,2,32,512]{3,2,1,0:T(8,128)(2,1)} custom-call(s32[1]{0:T(128)} %bitcast.1.place_ref, bf16[16,136,512]{2,1,0:T(8,128)(2,1)S(1)} %all-to-all-done.both_ref, bf16[512,1024]{1,0:T(8,128)(2,1)} %constant.66.clone.head_ref, bf16[1024,512]{1,0:T(8,128)(2,1)} %constant.67.clone.back_ref, f32[64,128]{1,0:T(8,128)} %broadcast_in_dim.18.skip_ref, ...), custom_call_target="tpu_custom_call" | custom-call | flops 1610612736 | bytes 2097152 | tf_op jit(solution)/shard_map/pallas_call | solution.py:72
  85.0 5.2 %all-to-all-done.1.long_ref = bf16[16,32,512]{2,1,0:T(8,128)(2,1)S(1)} async-done(((bf16[16,32,512]{2,1,0:T(8,128)(2,1)}), bf16[16,32,512]{2,1,0:T(8,128)(2,1)S(1)}, u32[]{:S(2)}, u32[]{:S(2)}) %all-to-all-start.1) | async-done | bytes 524320 | tf_op jit(solution)/shard_map/all_to_all | solution.py:516
  90.2 4.0 %all-to-all-start.2 = ((bf16[32,32,512]{2,1,0:T(8,128)(2,1)}), bf16[32,32,512]{2,1,0:T(8,128)(2,1)S(1)}, u32[]{:S(2)}, u32[]{:S(2)}) async-start(bf16[32,32,512]{2,1,0:T(8,128)(2,1)} %bitcast.30), calls=%async_computation.2 | async-start | bytes 2097152 | tf_op jit(solution)/shard_map/all_to_all | solution.py:609
  94.2 0.3 collective-permute-start.5
  94.5 0.3 collective-permute-start.6
  94.8 2.1 %shard_map.77.gated_ref = bf16[512,512]{1,0:T(8,128)(2,1)} custom-call(bf16[16,32,512]{2,1,0:T(8,128)(2,1)S(1)} %all-to-all-done.1.long_ref, bf16[512,1024]{1,0:T(8,128)(2,1)} %shard_map.74.outer_ref.mine_ref, f32[8,1024]{1,0:T(8,128)} %copy-done.3), custom_call_target="tpu_custom_call" | custom-call | bytes 1572864 | tf_op jit(solution)/shard_map/pallas_call | solution.py:72
  96.9 1.8 %collective-permute-start.4 = (bf16[512,512]{1,0:T(8,128)(2,1)}, bf16[512,512]{1,0:T(8,128)(2,1)S(1)}, u32[]{:S(2)}, u32[]{:S(2)}) collective-permute-start(bf16[512,512]{1,0:T(8,128)(2,1)} %shard_map.77.gated_ref), channel_id=1, source_target_pairs={{0,1},{1,0},{2,3},{3,2},{4,5},{5,4},{6,7},{7,6},{8,9},{9,8},{10,11... | collective-permute-start | bytes 1572872 | tf_op jit(solution)/shard_map/ppermute | solution.py:522
  98.7 0.1 pad_add_fusion.place_ref
  98.8 3.9 %shard_map.78.sum_ref = bf16[512,2048]{1,0:T(8,128)(2,1)} custom-call(s32[1]{0:T(128)} %bitcast.here_ref, bf16[512,512]{1,0:T(8,128)(2,1)} %shard_map.77.gated_ref, bf16[1024,4096]{1,0:T(8,128)(2,1)} %refs_4_.1), custom_call_target="tpu_custom_call" | custom-call | flops 1073741824 | bytes 4194304 | tf_op jit(solution)/shard_map/pallas_call | solution.py:72
  102.7 1.0 copy-done
  103.7 1.0 copy-done.1
  104.6 14.6 %collective-permute-done.4.sent_ref = bf16[512,512]{1,0:T(8,128)(2,1)S(1)} collective-permute-done((bf16[512,512]{1,0:T(8,128)(2,1)}, bf16[512,512]{1,0:T(8,128)(2,1)S(1)}, u32[]{:S(2)}, u32[]{:S(2)}) %collective-permute-start.4) | collective-permute-done | bytes 524320 | tf_op jit(solution)/shard_map/ppermute | solution.py:522
  119.2 1.3 all-to-all-done.2
  120.5 7.3 %shard_map.79 = bf16[512,2048]{1,0:T(8,128)(2,1)} custom-call(s32[2]{0:T(128)S(1)} %pad_add_fusion.place_ref, bf16[512,512]{1,0:T(8,128)(2,1)S(1)} %collective-permute-done.4.sent_ref, bf16[16,2,32,512]{3,2,1,0:T(8,128)(2,1)S(1)} %bitcast.27, f32[2,8,512]{2,1,0:T(8,128)S(1)} %pad_maximum_fusion.first_ref, bf16[512,2048]{1,0:T(8,128)(2,1)} %shard_map.78.sum_ref, ...), custom_call_target="tpu_custom_call" | custom-call | flops 3221225472 | bytes 10485760 | tf_op jit(solution)/shard_map/pallas_call | solution.py:72
  (33 shorter events, 0.3 us)
Async XLA Ops:
  5.7 7.5 %copy-start.6 = (f32[1024]{0:T(1024)S(1)}, f32[1024]{0:T(1024)}, u32[]{:S(2)}) copy-start(f32[1024]{0:T(1024)} %param.10) | copy-start | bytes 12292
  5.7 7.7 %slice-start = ((f32[3,3,1024]{2,1,0:T(4,128)}), f32[3,2,1024]{2,1,0:T(2,128)S(1)}, s32[]{:S(2)}) async-start(f32[3,3,1024]{2,1,0:T(4,128)} %t_ref.1), calls=%async_computation.3 | async-start | bytes 49152 | tf_op jit(solution)/shard_map/slice | solution.py:572
  5.7 53.8 %all-to-all-start = ((bf16[16,136,512]{2,1,0:T(8,128)(2,1)}), bf16[16,136,512]{2,1,0:T(8,128)(2,1)S(1)}, u32[]{:S(2)}, u32[]{:S(2)}) async-start(bf16[16,136,512]{2,1,0:T(8,128)(2,1)} %shard_map.73), calls=%async_computation | async-start | bytes 4456448 | tf_op jit(solution)/shard_map/all_to_all | solution.py:516
  13.1 4.4 %copy-start.5 = (f32[3,3,1024]{2,1,0:T(4,128)S(1)}, f32[3,3,1024]{2,1,0:T(4,128)}, u32[]{:S(2)}) copy-start(f32[3,3,1024]{2,1,0:T(4,128)} %t_ref.1) | copy-start | bytes 110596
  16.0 25.6 %collective-permute-start = (bf16[1024,512]{1,0:T(8,128)(2,1)S(1)}, bf16[1024,512]{1,0:T(8,128)(2,1)}, u32[]{:S(2)}, u32[]{:S(2)}) collective-permute-start(bf16[1024,512]{1,0:T(8,128)(2,1)S(1)} %constant_dynamic-slice_fusion.1), channel_id=1, source_target_pairs={{0,1},{1,0},{2,3},{3,2},{4,5},{5,4},{6,7},{7,6},{8,9},{9,8},{10,11... | collective-permute-start | bytes 3145736 | tf_op jit(solution)/shard_map/ppermute | solution.py:522
  46.0 13.5 %collective-permute-start.1 = (bf16[512,512]{1,0:T(8,128)(2,1)S(1)}, bf16[512,512]{1,0:T(8,128)(2,1)S(1)}, u32[]{:S(2)}, u32[]{:S(2)}) collective-permute-start(bf16[512,512]{1,0:T(8,128)(2,1)S(1)} %slice.46), channel_id=1, source_target_pairs={{0,1},{1,0},{2,3},{3,2},{4,5},{5,4},{6,7},{7,6},{8,9},{9,8},{10,11... | collective-permute-start | bytes 1572872 | tf_op jit(solution)/shard_map/ppermute | solution.py:522
  47.5 37.4 %collective-permute-start.2 = (bf16[1024,512]{1,0:T(8,128)(2,1)}, bf16[1024,512]{1,0:T(8,128)(2,1)}, u32[]{:S(2)}, u32[]{:S(2)}) collective-permute-start(bf16[1024,512]{1,0:T(8,128)(2,1)} %collective-permute-done.refs_0_), channel_id=1, source_target_pairs={{0,4},{2,6},{4,0},{6,2},{8,12},{10,14},{12,8},{14,10},{16,20},{18,... | collective-permute-start | bytes 3145736 | tf_op jit(solution)/shard_map/ppermute | solution.py:588
  59.5 7.3 %copy-start.2 = (bf16[512,512]{1,0:T(8,128)(2,1)}, bf16[512,512]{1,0:T(8,128)(2,1)S(1)}, u32[]{:S(2)}) copy-start(bf16[512,512]{1,0:T(8,128)(2,1)S(1)} %collective-permute-done.1.theirs_ref) | copy-start | bytes 1572868
  66.8 23.4 %all-to-all-start.1 = ((bf16[16,32,512]{2,1,0:T(8,128)(2,1)}), bf16[16,32,512]{2,1,0:T(8,128)(2,1)S(1)}, u32[]{:S(2)}, u32[]{:S(2)}) async-start(bf16[16,32,512]{2,1,0:T(8,128)(2,1)} %bitcast.31), calls=%async_computation.1 | async-start | bytes 1048576 | tf_op jit(solution)/shard_map/all_to_all | solution.py:516
  75.9 9.1 %copy-start.3 = (f32[8,1024]{1,0:T(8,128)}, f32[8,1024]{1,0:T(8,128)S(1)}, u32[]{:S(2)}) copy-start(f32[8,1024]{1,0:T(8,128)S(1)} %select_maximum_fusion.first_ref) | copy-start | bytes 98308
  75.9 9.1 %collective-permute-start.3 = (f32[8,512]{1,0:T(8,128)S(1)}, f32[8,512]{1,0:T(8,128)S(1)}, u32[]{:S(2)}, u32[]{:S(2)}) collective-permute-start(f32[8,512]{1,0:T(8,128)S(1)} %slice.49), channel_id=1, source_target_pairs={{0,1},{1,0},{2,3},{3,2},{4,5},{5,4},{6,7},{7,6},{8,9},{9,8},{10,11... | collective-permute-start | bytes 49160 | tf_op jit(solution)/shard_map/ppermute | solution.py:522
  90.2 30.3 %all-to-all-start.2 = ((bf16[32,32,512]{2,1,0:T(8,128)(2,1)}), bf16[32,32,512]{2,1,0:T(8,128)(2,1)S(1)}, u32[]{:S(2)}, u32[]{:S(2)}) async-start(bf16[32,32,512]{2,1,0:T(8,128)(2,1)} %bitcast.30), calls=%async_computation.2 | async-start | bytes 2097152 | tf_op jit(solution)/shard_map/all_to_all | solution.py:609
  94.2 8.4 %collective-permute-start.5 = (bf16[1024,512]{1,0:T(8,128)(2,1)}, bf16[1024,512]{1,0:T(8,128)(2,1)S(1)}, u32[]{:S(2)}, u32[]{:S(2)}) collective-permute-start(bf16[1024,512]{1,0:T(8,128)(2,1)} %collective-permute-done.refs_0_), channel_id=1, source_target_pairs={{0,2},{2,0},{4,6},{6,4},{8,10},{10,8},{12,14},{14,12},{16,18},{18,... | collective-permute-start | bytes 3145736 | tf_op jit(solution)/shard_map/ppermute | solution.py:588
  94.5 8.1 %collective-permute-start.6 = (bf16[1024,512]{1,0:T(8,128)(2,1)}, bf16[1024,512]{1,0:T(8,128)(2,1)S(1)}, u32[]{:S(2)}, u32[]{:S(2)}) collective-permute-start(bf16[1024,512]{1,0:T(8,128)(2,1)} %collective-permute-done.2.refs_2_), channel_id=1, source_target_pairs={{0,2},{2,0},{4,6},{6,4},{8,10},{10,8},{12,14},{14,12},{16,18},{18,... | collective-permute-start | bytes 3145736 | tf_op jit(solution)/shard_map/ppermute | solution.py:588
  96.9 22.3 %collective-permute-start.4 = (bf16[512,512]{1,0:T(8,128)(2,1)}, bf16[512,512]{1,0:T(8,128)(2,1)S(1)}, u32[]{:S(2)}, u32[]{:S(2)}) collective-permute-start(bf16[512,512]{1,0:T(8,128)(2,1)} %shard_map.77.gated_ref), channel_id=1, source_target_pairs={{0,1},{1,0},{2,3},{3,2},{4,5},{5,4},{6,7},{7,6},{8,9},{9,8},{10,11... | collective-permute-start | bytes 1572872 | tf_op jit(solution)/shard_map/ppermute | solution.py:522
  98.8 3.9 %copy-start.4 = (f32[8,1024]{1,0:T(8,128)S(1)}, f32[8,1024]{1,0:T(8,128)}, u32[]{:S(2)}) copy-start(f32[8,1024]{1,0:T(8,128)} %copy-done.3) | copy-start | bytes 98308
  102.6 1.0 copy-start
  103.6 1.0 copy-start.1

commit v3 on v2

--- a/solution.py
+++ b/solution.py
@@ -164,75 +164,74 @@
     )(streams, edges, taps)[0]
 
 
-def deal_kernel(f_ref, s_ref, t_ref, o_ref, f_buf, s_buf, tail_buf, sems):
-    count, height, rows = o_ref.shape
-    step = (height - 8) // 4
-    chan = f_ref.shape[1]
-    tile = chan // 2
-    last = tail_buf.shape[0]
+def deal_kernel(f_ref, s_ref, t_ref, o_ref, f_buf, s_buf, out_buf, sems):
+    count, height, _, wide = out_buf.shape
+    step = height - 1
+    rows, chan = f_ref.shape
+    tile = chan // 4
+    few = count // 2
     per = LANES // step
-    copies = [
-        pltpu.make_async_copy(f_ref.at[:, pl.ds(p * tile, tile)], f_buf.at[p], sems.at[2 * p])
-        for p in range(2)
-    ] + [
-        pltpu.make_async_copy(
-            s_ref.at[pl.ds(0, 2), :, pl.ds(p * tile, tile)], s_buf.at[p], sems.at[2 * p + 1]
+    ins = []
+    for q in range(4):
+        lanes = pl.ds(q * tile, tile)
+        ins.append(pltpu.make_async_copy(f_ref.at[:, lanes], f_buf.at[q], sems.at[2 * q]))
+        ins.append(
+            pltpu.make_async_copy(s_ref.at[pl.ds(0, 2), :, lanes], s_buf.at[q], sems.at[2 * q + 1])
         )
-        for p in range(2)
-    ]
-    copies.append(
-        pltpu.make_async_copy(s_ref.at[2, pl.ds(rows - last, last)], tail_buf, sems.at[4])
-    )
-    for k in (0, 2, 1, 3, 4):
-        copies[k].start()
-    for p in range(2):
-        start = p * 2 * step
-        lanes = slice(p * tile, (p + 1) * tile)
-        copies[p].wait()
-        value = f_buf[p].astype(jnp.float32).T.reshape(count, step, rows)
-        o_ref[:, start : start + step] = value.astype(o_ref.dtype)
-        copies[2 + p].wait()
+    for copy in ins:
+        copy.start()
+    outs = []
+    for q in range(4):
+        p, owner = (q // 2, q % 2 * few)
+        lanes = slice(q * tile, (q + 1) * tile)
+        ins[2 * q].wait()
+        values = [f_buf[q].astype(jnp.float32)]
+        ins[2 * q + 1].wait()
         both = []
-        for q in range(2):
-            now = s_buf[p, q].astype(jnp.float32)
-            value = t_ref[0, q : q + 1, lanes] * now
-            value = value + t_ref[1, q : q + 1, lanes] * pltpu.roll(now, 1, 0)
-            both.append(value + t_ref[2, q : q + 1, lanes] * pltpu.roll(now, 2, 0))
-        value = (both[0] * both[1]).T.reshape(count, step, rows)
-        o_ref[:, start + step : start + 2 * step] = value.astype(o_ref.dtype)
-        ends = [s_buf[p, q, a : a + 2].astype(jnp.float32) for a in (0, rows - 2) for q in range(2)]
+        for stream in range(2):
+            now = s_buf[q, stream].astype(jnp.float32)
+            value = t_ref[0, stream : stream + 1, lanes] * now
+            value = value + t_ref[1, stream : stream + 1, lanes] * pltpu.roll(now, 1, 0)
+            both.append(value + t_ref[2, stream : stream + 1, lanes] * pltpu.roll(now, 2, 0))
+        values.append(both[0] * both[1])
+        for k in range(2):
+            value = values[k].T.astype(o_ref.dtype)
+            for half in range(2):
+                place = (4 * p + 2 * k + half) * step // 8
+                out_buf[owner : owner + few, place : place + step // 8] = value[
+                    :, half * wide : (half + 1) * wide
+                ].reshape(few, step // 8, 8, wide)
+        ends = [s_buf[q, k, a : a + 2].astype(jnp.float32) for a in (0, rows - 2) for k in range(2)]
         ends = jnp.concatenate(ends, axis=0).astype(o_ref.dtype)
         for g in range(tile // LANES):
-            value = ends[:, g * LANES : (g + 1) * LANES]
-            o_ref[g * per : (g + 1) * per, 4 * step :, p * LANES : (p + 1) * LANES] = (
-                jnp.broadcast_to(value[None], (per, 8, LANES))
-            )
-    copies[4].wait()
-    tail = tail_buf[last - 2 :].astype(jnp.float32)
-    wide = chan // 4
-    tail = jnp.concatenate(
-        [tail[t : t + 1, q * wide : (q + 1) * wide] for t in range(2) for q in range(4)], axis=0
-    ).astype(o_ref.dtype)
-    o_ref[:, 4 * step :, 2 * LANES : 2 * LANES + wide] = jnp.broadcast_to(
-        tail[None], (count, 8, wide)
-    )
+            value = jnp.broadcast_to(ends[:, g * LANES : (g + 1) * LANES][None], (per, 8, LANES))
+            first = owner + g * per
+            out_buf[first : first + per, height - 1, :, p * LANES : (p + 1) * LANES] = value
+        some = (pl.ds(owner, few), pl.ds(p * step // 2, step // 2))
+        outs.append(pltpu.make_async_copy(out_buf.at[some], o_ref.at[some], sems.at[8 + q]))
+        outs[q].start()
+    some = pl.ds(height - 1, 1)
+    outs.append(pltpu.make_async_copy(out_buf.at[:, some], o_ref.at[:, some], sems.at[12]))
+    outs[4].start()
+    for copy in outs:
+        copy.wait()
 
 
 def deal(filters, streams, taps, count):
     rows, chan = filters.shape
-    height = 2 * chan // count + 8
+    shape = (count, chan // count // 2 + 1, 8, rows // 2)
     anywhere, vmem = (pl.BlockSpec(memory_space=pl.ANY), pl.BlockSpec(memory_space=pltpu.VMEM))
     bf16 = jnp.bfloat16
     return call(
         deal_kernel,
         [anywhere, anywhere, vmem],
-        [vmem],
-        [((count, height, rows), bf16)],
+        [anywhere],
+        [(shape, bf16)],
         scratch=[
-            pltpu.VMEM((2, rows, chan // 2), bf16),
-            pltpu.VMEM((2, 2, rows, chan // 2), bf16),
-            pltpu.VMEM((16, chan), bf16),
-            pltpu.SemaphoreType.DMA((5,)),
+            pltpu.VMEM((4, rows, chan // 4), bf16),
+            pltpu.VMEM((4, 2, rows, chan // 4), bf16),
+            pltpu.VMEM(shape, bf16),
+            pltpu.SemaphoreType.DMA((13,)),
         ],
         megabytes=32,
         moved=10 * rows * chan,
@@ -267,7 +266,7 @@
     tiles = rows // LANES
     high = min(part, 16)
     group = 2
-    low = 2 * part * (split or 0)
+    low = part * (split or 0)
     copies = [
         pltpu.make_async_copy(
             head_ref.at[:, pl.ds(t * 2 * LANES, 2 * LANES)], head_buf.at[t], sems.at[t]
@@ -277,9 +276,18 @@
     copies.append(pltpu.make_async_copy(back_ref, back_buf, sems.at[tiles]))
     for copy in copies:
         copy.start()
-    x_buf[...] = both_ref[:, low + part : low + 2 * part]
+    height = count * part
+
+    def arrived(kind):
+        if split is None:
+            return both_ref[:, kind * part : (kind + 1) * part].reshape(height, rows)
+        first = (4 * split + 2 * kind) * part // 8
+        halves = [both_ref[:, a : a + part // 8] for a in (first, first + part // 8)]
+        return jnp.concatenate([h.reshape(height, rows // 2) for h in halves], axis=1)
+
+    x_buf[...] = arrived(1).reshape(count, part, rows)
     if split is not None:
-        ends = both_ref[:, 4 * part :, split * LANES : (split + 1) * LANES]
+        ends = both_ref[:, both_ref.shape[1] - 1, :, split * LANES : (split + 1) * LANES]
         fix_ref[...] = first_tokens(ends, taps_ref[split], place_ref[0])
         mine = fix_ref[pl.ds(pl.multiple_of(place_ref[0] * part, part), part), :]
         lane = lax.broadcasted_iota(jnp.int32, (part, LANES), 1)
@@ -289,16 +297,23 @@
             value = x_buf[block, :, :LANES].astype(jnp.float32)
             value = jnp.where(lane == 0, one, jnp.where(lane == 1, two, value))
             x_buf[block, :, :LANES] = value.astype(x_buf.dtype)
-    height = count * part
-    filters = both_ref[:, low : low + part].reshape(height, rows)
+    filters = arrived(0)
     odd = lax.broadcasted_iota(jnp.int32, (height, 2 * LANES), 1) % 2 == 1
     lane = lax.broadcasted_iota(jnp.int32, (high, LANES), 1)
 
+    lane0 = lax.broadcasted_iota(jnp.int32, (height, LANES), 1) == 0
+
     def spectra(t):
-        copies[t].wait()
         value = jnp.dot(filters, head_buf[t], preferred_element_type=jnp.float32)
         earlier = jnp.concatenate([jnp.zeros_like(value[:part]), value[:-part]], axis=0)
-        factor_ref[t] = earlier + jnp.where(odd, -value, value)
+        window = earlier + jnp.where(odd, -value, value)
+        real, imag = (window[:, :LANES], window[:, LANES:])
+        factor_ref[t, :, :LANES] = real
+        less, more = (imag - real, real + imag)
+        if t == 0:
+            less, more = (jnp.where(lane0, real, less), jnp.where(lane0, imag, more))
+        factor_ref[t, :, LANES : 2 * LANES] = less
+        factor_ref[t, :, 2 * LANES :] = more
         spec_ref[t] = jnp.dot(
             x_buf[...].reshape(height, rows), head_buf[t], preferred_element_type=jnp.float32
         )
@@ -313,26 +328,31 @@
             for source in range(start + group):
                 place = pl.ds(base + source * part, high)
                 real, imag = (spec_ref[t, place, :LANES], spec_ref[t, place, LANES:])
+                both = real + imag
                 for g in range(group):
                     lag = start + g - source
                     if lag < 0:
                         continue
                     if lag not in factors:
                         place = pl.ds(base + lag * part, high)
-                        factors[lag] = (factor_ref[t, place, :LANES], factor_ref[t, place, LANES:])
-                    a, b = factors[lag]
-                    terms = (real * a, imag * b, real * b + imag * a)
+                        factors[lag] = [
+                            factor_ref[t, place, c * LANES : (c + 1) * LANES] for c in range(3)
+                        ]
+                    a, b, c = factors[lag]
+                    terms = (both * a, real * b, imag * c)
                     before = sums[g]
                     sums[g] = [u if p is None else p + u for p, u in zip(before, terms)]
             for g in range(group):
-                rr, ii, ri = sums[g]
+                a, b, c = sums[g]
                 place = pl.ds(base + (start + g) * part, high)
-                re, im = (rr - ii, ri)
+                re, im = (a - c, a + b)
                 if t == 0:
-                    re, im = (jnp.where(lane == 0, rr, re), jnp.where(lane == 0, ii, im))
+                    re, im = (jnp.where(lane == 0, b, re), jnp.where(lane == 0, c, im))
                 low_ref[place, t * 2 * LANES : t * 2 * LANES + LANES] = re.astype(low_ref.dtype)
                 low_ref[place, t * 2 * LANES + LANES : (t + 1) * 2 * LANES] = im.astype(low_ref.dtype)
 
+    for copy in copies:
+        copy.wait()
     for t in range(tiles):
         spectra(t)
         if split is not None:
@@ -345,19 +365,18 @@
                 return carry
 
             lax.fori_loop(0, part // high, one_slab, 0)
-    copies[tiles].wait()
     back = jnp.dot(
         low_ref[...].astype(jnp.bfloat16), back_buf[...], preferred_element_type=jnp.float32
     )
     value = back.reshape(count, part, rows)
-    skip = skip_ref[low // 2 : low // 2 + part, :1][None]
+    skip = skip_ref[low : low + part, :1][None]
     value = value + skip * x_buf[...].astype(jnp.float32)
     for copy in range(o_ref.shape[1]):
         o_ref[:, copy] = value.astype(o_ref.dtype)
 
 
 def long_conv(both, head, back, skip, taps, place, split, copies=1):
-    count, _, rows = both.shape
+    count, rows = (both.shape[0], head.shape[0])
     own = skip.shape[0]
     part = own if split is None else own // 2
     height = count * part
@@ -371,7 +390,7 @@
             pltpu.VMEM((rows // LANES, rows, 2 * LANES), jnp.bfloat16),
             pltpu.VMEM(back.shape, jnp.bfloat16),
             pltpu.VMEM((rows // LANES, height, 2 * LANES), jnp.float32),
-            pltpu.VMEM((rows // LANES, height, 2 * LANES), jnp.float32),
+            pltpu.VMEM((rows // LANES, height, 3 * LANES), jnp.float32),
             pltpu.VMEM((height, 2 * rows), jnp.float32 if part % 16 else jnp.bfloat16),
             pltpu.VMEM((count, part, rows), jnp.bfloat16),
             pltpu.VMEM((LANES, LANES), jnp.float32),
@@ -547,8 +566,8 @@
     groups = lax.axis_size("ch")
     own = chan // count
     step = own // 2
-    fast = groups == 2 and count % 4 == 0 and own % 32 == 0 and LANES % step == 0
-    fast = fast and chan // 4 + 2 * LANES <= rows and 2 * count <= LANES
+    fast = groups == 2 and count % 4 == 0 and own % 32 == 0 and count % 2 == 0 and LANES % step == 0
+    fast = fast and rows % (4 * LANES) == 0 and 2 * count <= LANES and chan % (4 * LANES) == 0
     after = lax.optimization_barrier
     position, here = (lax.axis_index("ctx"), lax.axis_index("ch"))
     head = jnp.asarray(head_table(2 * rows))
@@ -588,12 +607,9 @@
         return lax.ppermute(value, "ctx", [(i, i ^ bit) for i in range(count)])
 
     across = swapped(near, 2)
-    both, outer, theirs = after((both, outer, theirs))
+    edges = passed_along(streams[2, rows - 2 :], "ctx", 1).astype(jnp.float32)
+    both, outer, theirs, edges = after((both, outer, theirs, edges))
     early = long_conv(both, head, back, skip, taps, place, 0)[:, 0]
-    edges = lax.dynamic_slice(
-        both, (jnp.maximum(position - 1, 0), 4 * step, 2 * LANES), (1, 8, chan // 4)
-    )
-    edges = jnp.where(position == 0, 0.0, edges.reshape(2, chan).astype(jnp.float32))
     first = jnp.stack(
         [short_taps[1, 2] * edges[1] + short_taps[2, 2] * edges[0], short_taps[2, 2] * edges[1]]
     )

time: 129 us -> 127 us (0.984)
  waiting for transfers between devices: 54.9 us -> 50.8 us
  starting transfers between devices: 28.9 us -> 32.5 us
  Pallas kernels: 36.4 us -> 34.1 us
    ppermute x4, waiting for transfers between devices: 48.4 us -> 42.6 us  [to_groups(): lax.ppermute(value, 'ch', [(g, (g + s) % groups) for g in range(groups)])]
    ppermute x3, starting transfers between devices: 2.22 us -> 5.06 us  [swapped(): return lax.ppermute(value, 'ctx', [(i, i ^ bit) for i in range(count)])]
    pallas_call x7, Pallas kernels: 36.4 us -> 34.1 us  [run(): return inner(*pinned)]
  transfers between devices with their start and end apart: 10 -> 11, of which waited for: 5 -> 6; matrix products, arithmetic and copies ran while one was open for 4% -> 5% of each run, Pallas kernels for 18% -> 17%
where the time goes in v3:
time: 127 us; the launch traced here: 126 us
  waiting for transfers between devices  50.8 us (40%)
  Pallas kernels  34.1 us (27%)
  starting transfers between devices  32.5 us (26%)
  local copies, waits for them, and re-layouts  7.78 us (6%)
    ppermute x4, waiting for transfers between devices, to_groups(): lax.ppermute(value, 'ch', [(g, (g + s) % groups) for g in range(groups)])  42.6 us
    pallas_call x7, Pallas kernels, run(): return inner(*pinned)  34.1 us
    all_to_all x2, starting transfers between devices, exchanged(): return lax.all_to_all(value, 'ctx', 0, 0, tiled=True)  15.8 us
    ppermute x4, starting transfers between devices, to_groups(): lax.ppermute(value, 'ch', [(g, (g + s) % groups) for g in range(groups)])  6.21 us
    all_to_all x2, waiting for transfers between devices, exchanged(): return lax.all_to_all(value, 'ctx', 0, 0, tiled=True)  6.14 us
    ppermute x3, starting transfers between devices, swapped(): return lax.ppermute(value, 'ctx', [(i, i ^ bit) for i in range(count)])  5.06 us
    all_to_all x1, starting transfers between devices, local(): lax.all_to_all(late.reshape(count * groups, step, rows), ('ctx', 'ch'), 0...  4.19 us
  transfers between devices with their start and end apart: 11, of which 6 were waited for; matrix products, arithmetic and copies ran while one was open for 5% of the time, Pallas kernels for 17%

profile of v3, /device:TPU:0, one launch (start us, length us, event | category | flops | bytes accessed | tf_op | source)
XLA Modules:
  0.0 125.7 jit_solution(8645856172589284127)
XLA Ops:
  0.0 5.0 %shard_map.73 = bf16[16,33,8,256]{3,2,1,0:T(8,128)(2,1)} custom-call(bf16[512,1024]{1,0:T(8,128)(2,1)} %f_ref.1, bf16[3,512,1024]{2,1,0:T(8,128)(2,1)} %bitcast.24, f32[3,3,1024]{2,1,0:T(4,128)} %t_ref.1), custom_call_target="tpu_custom_call" | custom-call | bytes 5242880 | tf_op jit(solution)/shard_map/pallas_call | solution.py:72
  5.0 7.5 %all-to-all-start = ((bf16[16,33,8,256]{3,2,1,0:T(8,128)(2,1)}), bf16[16,33,8,256]{3,2,1,0:T(8,128)(2,1)S(1)}, u32[]{:S(2)}, u32[]{:S(2)}) async-start(bf16[16,33,8,256]{3,2,1,0:T(8,128)(2,1)} %shard_map.73), calls=%async_computation | async-start | bytes 4325376 | tf_op jit(solution)/shard_map/all_to_all | solution.py:535
  12.9 0.6 pad.8.taps_ref
  13.5 1.3 %constant_dynamic-slice_fusion.1 = bf16[1024,512]{1,0:T(8,128)(2,1)S(1)} fusion(bf16[1024,4096]{1,0:T(8,128)(2,1)} %refs_4_.1, s32[]{:T(128)S(6)} %select_n.26), kind=kLoop, calls=%fused_computation.12 | loop fusion | bytes 2097156 | tf_op jit(solution)/shard_map/dynamic_slice | solution.py:598
  14.8 0.7 broadcast_in_dim.14.skip_ref
  15.4 1.5 %collective-permute-start = (bf16[1024,512]{1,0:T(8,128)(2,1)S(1)}, bf16[1024,512]{1,0:T(8,128)(2,1)}, u32[]{:S(2)}, u32[]{:S(2)}) collective-permute-start(bf16[1024,512]{1,0:T(8,128)(2,1)S(1)} %constant_dynamic-slice_fusion.1), channel_id=1, source_target_pairs={{0,1},{1,0},{2,3},{3,2},{4,5},{5,4},{6,7},{7,6},{8,9},{9,8},{10,11... | collective-permute-start | bytes 3145736 | tf_op jit(solution)/shard_map/ppermute | solution.py:541
  16.9 0.6 slice.33.t_ref
  17.6 23.4 %collective-permute-done.refs_0_ = bf16[1024,512]{1,0:T(8,128)(2,1)} collective-permute-done((bf16[1024,512]{1,0:T(8,128)(2,1)S(1)}, bf16[1024,512]{1,0:T(8,128)(2,1)}, u32[]{:S(2)}, u32[]{:S(2)}) %collective-permute-start) | collective-permute-done | bytes 1048608 | tf_op jit(solution)/shard_map/ppermute | solution.py:541
  41.0 0.6 broadcast_in_dim.12.e_ref
  41.6 2.6 %shard_map.74.outer_ref.mine_ref = bf16[512,1024]{1,0:T(8,128)(2,1)} custom-call(bf16[3,512,1024]{2,1,0:T(8,128)(2,1)} %bitcast.25, f32[1,2,1024]{2,1,0:T(2,128)} %broadcast_in_dim.12.e_ref, f32[3,1,1024]{2,1,0:T(1,128)} %slice.33.t_ref), custom_call_target="tpu_custom_call" | custom-call | bytes 2097152 | tf_op jit(solution)/shard_map/pallas_call | solution.py:72
  44.2 1.1 slice.42
  45.3 1.6 %collective-permute-start.1 = (bf16[512,512]{1,0:T(8,128)(2,1)S(1)}, bf16[512,512]{1,0:T(8,128)(2,1)S(1)}, u32[]{:S(2)}, u32[]{:S(2)}) collective-permute-start(bf16[512,512]{1,0:T(8,128)(2,1)S(1)} %slice.42), channel_id=1, source_target_pairs={{0,1},{1,0},{2,3},{3,2},{4,5},{5,4},{6,7},{7,6},{8,9},{9,8},{10,11... | collective-permute-start | bytes 1572872 | tf_op jit(solution)/shard_map/ppermute | solution.py:541
  46.9 0.7 slice_bitcast_fusion.1
  47.6 1.3 %collective-permute-start.2 = (bf16[2,1024]{1,0:T(2,128)(2,1)S(1)}, bf16[2,1024]{1,0:T(2,128)(2,1)S(1)}, u32[]{:S(2)}, u32[]{:S(2)}) collective-permute-start(bf16[2,1024]{1,0:T(2,128)(2,1)S(1)} %slice_bitcast_fusion.1), channel_id=1, source_target_pairs={{0,2},{2,4},{4,6},{6,8},{8,10},{10,12},{12,14},{14,16},{16,18},{18... | collective-permute-start | bytes 12296 | tf_op jit(solution)/shard_map/ppermute | solution.py:18
  48.9 0.8 collective-permute-done.2
  49.7 4.5 %collective-permute-start.3 = (bf16[1024,512]{1,0:T(8,128)(2,1)}, bf16[1024,512]{1,0:T(8,128)(2,1)}, u32[]{:S(2)}, u32[]{:S(2)}) collective-permute-start(bf16[1024,512]{1,0:T(8,128)(2,1)} %collective-permute-done.refs_0_), channel_id=1, source_target_pairs={{0,4},{2,6},{4,0},{6,2},{8,12},{10,14},{12,8},{14,10},{16,20},{18,... | collective-permute-start | bytes 3145736 | tf_op jit(solution)/shard_map/ppermute | solution.py:607
  54.2 4.6 %collective-permute-done.1.theirs_ref = bf16[512,512]{1,0:T(8,128)(2,1)S(1)} collective-permute-done((bf16[512,512]{1,0:T(8,128)(2,1)S(1)}, bf16[512,512]{1,0:T(8,128)(2,1)S(1)}, u32[]{:S(2)}, u32[]{:S(2)}) %collective-permute-start.1) | collective-permute-done | bytes 524320 | tf_op jit(solution)/shard_map/ppermute | solution.py:541
  58.8 6.5 %shard_map.75 = bf16[16,1,32,512]{3,2,1,0:T(8,128)(2,1)} custom-call(s32[1]{0:T(128)} %bitcast.1.place_ref, bf16[16,33,8,256]{3,2,1,0:T(8,128)(2,1)S(1)} %all-to-all-done.both_ref, bf16[512,1024]{1,0:T(8,128)(2,1)} %constant.60.clone.head_ref, bf16[1024,512]{1,0:T(8,128)(2,1)} %constant.61.clone.back_ref, f32[64,128]{1,0:T(8,128)} %broadcast_in_dim.14.skip_ref, ...), custom_call_target="tpu_custom_call" | custom-call | flops 1610612736 | bytes 2097152 | tf_op jit(solution)/shard_map/pallas_call | solution.py:72
  65.3 8.3 %all-to-all-start.1 = ((bf16[16,32,512]{2,1,0:T(8,128)(2,1)}), bf16[16,32,512]{2,1,0:T(8,128)(2,1)S(1)}, u32[]{:S(2)}, u32[]{:S(2)}) async-start(bf16[16,32,512]{2,1,0:T(8,128)(2,1)} %bitcast.28), calls=%async_computation.1 | async-start | bytes 1048576 | tf_op jit(solution)/shard_map/all_to_all | solution.py:535
  73.6 1.6 %collective-permute-start.4 = (f32[8,512]{1,0:T(8,128)S(1)}, f32[8,512]{1,0:T(8,128)S(1)}, u32[]{:S(2)}, u32[]{:S(2)}) collective-permute-start(f32[8,512]{1,0:T(8,128)S(1)} %slice.44), channel_id=1, source_target_pairs={{0,1},{1,0},{2,3},{3,2},{4,5},{5,4},{6,7},{7,6},{8,9},{9,8},{10,11... | collective-permute-start | bytes 49160 | tf_op jit(solution)/shard_map/ppermute | solution.py:541
  75.2 6.7 %shard_map.76 = bf16[16,2,32,512]{3,2,1,0:T(8,128)(2,1)} custom-call(s32[1]{0:T(128)} %bitcast.1.place_ref, bf16[16,33,8,256]{3,2,1,0:T(8,128)(2,1)S(1)} %all-to-all-done.both_ref, bf16[512,1024]{1,0:T(8,128)(2,1)} %constant.60.clone.head_ref, bf16[1024,512]{1,0:T(8,128)(2,1)} %constant.61.clone.back_ref, f32[64,128]{1,0:T(8,128)} %broadcast_in_dim.14.skip_ref, ...), custom_call_target="tpu_custom_call" | custom-call | flops 1610612736 | bytes 2097152 | tf_op jit(solution)/shard_map/pallas_call | solution.py:72
  81.9 6.1 %all-to-all-done.1.long_ref = bf16[16,32,512]{2,1,0:T(8,128)(2,1)S(1)} async-done(((bf16[16,32,512]{2,1,0:T(8,128)(2,1)}), bf16[16,32,512]{2,1,0:T(8,128)(2,1)S(1)}, u32[]{:S(2)}, u32[]{:S(2)}) %all-to-all-start.1) | async-done | bytes 524320 | tf_op jit(solution)/shard_map/all_to_all | solution.py:535
  88.1 4.2 %all-to-all-start.2 = ((bf16[32,32,512]{2,1,0:T(8,128)(2,1)}), bf16[32,32,512]{2,1,0:T(8,128)(2,1)S(1)}, u32[]{:S(2)}, u32[]{:S(2)}) async-start(bf16[32,32,512]{2,1,0:T(8,128)(2,1)} %bitcast.27), calls=%async_computation.2 | async-start | bytes 2097152 | tf_op jit(solution)/shard_map/all_to_all | solution.py:625
  92.4 0.4 collective-permute-start.7
  92.8 2.1 %shard_map.77.gated_ref = bf16[512,512]{1,0:T(8,128)(2,1)} custom-call(bf16[16,32,512]{2,1,0:T(8,128)(2,1)S(1)} %all-to-all-done.1.long_ref, bf16[512,1024]{1,0:T(8,128)(2,1)} %shard_map.74.outer_ref.mine_ref, f32[8,1024]{1,0:T(8,128)} %copy-done.3), custom_call_target="tpu_custom_call" | custom-call | bytes 1572864 | tf_op jit(solution)/shard_map/pallas_call | solution.py:72
  94.9 1.6 %collective-permute-start.5 = (bf16[512,512]{1,0:T(8,128)(2,1)}, bf16[512,512]{1,0:T(8,128)(2,1)S(1)}, u32[]{:S(2)}, u32[]{:S(2)}) collective-permute-start(bf16[512,512]{1,0:T(8,128)(2,1)} %shard_map.77.gated_ref), channel_id=1, source_target_pairs={{0,1},{1,0},{2,3},{3,2},{4,5},{5,4},{6,7},{7,6},{8,9},{9,8},{10,11... | collective-permute-start | bytes 1572872 | tf_op jit(solution)/shard_map/ppermute | solution.py:541
  96.6 3.9 %shard_map.78.sum_ref = bf16[512,2048]{1,0:T(8,128)(2,1)} custom-call(s32[1]{0:T(128)} %bitcast.here_ref, bf16[512,512]{1,0:T(8,128)(2,1)} %shard_map.77.gated_ref, bf16[1024,4096]{1,0:T(8,128)(2,1)} %refs_4_.1), custom_call_target="tpu_custom_call" | custom-call | flops 1073741824 | bytes 4194304 | tf_op jit(solution)/shard_map/pallas_call | solution.py:72
  100.5 1.0 copy-done
  101.5 1.0 copy-done.1
  102.5 14.6 %collective-permute-done.5.sent_ref = bf16[512,512]{1,0:T(8,128)(2,1)S(1)} collective-permute-done((bf16[512,512]{1,0:T(8,128)(2,1)}, bf16[512,512]{1,0:T(8,128)(2,1)S(1)}, u32[]{:S(2)}, u32[]{:S(2)}) %collective-permute-start.5) | collective-permute-done | bytes 524320 | tf_op jit(solution)/shard_map/ppermute | solution.py:541
  117.0 1.3 all-to-all-done.2
  118.3 7.3 %shard_map.79 = bf16[512,2048]{1,0:T(8,128)(2,1)} custom-call(s32[2]{0:T(128)S(1)} %pad_add_fusion.place_ref, bf16[512,512]{1,0:T(8,128)(2,1)S(1)} %collective-permute-done.5.sent_ref, bf16[16,2,32,512]{3,2,1,0:T(8,128)(2,1)S(1)} %bitcast.23, f32[2,8,512]{2,1,0:T(8,128)S(1)} %pad_maximum_fusion.first_ref, bf16[512,2048]{1,0:T(8,128)(2,1)} %shard_map.78.sum_ref, ...), custom_call_target="tpu_custom_call" | custom-call | flops 3221225472 | bytes 10485760 | tf_op jit(solution)/shard_map/pallas_call | solution.py:72
  (33 shorter events, 0.5 us)
Async XLA Ops:
  5.0 7.6 %copy-start.6 = (f32[1024]{0:T(1024)S(1)}, f32[1024]{0:T(1024)}, u32[]{:S(2)}) copy-start(f32[1024]{0:T(1024)} %param.10) | copy-start | bytes 12292
  5.0 7.8 %slice-start = ((f32[3,3,1024]{2,1,0:T(4,128)}), f32[3,2,1024]{2,1,0:T(2,128)S(1)}, s32[]{:S(2)}) async-start(f32[3,3,1024]{2,1,0:T(4,128)} %t_ref.1), calls=%async_computation.3 | async-start | bytes 49152 | tf_op jit(solution)/shard_map/slice | solution.py:591
  5.0 11.9 %copy-start.5 = (f32[3,3,1024]{2,1,0:T(4,128)S(1)}, f32[3,3,1024]{2,1,0:T(4,128)}, u32[]{:S(2)}) copy-start(f32[3,3,1024]{2,1,0:T(4,128)} %t_ref.1) | copy-start | bytes 110596
  5.0 53.7 %all-to-all-start = ((bf16[16,33,8,256]{3,2,1,0:T(8,128)(2,1)}), bf16[16,33,8,256]{3,2,1,0:T(8,128)(2,1)S(1)}, u32[]{:S(2)}, u32[]{:S(2)}) async-start(bf16[16,33,8,256]{3,2,1,0:T(8,128)(2,1)} %shard_map.73), calls=%async_computation | async-start | bytes 4325376 | tf_op jit(solution)/shard_map/all_to_all | solution.py:535
  15.4 25.5 %collective-permute-start = (bf16[1024,512]{1,0:T(8,128)(2,1)S(1)}, bf16[1024,512]{1,0:T(8,128)(2,1)}, u32[]{:S(2)}, u32[]{:S(2)}) collective-permute-start(bf16[1024,512]{1,0:T(8,128)(2,1)S(1)} %constant_dynamic-slice_fusion.1), channel_id=1, source_target_pairs={{0,1},{1,0},{2,3},{3,2},{4,5},{5,4},{6,7},{7,6},{8,9},{9,8},{10,11... | collective-permute-start | bytes 3145736 | tf_op jit(solution)/shard_map/ppermute | solution.py:541
  45.3 13.4 %collective-permute-start.1 = (bf16[512,512]{1,0:T(8,128)(2,1)S(1)}, bf16[512,512]{1,0:T(8,128)(2,1)S(1)}, u32[]{:S(2)}, u32[]{:S(2)}) collective-permute-start(bf16[512,512]{1,0:T(8,128)(2,1)S(1)} %slice.42), channel_id=1, source_target_pairs={{0,1},{1,0},{2,3},{3,2},{4,5},{5,4},{6,7},{7,6},{8,9},{9,8},{10,11... | collective-permute-start | bytes 1572872 | tf_op jit(solution)/shard_map/ppermute | solution.py:541
  47.6 2.1 %collective-permute-start.2 = (bf16[2,1024]{1,0:T(2,128)(2,1)S(1)}, bf16[2,1024]{1,0:T(2,128)(2,1)S(1)}, u32[]{:S(2)}, u32[]{:S(2)}) collective-permute-start(bf16[2,1024]{1,0:T(2,128)(2,1)S(1)} %slice_bitcast_fusion.1), channel_id=1, source_target_pairs={{0,2},{2,4},{4,6},{6,8},{8,10},{10,12},{12,14},{14,16},{16,18},{18... | collective-permute-start | bytes 12296 | tf_op jit(solution)/shard_map/ppermute | solution.py:18
  49.7 32.2 %collective-permute-start.3 = (bf16[1024,512]{1,0:T(8,128)(2,1)}, bf16[1024,512]{1,0:T(8,128)(2,1)}, u32[]{:S(2)}, u32[]{:S(2)}) collective-permute-start(bf16[1024,512]{1,0:T(8,128)(2,1)} %collective-permute-done.refs_0_), channel_id=1, source_target_pairs={{0,4},{2,6},{4,0},{6,2},{8,12},{10,14},{12,8},{14,10},{16,20},{18,... | collective-permute-start | bytes 3145736 | tf_op jit(solution)/shard_map/ppermute | solution.py:607
  58.7 6.5 %copy-start.2 = (bf16[512,512]{1,0:T(8,128)(2,1)}, bf16[512,512]{1,0:T(8,128)(2,1)S(1)}, u32[]{:S(2)}) copy-start(bf16[512,512]{1,0:T(8,128)(2,1)S(1)} %collective-permute-done.1.theirs_ref) | copy-start | bytes 1572868
  65.3 22.8 %all-to-all-start.1 = ((bf16[16,32,512]{2,1,0:T(8,128)(2,1)}), bf16[16,32,512]{2,1,0:T(8,128)(2,1)S(1)}, u32[]{:S(2)}, u32[]{:S(2)}) async-start(bf16[16,32,512]{2,1,0:T(8,128)(2,1)} %bitcast.28), calls=%async_computation.1 | async-start | bytes 1048576 | tf_op jit(solution)/shard_map/all_to_all | solution.py:535
  73.6 14.4 %copy-start.3 = (f32[8,1024]{1,0:T(8,128)}, f32[8,1024]{1,0:T(8,128)S(1)}, u32[]{:S(2)}) copy-start(f32[8,1024]{1,0:T(8,128)S(1)} %select_maximum_fusion.first_ref) | copy-start | bytes 98308
  73.6 8.3 %collective-permute-start.4 = (f32[8,512]{1,0:T(8,128)S(1)}, f32[8,512]{1,0:T(8,128)S(1)}, u32[]{:S(2)}, u32[]{:S(2)}) collective-permute-start(f32[8,512]{1,0:T(8,128)S(1)} %slice.44), channel_id=1, source_target_pairs={{0,1},{1,0},{2,3},{3,2},{4,5},{5,4},{6,7},{7,6},{8,9},{9,8},{10,11... | collective-permute-start | bytes 49160 | tf_op jit(solution)/shard_map/ppermute | solution.py:541
  88.1 30.3 %all-to-all-start.2 = ((bf16[32,32,512]{2,1,0:T(8,128)(2,1)}), bf16[32,32,512]{2,1,0:T(8,128)(2,1)S(1)}, u32[]{:S(2)}, u32[]{:S(2)}) async-start(bf16[32,32,512]{2,1,0:T(8,128)(2,1)} %bitcast.27), calls=%async_computation.2 | async-start | bytes 2097152 | tf_op jit(solution)/shard_map/all_to_all | solution.py:625
  92.2 8.2 %collective-permute-start.6 = (bf16[1024,512]{1,0:T(8,128)(2,1)}, bf16[1024,512]{1,0:T(8,128)(2,1)S(1)}, u32[]{:S(2)}, u32[]{:S(2)}) collective-permute-start(bf16[1024,512]{1,0:T(8,128)(2,1)} %collective-permute-done.refs_0_), channel_id=1, source_target_pairs={{0,2},{2,0},{4,6},{6,4},{8,10},{10,8},{12,14},{14,12},{16,18},{18,... | collective-permute-start | bytes 3145736 | tf_op jit(solution)/shard_map/ppermute | solution.py:607
  92.4 8.1 %collective-permute-start.7 = (bf16[1024,512]{1,0:T(8,128)(2,1)}, bf16[1024,512]{1,0:T(8,128)(2,1)S(1)}, u32[]{:S(2)}, u32[]{:S(2)}) collective-permute-start(bf16[1024,512]{1,0:T(8,128)(2,1)} %collective-permute-done.3.refs_2_), channel_id=1, source_target_pairs={{0,2},{2,0},{4,6},{6,4},{8,10},{10,8},{12,14},{14,12},{16,18},{18,... | collective-permute-start | bytes 3145736 | tf_op jit(solution)/shard_map/ppermute | solution.py:607
  94.9 22.1 %collective-permute-start.5 = (bf16[512,512]{1,0:T(8,128)(2,1)}, bf16[512,512]{1,0:T(8,128)(2,1)S(1)}, u32[]{:S(2)}, u32[]{:S(2)}) collective-permute-start(bf16[512,512]{1,0:T(8,128)(2,1)} %shard_map.77.gated_ref), channel_id=1, source_target_pairs={{0,1},{1,0},{2,3},{3,2},{4,5},{5,4},{6,7},{7,6},{8,9},{9,8},{10,11... | collective-permute-start | bytes 1572872 | tf_op jit(solution)/shard_map/ppermute | solution.py:541
  96.6 3.9 %copy-start.4 = (f32[8,1024]{1,0:T(8,128)S(1)}, f32[8,1024]{1,0:T(8,128)}, u32[]{:S(2)}) copy-start(f32[8,1024]{1,0:T(8,128)} %copy-done.3) | copy-start | bytes 98308
  100.5 1.0 copy-start
  101.5 1.0 copy-start.1

commit v4 on v3

--- a/solution.py
+++ b/solution.py
@@ -165,12 +165,12 @@
 
 
 def deal_kernel(f_ref, s_ref, t_ref, o_ref, f_buf, s_buf, out_buf, sems):
-    count, height, _, wide = out_buf.shape
-    step = height - 1
+    count, height, _, _ = out_buf.shape
     rows, chan = f_ref.shape
+    step = chan // count // 2
     tile = chan // 4
     few = count // 2
-    per = LANES // step
+    per = LANES // step // 2
     ins = []
     for q in range(4):
         lanes = pl.ds(q * tile, tile)
@@ -180,7 +180,7 @@
         )
     for copy in ins:
         copy.start()
-    outs = []
+    outs, edges = ([], [])
     for q in range(4):
         p, owner = (q // 2, q % 2 * few)
         lanes = slice(q * tile, (q + 1) * tile)
@@ -195,19 +195,24 @@
             both.append(value + t_ref[2, stream : stream + 1, lanes] * pltpu.roll(now, 2, 0))
         values.append(both[0] * both[1])
         for k in range(2):
-            value = values[k].T.astype(o_ref.dtype)
-            for half in range(2):
-                place = (4 * p + 2 * k + half) * step // 8
+            value = values[k].astype(o_ref.dtype).T
+            for c in range(rows // LANES):
+                place = ((2 * p + k) * rows // LANES + c) * step // 8
                 out_buf[owner : owner + few, place : place + step // 8] = value[
-                    :, half * wide : (half + 1) * wide
-                ].reshape(few, step // 8, 8, wide)
+                    :, c * LANES : (c + 1) * LANES
+                ].reshape(few, step // 8, 8, LANES)
         ends = [s_buf[q, k, a : a + 2].astype(jnp.float32) for a in (0, rows - 2) for k in range(2)]
-        ends = jnp.concatenate(ends, axis=0).astype(o_ref.dtype)
-        for g in range(tile // LANES):
-            value = jnp.broadcast_to(ends[:, g * LANES : (g + 1) * LANES][None], (per, 8, LANES))
-            first = owner + g * per
-            out_buf[first : first + per, height - 1, :, p * LANES : (p + 1) * LANES] = value
-        some = (pl.ds(owner, few), pl.ds(p * step // 2, step // 2))
+        ends = jnp.concatenate(ends, axis=0)
+        edges.append(ends)
+        if p == 1:
+            for g in range(few // per):
+                lanes = slice(g * LANES // 2, (g + 1) * LANES // 2)
+                value = jnp.concatenate([edges[q - 2][:, lanes], edges[q][:, lanes]], axis=1)
+                first = owner + g * per
+                out_buf[first : first + per, height - 1] = jnp.broadcast_to(
+                    value[None].astype(o_ref.dtype), (per, 8, LANES)
+                )
+        some = (pl.ds(owner, few), pl.ds(p * (height // 2), height // 2))
         outs.append(pltpu.make_async_copy(out_buf.at[some], o_ref.at[some], sems.at[8 + q]))
         outs[q].start()
     some = pl.ds(height - 1, 1)
@@ -219,7 +224,7 @@
 
 def deal(filters, streams, taps, count):
     rows, chan = filters.shape
-    shape = (count, chan // count // 2 + 1, 8, rows // 2)
+    shape = (count, chan // count * rows // LANES // 4 + 1, 8, LANES)
     anywhere, vmem = (pl.BlockSpec(memory_space=pl.ANY), pl.BlockSpec(memory_space=pltpu.VMEM))
     bf16 = jnp.bfloat16
     return call(
@@ -238,7 +243,7 @@
     )(filters, streams, taps)[0]
 
 
-def first_tokens(ends, taps, place):
+def first_tokens(ends, taps):
     count = ends.shape[0]
 
     def at(row):
@@ -281,15 +286,17 @@
     def arrived(kind):
         if split is None:
             return both_ref[:, kind * part : (kind + 1) * part].reshape(height, rows)
-        first = (4 * split + 2 * kind) * part // 8
-        halves = [both_ref[:, a : a + part // 8] for a in (first, first + part // 8)]
-        return jnp.concatenate([h.reshape(height, rows // 2) for h in halves], axis=1)
+        first = (2 * split + kind) * tiles
+        places = [(first + c) * part // 8 for c in range(tiles)]
+        pieces = [both_ref[:, a : a + part // 8].reshape(height, LANES) for a in places]
+        return jnp.concatenate(pieces, axis=1)
 
     x_buf[...] = arrived(1).reshape(count, part, rows)
     if split is not None:
-        ends = both_ref[:, both_ref.shape[1] - 1, :, split * LANES : (split + 1) * LANES]
-        fix_ref[...] = first_tokens(ends, taps_ref[split], place_ref[0])
-        mine = fix_ref[pl.ds(pl.multiple_of(place_ref[0] * part, part), part), :]
+        ends = both_ref[:, both_ref.shape[1] - 1]
+        fix_ref[...] = first_tokens(ends, taps_ref[...])
+        first = split * (LANES // 2) + place_ref[0] * part
+        mine = fix_ref[pl.ds(pl.multiple_of(first, part), part), :]
         lane = lax.broadcasted_iota(jnp.int32, (part, LANES), 1)
         for block in range(count):
             one = pltpu.roll(mine, (LANES - block) % LANES, 1)
@@ -566,8 +573,8 @@
     groups = lax.axis_size("ch")
     own = chan // count
     step = own // 2
-    fast = groups == 2 and count % 4 == 0 and own % 32 == 0 and count % 2 == 0 and LANES % step == 0
-    fast = fast and rows % (4 * LANES) == 0 and 2 * count <= LANES and chan % (4 * LANES) == 0
+    fast = groups == 2 and count % 4 == 0 and own % 32 == 0 and count % 2 == 0 and LANES % (2 * step) == 0
+    fast = fast and rows % LANES == 0 and 2 * count <= LANES and chan % (4 * LANES) == 0
     after = lax.optimization_barrier
     position, here = (lax.axis_index("ctx"), lax.axis_index("ch"))
     head = jnp.asarray(head_table(2 * rows))
@@ -583,14 +590,14 @@
         both = exchanged(with_inner(both, streams, edges, short_taps, parts))
         both = both.reshape(count, 2 * own, rows)
         outer = outer_gate(streams, 2, edges[2:], short_taps[:, 2:], parts)
-        none = jnp.zeros((2, 8, LANES), jnp.float32)
+        none = jnp.zeros((8, LANES), jnp.float32)
         long = long_conv(both, head, back, skip, none, jnp.zeros((1,), jnp.int32), None)
         return any_groups(exchanged(long[:, 0]), outer, out_weight)
-    per = LANES // step
+    per = LANES // step // 2
     place = (position % per)[None]
     taps = short_taps[:, :2].reshape(6, 2, chan // 2)
-    taps = lax.dynamic_slice(taps, (0, 0, position // per * LANES), (6, 2, LANES))
-    taps = jnp.pad(taps.transpose(1, 0, 2), ((0, 0), (0, 2), (0, 0)))
+    taps = lax.dynamic_slice(taps, (0, 0, position // per * (LANES // 2)), (6, 2, LANES // 2))
+    taps = jnp.pad(taps.reshape(6, LANES), ((0, 2), (0, 0)))
     both = exchanged(deal(filters, streams, short_taps, count))
     cols = out_weight.shape[1] // groups
     wide = cols // 4

time: 127 us -> 126 us (level)
  no operation moved by 1% of the time
where the time goes in v4:
time: 126 us; the launch traced here: 125 us
  waiting for transfers between devices  50.8 us (40%)
  Pallas kernels  33.9 us (27%)
  starting transfers between devices  31.7 us (25%)
  local copies, waits for them, and re-layouts  7.93 us (6%)
    ppermute x4, waiting for transfers between devices, to_groups(): lax.ppermute(value, 'ch', [(g, (g + s) % groups) for g in range(groups)])  42.6 us
    pallas_call x7, Pallas kernels, run(): return inner(*pinned)  33.9 us
    all_to_all x2, starting transfers between devices, exchanged(): return lax.all_to_all(value, 'ctx', 0, 0, tiled=True)  15 us
    ppermute x4, starting transfers between devices, to_groups(): lax.ppermute(value, 'ch', [(g, (g + s) % groups) for g in range(groups)])  6.21 us
    all_to_all x2, waiting for transfers between devices, exchanged(): return lax.all_to_all(value, 'ctx', 0, 0, tiled=True)  6.14 us
    ppermute x3, starting transfers between devices, swapped(): return lax.ppermute(value, 'ctx', [(i, i ^ bit) for i in range(count)])  5.06 us
    all_to_all x1, starting transfers between devices, local(): lax.all_to_all(late.reshape(count * groups, step, rows), ('ctx', 'ch'), 0...  4.19 us
  transfers between devices with their start and end apart: 11, of which 6 were waited for; matrix products, arithmetic and copies ran while one was open for 5% of the time, Pallas kernels for 17%

profile of v4, /device:TPU:0, one launch (start us, length us, event | category | flops | bytes accessed | tf_op | source)
XLA Modules:
  0.0 124.8 jit_solution(7264399023945023621)
XLA Ops:
  0.0 4.8 %shard_map.73 = bf16[16,65,8,128]{3,2,1,0:T(8,128)(2,1)} custom-call(bf16[512,1024]{1,0:T(8,128)(2,1)} %f_ref.1, bf16[3,512,1024]{2,1,0:T(8,128)(2,1)} %bitcast.22, f32[3,3,1024]{2,1,0:T(4,128)} %t_ref.1), custom_call_target="tpu_custom_call" | custom-call | bytes 5242880 | tf_op jit(solution)/shard_map/pallas_call | solution.py:72
  4.8 7.5 %all-to-all-start = ((bf16[16,65,8,128]{3,2,1,0:T(8,128)(2,1)}), bf16[16,65,8,128]{3,2,1,0:T(8,128)(2,1)S(1)}, u32[]{:S(2)}, u32[]{:S(2)}) async-start(bf16[16,65,8,128]{3,2,1,0:T(8,128)(2,1)} %shard_map.73), calls=%async_computation | async-start | bytes 4259840 | tf_op jit(solution)/shard_map/all_to_all | solution.py:542
  12.8 0.6 pad.8.taps_ref
  13.4 1.3 %constant_dynamic-slice_fusion.1 = bf16[1024,512]{1,0:T(8,128)(2,1)S(1)} fusion(bf16[1024,4096]{1,0:T(8,128)(2,1)} %refs_4_.1, s32[]{:T(128)S(6)} %select_n.29), kind=kLoop, calls=%fused_computation.11 | loop fusion | bytes 2097156 | tf_op jit(solution)/shard_map/dynamic_slice | solution.py:605
  14.7 0.7 broadcast_in_dim.17.skip_ref
  15.4 1.5 %collective-permute-start = (bf16[1024,512]{1,0:T(8,128)(2,1)S(1)}, bf16[1024,512]{1,0:T(8,128)(2,1)}, u32[]{:S(2)}, u32[]{:S(2)}) collective-permute-start(bf16[1024,512]{1,0:T(8,128)(2,1)S(1)} %constant_dynamic-slice_fusion.1), channel_id=1, source_target_pairs={{0,1},{1,0},{2,3},{3,2},{4,5},{5,4},{6,7},{7,6},{8,9},{9,8},{10,11... | collective-permute-start | bytes 3145736 | tf_op jit(solution)/shard_map/ppermute | solution.py:548
  16.9 0.6 slice.33.t_ref
  17.5 23.4 %collective-permute-done.refs_0_ = bf16[1024,512]{1,0:T(8,128)(2,1)} collective-permute-done((bf16[1024,512]{1,0:T(8,128)(2,1)S(1)}, bf16[1024,512]{1,0:T(8,128)(2,1)}, u32[]{:S(2)}, u32[]{:S(2)}) %collective-permute-start) | collective-permute-done | bytes 1048608 | tf_op jit(solution)/shard_map/ppermute | solution.py:548
  40.9 0.6 broadcast_in_dim.15.e_ref
  41.5 2.6 %shard_map.74.outer_ref.mine_ref = bf16[512,1024]{1,0:T(8,128)(2,1)} custom-call(bf16[3,512,1024]{2,1,0:T(8,128)(2,1)} %bitcast.23, f32[1,2,1024]{2,1,0:T(2,128)} %broadcast_in_dim.15.e_ref, f32[3,1,1024]{2,1,0:T(1,128)} %slice.33.t_ref), custom_call_target="tpu_custom_call" | custom-call | bytes 2097152 | tf_op jit(solution)/shard_map/pallas_call | solution.py:72
  44.1 1.1 slice.42
  45.2 1.6 %collective-permute-start.1 = (bf16[512,512]{1,0:T(8,128)(2,1)S(1)}, bf16[512,512]{1,0:T(8,128)(2,1)S(1)}, u32[]{:S(2)}, u32[]{:S(2)}) collective-permute-start(bf16[512,512]{1,0:T(8,128)(2,1)S(1)} %slice.42), channel_id=1, source_target_pairs={{0,1},{1,0},{2,3},{3,2},{4,5},{5,4},{6,7},{7,6},{8,9},{9,8},{10,11... | collective-permute-start | bytes 1572872 | tf_op jit(solution)/shard_map/ppermute | solution.py:548
  46.8 0.7 slice_bitcast_fusion.1
  47.5 1.3 %collective-permute-start.2 = (bf16[2,1024]{1,0:T(2,128)(2,1)S(1)}, bf16[2,1024]{1,0:T(2,128)(2,1)S(1)}, u32[]{:S(2)}, u32[]{:S(2)}) collective-permute-start(bf16[2,1024]{1,0:T(2,128)(2,1)S(1)} %slice_bitcast_fusion.1), channel_id=1, source_target_pairs={{0,2},{2,4},{4,6},{6,8},{8,10},{10,12},{12,14},{14,16},{16,18},{18... | collective-permute-start | bytes 12296 | tf_op jit(solution)/shard_map/ppermute | solution.py:18
  48.8 0.8 collective-permute-done.2
  49.6 4.5 %collective-permute-start.3 = (bf16[1024,512]{1,0:T(8,128)(2,1)}, bf16[1024,512]{1,0:T(8,128)(2,1)}, u32[]{:S(2)}, u32[]{:S(2)}) collective-permute-start(bf16[1024,512]{1,0:T(8,128)(2,1)} %collective-permute-done.refs_0_), channel_id=1, source_target_pairs={{0,4},{2,6},{4,0},{6,2},{8,12},{10,14},{12,8},{14,10},{16,20},{18,... | collective-permute-start | bytes 3145736 | tf_op jit(solution)/shard_map/ppermute | solution.py:614
  54.1 4.6 %collective-permute-done.1.theirs_ref = bf16[512,512]{1,0:T(8,128)(2,1)S(1)} collective-permute-done((bf16[512,512]{1,0:T(8,128)(2,1)S(1)}, bf16[512,512]{1,0:T(8,128)(2,1)S(1)}, u32[]{:S(2)}, u32[]{:S(2)}) %collective-permute-start.1) | collective-permute-done | bytes 524320 | tf_op jit(solution)/shard_map/ppermute | solution.py:548
  58.7 6.5 %shard_map.75 = bf16[16,1,32,512]{3,2,1,0:T(8,128)(2,1)} custom-call(s32[1]{0:T(128)} %bitcast.2.place_ref, bf16[16,65,8,128]{3,2,1,0:T(8,128)(2,1)S(1)} %all-to-all-done.both_ref, bf16[512,1024]{1,0:T(8,128)(2,1)} %constant.66.clone.head_ref, bf16[1024,512]{1,0:T(8,128)(2,1)} %constant.67.clone.back_ref, f32[64,128]{1,0:T(8,128)} %broadcast_in_dim.17.skip_ref, ...), custom_call_target="tpu_custom_call" | custom-call | flops 1610612736 | bytes 2097152 | tf_op jit(solution)/shard_map/pallas_call | solution.py:72
  65.2 7.4 %all-to-all-start.1 = ((bf16[16,32,512]{2,1,0:T(8,128)(2,1)}), bf16[16,32,512]{2,1,0:T(8,128)(2,1)S(1)}, u32[]{:S(2)}, u32[]{:S(2)}) async-start(bf16[16,32,512]{2,1,0:T(8,128)(2,1)} %bitcast.26), calls=%async_computation.1 | async-start | bytes 1048576 | tf_op jit(solution)/shard_map/all_to_all | solution.py:542
  72.7 1.6 %collective-permute-start.4 = (f32[8,512]{1,0:T(8,128)S(1)}, f32[8,512]{1,0:T(8,128)S(1)}, u32[]{:S(2)}, u32[]{:S(2)}) collective-permute-start(f32[8,512]{1,0:T(8,128)S(1)} %slice.44), channel_id=1, source_target_pairs={{0,1},{1,0},{2,3},{3,2},{4,5},{5,4},{6,7},{7,6},{8,9},{9,8},{10,11... | collective-permute-start | bytes 49160 | tf_op jit(solution)/shard_map/ppermute | solution.py:548
  74.3 6.7 %shard_map.76 = bf16[16,2,32,512]{3,2,1,0:T(8,128)(2,1)} custom-call(s32[1]{0:T(128)} %bitcast.2.place_ref, bf16[16,65,8,128]{3,2,1,0:T(8,128)(2,1)S(1)} %all-to-all-done.both_ref, bf16[512,1024]{1,0:T(8,128)(2,1)} %constant.66.clone.head_ref, bf16[1024,512]{1,0:T(8,128)(2,1)} %constant.67.clone.back_ref, f32[64,128]{1,0:T(8,128)} %broadcast_in_dim.17.skip_ref, ...), custom_call_target="tpu_custom_call" | custom-call | flops 1610612736 | bytes 2097152 | tf_op jit(solution)/shard_map/pallas_call | solution.py:72
  81.0 6.1 %all-to-all-done.1.long_ref = bf16[16,32,512]{2,1,0:T(8,128)(2,1)S(1)} async-done(((bf16[16,32,512]{2,1,0:T(8,128)(2,1)}), bf16[16,32,512]{2,1,0:T(8,128)(2,1)S(1)}, u32[]{:S(2)}, u32[]{:S(2)}) %all-to-all-start.1) | async-done | bytes 524320 | tf_op jit(solution)/shard_map/all_to_all | solution.py:542
  87.1 4.2 %all-to-all-start.2 = ((bf16[32,32,512]{2,1,0:T(8,128)(2,1)}), bf16[32,32,512]{2,1,0:T(8,128)(2,1)S(1)}, u32[]{:S(2)}, u32[]{:S(2)}) async-start(bf16[32,32,512]{2,1,0:T(8,128)(2,1)} %bitcast.25), calls=%async_computation.2 | async-start | bytes 2097152 | tf_op jit(solution)/shard_map/all_to_all | solution.py:632
  91.5 0.4 collective-permute-start.7
  91.9 2.1 %shard_map.77.gated_ref = bf16[512,512]{1,0:T(8,128)(2,1)} custom-call(bf16[16,32,512]{2,1,0:T(8,128)(2,1)S(1)} %all-to-all-done.1.long_ref, bf16[512,1024]{1,0:T(8,128)(2,1)} %shard_map.74.outer_ref.mine_ref, f32[8,1024]{1,0:T(8,128)} %copy-done.3), custom_call_target="tpu_custom_call" | custom-call | bytes 1572864 | tf_op jit(solution)/shard_map/pallas_call | solution.py:72
  94.0 1.6 %collective-permute-start.5 = (bf16[512,512]{1,0:T(8,128)(2,1)}, bf16[512,512]{1,0:T(8,128)(2,1)S(1)}, u32[]{:S(2)}, u32[]{:S(2)}) collective-permute-start(bf16[512,512]{1,0:T(8,128)(2,1)} %shard_map.77.gated_ref), channel_id=1, source_target_pairs={{0,1},{1,0},{2,3},{3,2},{4,5},{5,4},{6,7},{7,6},{8,9},{9,8},{10,11... | collective-permute-start | bytes 1572872 | tf_op jit(solution)/shard_map/ppermute | solution.py:548
  95.7 3.9 %shard_map.78.sum_ref = bf16[512,2048]{1,0:T(8,128)(2,1)} custom-call(s32[1]{0:T(128)} %bitcast.here_ref, bf16[512,512]{1,0:T(8,128)(2,1)} %shard_map.77.gated_ref, bf16[1024,4096]{1,0:T(8,128)(2,1)} %refs_4_.1), custom_call_target="tpu_custom_call" | custom-call | flops 1073741824 | bytes 4194304 | tf_op jit(solution)/shard_map/pallas_call | solution.py:72
  99.6 1.0 copy-done
  100.6 1.0 copy-done.1
  101.6 14.6 %collective-permute-done.5.sent_ref = bf16[512,512]{1,0:T(8,128)(2,1)S(1)} collective-permute-done((bf16[512,512]{1,0:T(8,128)(2,1)}, bf16[512,512]{1,0:T(8,128)(2,1)S(1)}, u32[]{:S(2)}, u32[]{:S(2)}) %collective-permute-start.5) | collective-permute-done | bytes 524320 | tf_op jit(solution)/shard_map/ppermute | solution.py:548
  116.1 1.3 %all-to-all-done.2 = bf16[32,32,512]{2,1,0:T(8,128)(2,1)S(1)} async-done(((bf16[32,32,512]{2,1,0:T(8,128)(2,1)}), bf16[32,32,512]{2,1,0:T(8,128)(2,1)S(1)}, u32[]{:S(2)}, u32[]{:S(2)}) %all-to-all-start.2) | async-done | bytes 1048608 | tf_op jit(solution)/shard_map/all_to_all | solution.py:632
  117.4 7.3 %shard_map.79 = bf16[512,2048]{1,0:T(8,128)(2,1)} custom-call(s32[2]{0:T(128)S(1)} %pad_add_fusion.place_ref, bf16[512,512]{1,0:T(8,128)(2,1)S(1)} %collective-permute-done.5.sent_ref, bf16[16,2,32,512]{3,2,1,0:T(8,128)(2,1)S(1)} %bitcast.21, f32[2,8,512]{2,1,0:T(8,128)S(1)} %pad_maximum_fusion.first_ref, bf16[512,2048]{1,0:T(8,128)(2,1)} %shard_map.78.sum_ref, ...), custom_call_target="tpu_custom_call" | custom-call | flops 3221225472 | bytes 10485760 | tf_op jit(solution)/shard_map/pallas_call | solution.py:72
  (33 shorter events, 0.7 us)
Async XLA Ops:
  4.8 7.6 %copy-start.6 = (f32[1024]{0:T(1024)S(1)}, f32[1024]{0:T(1024)}, u32[]{:S(2)}) copy-start(f32[1024]{0:T(1024)} %param.10) | copy-start | bytes 12292
  4.8 7.8 %slice-start = ((f32[3,3,1024]{2,1,0:T(4,128)}), f32[3,2,1024]{2,1,0:T(2,128)S(1)}, s32[]{:S(2)}) async-start(f32[3,3,1024]{2,1,0:T(4,128)} %t_ref.1), calls=%async_computation.3 | async-start | bytes 49152 | tf_op jit(solution)/shard_map/slice | solution.py:598
  4.8 12.1 %copy-start.5 = (f32[3,3,1024]{2,1,0:T(4,128)S(1)}, f32[3,3,1024]{2,1,0:T(4,128)}, u32[]{:S(2)}) copy-start(f32[3,3,1024]{2,1,0:T(4,128)} %t_ref.1) | copy-start | bytes 110596
  4.8 53.9 %all-to-all-start = ((bf16[16,65,8,128]{3,2,1,0:T(8,128)(2,1)}), bf16[16,65,8,128]{3,2,1,0:T(8,128)(2,1)S(1)}, u32[]{:S(2)}, u32[]{:S(2)}) async-start(bf16[16,65,8,128]{3,2,1,0:T(8,128)(2,1)} %shard_map.73), calls=%async_computation | async-start | bytes 4259840 | tf_op jit(solution)/shard_map/all_to_all | solution.py:542
  15.4 25.5 %collective-permute-start = (bf16[1024,512]{1,0:T(8,128)(2,1)S(1)}, bf16[1024,512]{1,0:T(8,128)(2,1)}, u32[]{:S(2)}, u32[]{:S(2)}) collective-permute-start(bf16[1024,512]{1,0:T(8,128)(2,1)S(1)} %constant_dynamic-slice_fusion.1), channel_id=1, source_target_pairs={{0,1},{1,0},{2,3},{3,2},{4,5},{5,4},{6,7},{7,6},{8,9},{9,8},{10,11... | collective-permute-start | bytes 3145736 | tf_op jit(solution)/shard_map/ppermute | solution.py:548
  45.2 13.4 %collective-permute-start.1 = (bf16[512,512]{1,0:T(8,128)(2,1)S(1)}, bf16[512,512]{1,0:T(8,128)(2,1)S(1)}, u32[]{:S(2)}, u32[]{:S(2)}) collective-permute-start(bf16[512,512]{1,0:T(8,128)(2,1)S(1)} %slice.42), channel_id=1, source_target_pairs={{0,1},{1,0},{2,3},{3,2},{4,5},{5,4},{6,7},{7,6},{8,9},{9,8},{10,11... | collective-permute-start | bytes 1572872 | tf_op jit(solution)/shard_map/ppermute | solution.py:548
  47.5 2.1 %collective-permute-start.2 = (bf16[2,1024]{1,0:T(2,128)(2,1)S(1)}, bf16[2,1024]{1,0:T(2,128)(2,1)S(1)}, u32[]{:S(2)}, u32[]{:S(2)}) collective-permute-start(bf16[2,1024]{1,0:T(2,128)(2,1)S(1)} %slice_bitcast_fusion.1), channel_id=1, source_target_pairs={{0,2},{2,4},{4,6},{6,8},{8,10},{10,12},{12,14},{14,16},{16,18},{18... | collective-permute-start | bytes 12296 | tf_op jit(solution)/shard_map/ppermute | solution.py:18
  49.6 31.4 %collective-permute-start.3 = (bf16[1024,512]{1,0:T(8,128)(2,1)}, bf16[1024,512]{1,0:T(8,128)(2,1)}, u32[]{:S(2)}, u32[]{:S(2)}) collective-permute-start(bf16[1024,512]{1,0:T(8,128)(2,1)} %collective-permute-done.refs_0_), channel_id=1, source_target_pairs={{0,4},{2,6},{4,0},{6,2},{8,12},{10,14},{12,8},{14,10},{16,20},{18,... | collective-permute-start | bytes 3145736 | tf_op jit(solution)/shard_map/ppermute | solution.py:614
  58.7 6.5 %copy-start.2 = (bf16[512,512]{1,0:T(8,128)(2,1)}, bf16[512,512]{1,0:T(8,128)(2,1)S(1)}, u32[]{:S(2)}) copy-start(bf16[512,512]{1,0:T(8,128)(2,1)S(1)} %collective-permute-done.1.theirs_ref) | copy-start | bytes 1572868
  65.2 21.9 %all-to-all-start.1 = ((bf16[16,32,512]{2,1,0:T(8,128)(2,1)}), bf16[16,32,512]{2,1,0:T(8,128)(2,1)S(1)}, u32[]{:S(2)}, u32[]{:S(2)}) async-start(bf16[16,32,512]{2,1,0:T(8,128)(2,1)} %bitcast.26), calls=%async_computation.1 | async-start | bytes 1048576 | tf_op jit(solution)/shard_map/all_to_all | solution.py:542
  72.7 14.4 %copy-start.3 = (f32[8,1024]{1,0:T(8,128)}, f32[8,1024]{1,0:T(8,128)S(1)}, u32[]{:S(2)}) copy-start(f32[8,1024]{1,0:T(8,128)S(1)} %select_maximum_fusion.first_ref) | copy-start | bytes 98308
  72.7 8.3 %collective-permute-start.4 = (f32[8,512]{1,0:T(8,128)S(1)}, f32[8,512]{1,0:T(8,128)S(1)}, u32[]{:S(2)}, u32[]{:S(2)}) collective-permute-start(f32[8,512]{1,0:T(8,128)S(1)} %slice.44), channel_id=1, source_target_pairs={{0,1},{1,0},{2,3},{3,2},{4,5},{5,4},{6,7},{7,6},{8,9},{9,8},{10,11... | collective-permute-start | bytes 49160 | tf_op jit(solution)/shard_map/ppermute | solution.py:548
  87.1 30.3 %all-to-all-start.2 = ((bf16[32,32,512]{2,1,0:T(8,128)(2,1)}), bf16[32,32,512]{2,1,0:T(8,128)(2,1)S(1)}, u32[]{:S(2)}, u32[]{:S(2)}) async-start(bf16[32,32,512]{2,1,0:T(8,128)(2,1)} %bitcast.25), calls=%async_computation.2 | async-start | bytes 2097152 | tf_op jit(solution)/shard_map/all_to_all | solution.py:632
  91.3 8.2 %collective-permute-start.6 = (bf16[1024,512]{1,0:T(8,128)(2,1)}, bf16[1024,512]{1,0:T(8,128)(2,1)S(1)}, u32[]{:S(2)}, u32[]{:S(2)}) collective-permute-start(bf16[1024,512]{1,0:T(8,128)(2,1)} %collective-permute-done.refs_0_), channel_id=1, source_target_pairs={{0,2},{2,0},{4,6},{6,4},{8,10},{10,8},{12,14},{14,12},{16,18},{18,... | collective-permute-start | bytes 3145736 | tf_op jit(solution)/shard_map/ppermute | solution.py:614
  91.5 8.1 %collective-permute-start.7 = (bf16[1024,512]{1,0:T(8,128)(2,1)}, bf16[1024,512]{1,0:T(8,128)(2,1)S(1)}, u32[]{:S(2)}, u32[]{:S(2)}) collective-permute-start(bf16[1024,512]{1,0:T(8,128)(2,1)} %collective-permute-done.3.refs_2_), channel_id=1, source_target_pairs={{0,2},{2,0},{4,6},{6,4},{8,10},{10,8},{12,14},{14,12},{16,18},{18,... | collective-permute-start | bytes 3145736 | tf_op jit(solution)/shard_map/ppermute | solution.py:614
  94.0 22.1 %collective-permute-start.5 = (bf16[512,512]{1,0:T(8,128)(2,1)}, bf16[512,512]{1,0:T(8,128)(2,1)S(1)}, u32[]{:S(2)}, u32[]{:S(2)}) collective-permute-start(bf16[512,512]{1,0:T(8,128)(2,1)} %shard_map.77.gated_ref), channel_id=1, source_target_pairs={{0,1},{1,0},{2,3},{3,2},{4,5},{5,4},{6,7},{7,6},{8,9},{9,8},{10,11... | collective-permute-start | bytes 1572872 | tf_op jit(solution)/shard_map/ppermute | solution.py:548
  95.7 3.9 %copy-start.4 = (f32[8,1024]{1,0:T(8,128)S(1)}, f32[8,1024]{1,0:T(8,128)}, u32[]{:S(2)}) copy-start(f32[8,1024]{1,0:T(8,128)} %copy-done.3) | copy-start | bytes 98308
  99.6 1.0 copy-start
  100.6 1.0 copy-start.1

commit v5 on v4

--- a/solution.py
+++ b/solution.py
@@ -466,7 +466,7 @@
 ):
     blocks, (weight_ref, o_ref, *scratch) = (refs[:4], refs[4:])
     outer_buf, weight_buf, block_buf, sum_buf, out_buf, gated_ref, sems = scratch
-    here, quarter = (place_ref[0], place_ref[1])
+    here, core = (place_ref[0], place_ref[1])
     rows, used = outer_buf.shape[1:]
     wide = out_buf.shape[2]
     cols = 4 * wide
@@ -476,7 +476,7 @@
         copy.start()
     places, inputs = ([], [])
     for k in range(4):
-        column = pl.multiple_of((quarter ^ k) * wide, wide)
+        column = pl.multiple_of((2 * (core ^ k // 2) + k % 2) * wide, wide)
         places.append(pl.ds(column, wide))
         ours = pl.multiple_of(here * cols + column, wide)
         pairs = [
@@ -600,23 +600,23 @@
     taps = jnp.pad(taps.reshape(6, LANES), ((0, 2), (0, 0)))
     both = exchanged(deal(filters, streams, short_taps, count))
     cols = out_weight.shape[1] // groups
-    wide = cols // 4
-    columns = (1 - here) * cols + position % 4 * wide
-    near = lax.dynamic_slice(out_weight, (0, columns), (chan, wide))
-    near, skip, taps = after((near, skip, taps))
-    near = to_groups([near])[0]
     none = jnp.zeros((1, 2, chan), jnp.float32)
-    none, near = after((none, near))
     outer = outer_gate(streams, 2, none, short_taps[:, 2:], 2)
     theirs = to_groups([outer[:, chan // 2 :]])[0]
+    theirs, skip, taps, out_weight = after((theirs, skip, taps, out_weight))
+    wide = cols // 4
+    columns = [(1 - here) * cols + (position % 2 * 2 + k) * wide for k in range(2)]
+    near = [lax.dynamic_slice(out_weight, (0, c), (chan, wide)) for c in columns]
+    near, tail = after((near, streams[2, rows - 2 :]))
+    near = [to_groups([n])[0] for n in near]
 
     def swapped(value, bit):
         return lax.ppermute(value, "ctx", [(i, i ^ bit) for i in range(count)])
 
-    across = swapped(near, 2)
-    edges = passed_along(streams[2, rows - 2 :], "ctx", 1).astype(jnp.float32)
-    both, outer, theirs, edges = after((both, outer, theirs, edges))
+    both, outer, theirs = after((both, outer, theirs))
     early = long_conv(both, head, back, skip, taps, place, 0)[:, 0]
+    edges, early = after((passed_along(tail, "ctx", 1), early))
+    edges = edges.astype(jnp.float32)
     first = jnp.stack(
         [short_taps[1, 2] * edges[1] + short_taps[2, 2] * edges[0], short_taps[2, 2] * edges[1]]
     )
@@ -624,8 +624,8 @@
     other = to_groups([first[:, chan // 2 :]])[0]
     both, _ = after((both, early))
     late = long_conv(both, head, back, skip, taps, place, 1, copies=groups)
-    late, across = after((late, across))
-    blocks = [near, swapped(near, 1), across, swapped(across, 1)]
+    late, near = after((late, near))
+    blocks = near + [swapped(n, 1) for n in near]
     early, late, other, first = after((exchanged(early), late, other, first))
     gated = gate(early, outer, first)
     sent = to_groups([gated])[0]
@@ -634,7 +634,7 @@
     )
     dealt = dealt.reshape(count, groups, step, rows)
     total = own_term(here[None], gated, out_weight, cols)
-    place = jnp.stack([here, position % 4])
+    place = jnp.stack([here, position % 2])
     first = jnp.stack([first[:, chan // 2 :], other])
     return last_term(place, sent, dealt, first, total, outer, theirs, blocks, out_weight)
 

time: 126 us -> 125 us (level)
  waiting for transfers between devices: 50.8 us -> 48 us
  local copies, waits for them, and re-layouts: 7.93 us -> 9.76 us
    ppermute x4 -> x5, waiting for transfers between devices: 42.6 us -> 30.4 us  [to_groups(): lax.ppermute(value, 'ch', [(g, (g + s) % groups) for g in range(groups)])]
    all_to_all x2, waiting for transfers between devices: 6.14 us -> 16.4 us  [exchanged(): return lax.all_to_all(value, 'ctx', 0, 0, tiled=True)]
    ppermute x3 -> x2, starting transfers between devices: 5.06 us -> 0.58 us  [swapped(): return lax.ppermute(value, 'ctx', [(i, i ^ bit) for i in range(count)])]
    all_to_all x2, starting transfers between devices: 15 us -> 18.9 us  [exchanged(): return lax.all_to_all(value, 'ctx', 0, 0, tiled=True)]
    dynamic_slice x1, local copies, waits for them, and re-layouts: 1.29 us -> 3.03 us  [local(): lax.dynamic_slice(out_weight, (0, c), (chan, wide))]
    ppermute x4 -> x5, starting transfers between devices: 6.21 us -> 6.8 us  [to_groups(): lax.ppermute(value, 'ch', [(g, (g + s) % groups) for g in range(groups)])]
  transfers between devices with their start and end apart: 11 -> 11, of which waited for: 6 -> 7; matrix products, arithmetic and copies ran while one was open for 5% -> 6% of each run, Pallas kernels for 17% -> 17%
where the time goes in v5:
time: 125 us; the launch traced here: 124 us
  waiting for transfers between devices  48 us (38%)
  Pallas kernels  33.8 us (27%)
  starting transfers between devices  32.3 us (26%)
  local copies, waits for them, and re-layouts  9.76 us (8%)
    pallas_call x7, Pallas kernels, run(): return inner(*pinned)  33.8 us
    ppermute x5, waiting for transfers between devices, to_groups(): lax.ppermute(value, 'ch', [(g, (g + s) % groups) for g in range(groups)])  30.4 us
    all_to_all x2, starting transfers between devices, exchanged(): return lax.all_to_all(value, 'ctx', 0, 0, tiled=True)  18.9 us
    all_to_all x2, waiting for transfers between devices, exchanged(): return lax.all_to_all(value, 'ctx', 0, 0, tiled=True)  16.4 us
    ppermute x5, starting transfers between devices, to_groups(): lax.ppermute(value, 'ch', [(g, (g + s) % groups) for g in range(groups)])  6.8 us
    all_to_all x1, starting transfers between devices, local(): lax.all_to_all(late.reshape(count * groups, step, rows), ('ctx', 'ch'), 0...  4.51 us
    dynamic_slice x1, local copies, waits for them, and re-layouts, local(): lax.dynamic_slice(out_weight, (0, c), (chan, wide))  3.03 us
  transfers between devices with their start and end apart: 11, of which 7 were waited for; matrix products, arithmetic and copies ran while one was open for 6% of the time, Pallas kernels for 17%

profile of v5, /device:TPU:0, one launch (start us, length us, event | category | flops | bytes accessed | tf_op | source)
XLA Modules:
  0.0 124.3 jit_solution(14092914488891345648)
XLA Ops:
  0.0 4.8 %shard_map.74 = bf16[16,65,8,128]{3,2,1,0:T(8,128)(2,1)} custom-call(bf16[512,1024]{1,0:T(8,128)(2,1)} %f_ref.1, bf16[3,512,1024]{2,1,0:T(8,128)(2,1)} %bitcast.19, f32[3,3,1024]{2,1,0:T(4,128)} %t_ref.1), custom_call_target="tpu_custom_call" | custom-call | bytes 5242880 | tf_op jit(solution)/shard_map/pallas_call | solution.py:72
  4.8 7.5 %all-to-all-start = ((bf16[16,65,8,128]{3,2,1,0:T(8,128)(2,1)}), bf16[16,65,8,128]{3,2,1,0:T(8,128)(2,1)S(1)}, u32[]{:S(2)}, u32[]{:S(2)}) async-start(bf16[16,65,8,128]{3,2,1,0:T(8,128)(2,1)} %shard_map.74), calls=%async_computation | async-start | bytes 4259840 | tf_op jit(solution)/shard_map/all_to_all | solution.py:542
  12.3 0.6 slice.32.t_ref
  13.0 0.6 broadcast_in_dim.12.e_ref
  13.6 2.6 %shard_map.73.outer_ref.mine_ref = bf16[512,1024]{1,0:T(8,128)(2,1)} custom-call(bf16[3,512,1024]{2,1,0:T(8,128)(2,1)} %bitcast.20, f32[1,2,1024]{2,1,0:T(2,128)} %broadcast_in_dim.12.e_ref, f32[3,1,1024]{2,1,0:T(1,128)} %slice.32.t_ref), custom_call_target="tpu_custom_call" | custom-call | bytes 2097152 | tf_op jit(solution)/shard_map/pallas_call | solution.py:72
  16.2 1.1 slice.42
  17.3 1.6 %collective-permute-start = (bf16[512,512]{1,0:T(8,128)(2,1)S(1)}, bf16[512,512]{1,0:T(8,128)(2,1)S(1)}, u32[]{:S(2)}, u32[]{:S(2)}) collective-permute-start(bf16[512,512]{1,0:T(8,128)(2,1)S(1)} %slice.42), channel_id=1, source_target_pairs={{0,1},{1,0},{2,3},{3,2},{4,5},{5,4},{6,7},{7,6},{8,9},{9,8},{10,11... | collective-permute-start | bytes 1572872 | tf_op jit(solution)/shard_map/ppermute | solution.py:548
  19.2 0.6 pad.8.taps_ref
  19.8 0.7 slice_bitcast_fusion.1
  20.5 11.1 %collective-permute-done.theirs_ref = bf16[512,512]{1,0:T(8,128)(2,1)S(1)} collective-permute-done((bf16[512,512]{1,0:T(8,128)(2,1)S(1)}, bf16[512,512]{1,0:T(8,128)(2,1)S(1)}, u32[]{:S(2)}, u32[]{:S(2)}) %collective-permute-start) | collective-permute-done | bytes 524320 | tf_op jit(solution)/shard_map/ppermute | solution.py:548
  31.6 0.8 broadcast_in_dim.14.skip_ref
  32.4 3.0 %constant_dynamic-slice_fusion = (bf16[1024,512]{1,0:T(8,128)(2,1)}, bf16[1024,512]{1,0:T(8,128)(2,1)}) fusion(bf16[1024,4096]{1,0:T(8,128)(2,1)} %refs_4_, s32[]{:T(128)S(6)} %select_n.35, s32[]{:T(128)S(6)} %select_n.34), kind=kLoop, calls=%fused_computation.10 | loop fusion | bytes 4194312 | tf_op jit(solution)/shard_map/dynamic_slice | solution.py:609
  35.4 1.5 %collective-permute-start.1 = (bf16[2,1024]{1,0:T(2,128)(2,1)S(1)}, bf16[2,1024]{1,0:T(2,128)(2,1)S(1)}, u32[]{:S(2)}, u32[]{:S(2)}) collective-permute-start(bf16[2,1024]{1,0:T(2,128)(2,1)S(1)} %slice_bitcast_fusion.1), channel_id=1, source_target_pairs={{0,2},{2,4},{4,6},{6,8},{8,10},{10,12},{12,14},{14,16},{16,18},{18... | collective-permute-start | bytes 12296 | tf_op jit(solution)/shard_map/ppermute | solution.py:18
  37.0 1.6 %collective-permute-start.2 = (bf16[1024,512]{1,0:T(8,128)(2,1)}, bf16[1024,512]{1,0:T(8,128)(2,1)}, u32[]{:S(2)}, u32[]{:S(2)}) collective-permute-start(bf16[1024,512]{1,0:T(8,128)(2,1)} %get-tuple-element.33), channel_id=1, source_target_pairs={{0,1},{1,0},{2,3},{3,2},{4,5},{5,4},{6,7},{7,6},{8,9},{9,8},{10,11... | collective-permute-start | bytes 3145736 | tf_op jit(solution)/shard_map/ppermute | solution.py:548
  38.5 0.5 collective-permute-start.3
  39.0 14.9 %all-to-all-done.both_ref = bf16[16,65,8,128]{3,2,1,0:T(8,128)(2,1)S(1)} async-done(((bf16[16,65,8,128]{3,2,1,0:T(8,128)(2,1)}), bf16[16,65,8,128]{3,2,1,0:T(8,128)(2,1)S(1)}, u32[]{:S(2)}, u32[]{:S(2)}) %all-to-all-start) | async-done | bytes 2129952 | tf_op jit(solution)/shard_map/all_to_all | solution.py:542
  54.0 6.5 %shard_map.75 = bf16[16,1,32,512]{3,2,1,0:T(8,128)(2,1)} custom-call(s32[1]{0:T(128)} %bitcast.1.place_ref, bf16[16,65,8,128]{3,2,1,0:T(8,128)(2,1)S(1)} %all-to-all-done.both_ref, bf16[512,1024]{1,0:T(8,128)(2,1)} %constant.62.clone.head_ref, bf16[1024,512]{1,0:T(8,128)(2,1)} %constant.63.clone.back_ref, f32[64,128]{1,0:T(8,128)} %broadcast_in_dim.14.skip_ref, ...), custom_call_target="tpu_custom_call" | custom-call | flops 1610612736 | bytes 2097152 | tf_op jit(solution)/shard_map/pallas_call | solution.py:72
  60.5 11.4 %all-to-all-start.1 = ((bf16[16,32,512]{2,1,0:T(8,128)(2,1)}), bf16[16,32,512]{2,1,0:T(8,128)(2,1)S(1)}, u32[]{:S(2)}, u32[]{:S(2)}) async-start(bf16[16,32,512]{2,1,0:T(8,128)(2,1)} %bitcast.23), calls=%async_computation.1 | async-start | bytes 1048576 | tf_op jit(solution)/shard_map/all_to_all | solution.py:542
  72.0 1.6 %collective-permute-start.4 = (f32[8,512]{1,0:T(8,128)S(1)}, f32[8,512]{1,0:T(8,128)S(1)}, u32[]{:S(2)}, u32[]{:S(2)}) collective-permute-start(f32[8,512]{1,0:T(8,128)S(1)} %slice.46), channel_id=1, source_target_pairs={{0,1},{1,0},{2,3},{3,2},{4,5},{5,4},{6,7},{7,6},{8,9},{9,8},{10,11... | collective-permute-start | bytes 49160 | tf_op jit(solution)/shard_map/ppermute | solution.py:548
  73.5 6.7 %shard_map.76 = bf16[16,2,32,512]{3,2,1,0:T(8,128)(2,1)} custom-call(s32[1]{0:T(128)} %bitcast.1.place_ref, bf16[16,65,8,128]{3,2,1,0:T(8,128)(2,1)S(1)} %all-to-all-done.both_ref, bf16[512,1024]{1,0:T(8,128)(2,1)} %constant.62.clone.head_ref, bf16[1024,512]{1,0:T(8,128)(2,1)} %constant.63.clone.back_ref, f32[64,128]{1,0:T(8,128)} %broadcast_in_dim.14.skip_ref, ...), custom_call_target="tpu_custom_call" | custom-call | flops 1610612736 | bytes 2097152 | tf_op jit(solution)/shard_map/pallas_call | solution.py:72
  80.2 4.4 %collective-permute-done.3.refs_1_ = bf16[1024,512]{1,0:T(8,128)(2,1)} collective-permute-done((bf16[1024,512]{1,0:T(8,128)(2,1)}, bf16[1024,512]{1,0:T(8,128)(2,1)}, u32[]{:S(2)}, u32[]{:S(2)}) %collective-permute-start.3) | collective-permute-done | bytes 1048608 | tf_op jit(solution)/shard_map/ppermute | solution.py:548
  84.9 1.4 %all-to-all-done.1.long_ref = bf16[16,32,512]{2,1,0:T(8,128)(2,1)S(1)} async-done(((bf16[16,32,512]{2,1,0:T(8,128)(2,1)}), bf16[16,32,512]{2,1,0:T(8,128)(2,1)S(1)}, u32[]{:S(2)}, u32[]{:S(2)}) %all-to-all-start.1) | async-done | bytes 524320 | tf_op jit(solution)/shard_map/all_to_all | solution.py:542
  86.4 4.5 %all-to-all-start.2 = ((bf16[32,32,512]{2,1,0:T(8,128)(2,1)}), bf16[32,32,512]{2,1,0:T(8,128)(2,1)S(1)}, u32[]{:S(2)}, u32[]{:S(2)}) async-start(bf16[32,32,512]{2,1,0:T(8,128)(2,1)} %bitcast.22), calls=%async_computation.2 | async-start | bytes 2097152 | tf_op jit(solution)/shard_map/all_to_all | solution.py:632
  91.0 0.4 collective-permute-start.7
  91.5 2.1 %shard_map.77.gated_ref = bf16[512,512]{1,0:T(8,128)(2,1)} custom-call(bf16[16,32,512]{2,1,0:T(8,128)(2,1)S(1)} %all-to-all-done.1.long_ref, bf16[512,1024]{1,0:T(8,128)(2,1)} %shard_map.73.outer_ref.mine_ref, f32[8,1024]{1,0:T(8,128)} %copy-done.3), custom_call_target="tpu_custom_call" | custom-call | bytes 1572864 | tf_op jit(solution)/shard_map/pallas_call | solution.py:72
  93.6 1.6 %collective-permute-start.5 = (bf16[512,512]{1,0:T(8,128)(2,1)}, bf16[512,512]{1,0:T(8,128)(2,1)S(1)}, u32[]{:S(2)}, u32[]{:S(2)}) collective-permute-start(bf16[512,512]{1,0:T(8,128)(2,1)} %shard_map.77.gated_ref), channel_id=1, source_target_pairs={{0,1},{1,0},{2,3},{3,2},{4,5},{5,4},{6,7},{7,6},{8,9},{9,8},{10,11... | collective-permute-start | bytes 1572872 | tf_op jit(solution)/shard_map/ppermute | solution.py:548
  95.2 3.8 %shard_map.78.sum_ref = bf16[512,2048]{1,0:T(8,128)(2,1)} custom-call(s32[1]{0:T(128)} %bitcast.here_ref, bf16[512,512]{1,0:T(8,128)(2,1)} %shard_map.77.gated_ref, bf16[1024,4096]{1,0:T(8,128)(2,1)} %refs_4_), custom_call_target="tpu_custom_call" | custom-call | flops 1073741824 | bytes 4194304 | tf_op jit(solution)/shard_map/pallas_call | solution.py:72
  99.1 1.0 copy-done
  100.1 1.0 copy-done.1
  101.0 14.6 %collective-permute-done.5.sent_ref = bf16[512,512]{1,0:T(8,128)(2,1)S(1)} collective-permute-done((bf16[512,512]{1,0:T(8,128)(2,1)}, bf16[512,512]{1,0:T(8,128)(2,1)S(1)}, u32[]{:S(2)}, u32[]{:S(2)}) %collective-permute-start.5) | collective-permute-done | bytes 524320 | tf_op jit(solution)/shard_map/ppermute | solution.py:548
  115.7 1.3 %all-to-all-done.2 = bf16[32,32,512]{2,1,0:T(8,128)(2,1)S(1)} async-done(((bf16[32,32,512]{2,1,0:T(8,128)(2,1)}), bf16[32,32,512]{2,1,0:T(8,128)(2,1)S(1)}, u32[]{:S(2)}, u32[]{:S(2)}) %all-to-all-start.2) | async-done | bytes 1048608 | tf_op jit(solution)/shard_map/all_to_all | solution.py:632
  116.9 7.3 %shard_map.79 = bf16[512,2048]{1,0:T(8,128)(2,1)} custom-call(s32[2]{0:T(128)S(1)} %pad_add_fusion.place_ref, bf16[512,512]{1,0:T(8,128)(2,1)S(1)} %collective-permute-done.5.sent_ref, bf16[16,2,32,512]{3,2,1,0:T(8,128)(2,1)S(1)} %bitcast.18, f32[2,8,512]{2,1,0:T(8,128)S(1)} %pad_maximum_fusion.first_ref, bf16[512,2048]{1,0:T(8,128)(2,1)} %shard_map.78.sum_ref, ...), custom_call_target="tpu_custom_call" | custom-call | flops 3221225472 | bytes 10485760 | tf_op jit(solution)/shard_map/pallas_call | solution.py:72
  (33 shorter events, 0.9 us)
Async XLA Ops:
  4.8 7.6 %copy-start.5 = (f32[3,3,1024]{2,1,0:T(4,128)S(1)}, f32[3,3,1024]{2,1,0:T(4,128)}, u32[]{:S(2)}) copy-start(f32[3,3,1024]{2,1,0:T(4,128)} %t_ref.1) | copy-start | bytes 110596
  4.8 49.2 %all-to-all-start = ((bf16[16,65,8,128]{3,2,1,0:T(8,128)(2,1)}), bf16[16,65,8,128]{3,2,1,0:T(8,128)(2,1)S(1)}, u32[]{:S(2)}, u32[]{:S(2)}) async-start(bf16[16,65,8,128]{3,2,1,0:T(8,128)(2,1)} %shard_map.74), calls=%async_computation | async-start | bytes 4259840 | tf_op jit(solution)/shard_map/all_to_all | solution.py:542
  12.3 6.5 %copy-start.6 = (f32[1024]{0:T(1024)S(1)}, f32[1024]{0:T(1024)}, u32[]{:S(2)}) copy-start(f32[1024]{0:T(1024)} %param.10) | copy-start | bytes 12292
  12.3 6.7 %slice-start = ((f32[3,3,1024]{2,1,0:T(4,128)}), f32[3,2,1024]{2,1,0:T(2,128)S(1)}, s32[]{:S(2)}) async-start(f32[3,3,1024]{2,1,0:T(4,128)} %t_ref.1), calls=%async_computation.3 | async-start | bytes 49152 | tf_op jit(solution)/shard_map/slice | solution.py:598
  17.3 14.3 %collective-permute-start = (bf16[512,512]{1,0:T(8,128)(2,1)S(1)}, bf16[512,512]{1,0:T(8,128)(2,1)S(1)}, u32[]{:S(2)}, u32[]{:S(2)}) collective-permute-start(bf16[512,512]{1,0:T(8,128)(2,1)S(1)} %slice.42), channel_id=1, source_target_pairs={{0,1},{1,0},{2,3},{3,2},{4,5},{5,4},{6,7},{7,6},{8,9},{9,8},{10,11... | collective-permute-start | bytes 1572872 | tf_op jit(solution)/shard_map/ppermute | solution.py:548
  31.6 28.9 %copy-start.2 = (bf16[512,512]{1,0:T(8,128)(2,1)}, bf16[512,512]{1,0:T(8,128)(2,1)S(1)}, u32[]{:S(2)}) copy-start(bf16[512,512]{1,0:T(8,128)(2,1)S(1)} %collective-permute-done.theirs_ref) | copy-start | bytes 1572868
  35.4 25.1 %collective-permute-start.1 = (bf16[2,1024]{1,0:T(2,128)(2,1)S(1)}, bf16[2,1024]{1,0:T(2,128)(2,1)S(1)}, u32[]{:S(2)}, u32[]{:S(2)}) collective-permute-start(bf16[2,1024]{1,0:T(2,128)(2,1)S(1)} %slice_bitcast_fusion.1), channel_id=1, source_target_pairs={{0,2},{2,4},{4,6},{6,8},{8,10},{10,12},{12,14},{14,16},{16,18},{18... | collective-permute-start | bytes 12296 | tf_op jit(solution)/shard_map/ppermute | solution.py:18
  37.0 43.3 %collective-permute-start.2 = (bf16[1024,512]{1,0:T(8,128)(2,1)}, bf16[1024,512]{1,0:T(8,128)(2,1)}, u32[]{:S(2)}, u32[]{:S(2)}) collective-permute-start(bf16[1024,512]{1,0:T(8,128)(2,1)} %get-tuple-element.33), channel_id=1, source_target_pairs={{0,1},{1,0},{2,3},{3,2},{4,5},{5,4},{6,7},{7,6},{8,9},{9,8},{10,11... | collective-permute-start | bytes 3145736 | tf_op jit(solution)/shard_map/ppermute | solution.py:548
  38.5 46.2 %collective-permute-start.3 = (bf16[1024,512]{1,0:T(8,128)(2,1)}, bf16[1024,512]{1,0:T(8,128)(2,1)}, u32[]{:S(2)}, u32[]{:S(2)}) collective-permute-start(bf16[1024,512]{1,0:T(8,128)(2,1)} %get-tuple-element.34), channel_id=1, source_target_pairs={{0,1},{1,0},{2,3},{3,2},{4,5},{5,4},{6,7},{7,6},{8,9},{9,8},{10,11... | collective-permute-start | bytes 3145736 | tf_op jit(solution)/shard_map/ppermute | solution.py:548
  60.5 25.8 %all-to-all-start.1 = ((bf16[16,32,512]{2,1,0:T(8,128)(2,1)}), bf16[16,32,512]{2,1,0:T(8,128)(2,1)S(1)}, u32[]{:S(2)}, u32[]{:S(2)}) async-start(bf16[16,32,512]{2,1,0:T(8,128)(2,1)} %bitcast.23), calls=%async_computation.1 | async-start | bytes 1048576 | tf_op jit(solution)/shard_map/all_to_all | solution.py:542
  71.9 14.4 %copy-start.3 = (f32[8,1024]{1,0:T(8,128)}, f32[8,1024]{1,0:T(8,128)S(1)}, u32[]{:S(2)}) copy-start(f32[8,1024]{1,0:T(8,128)S(1)} %select_maximum_fusion.first_ref) | copy-start | bytes 98308
  72.0 12.9 %collective-permute-start.4 = (f32[8,512]{1,0:T(8,128)S(1)}, f32[8,512]{1,0:T(8,128)S(1)}, u32[]{:S(2)}, u32[]{:S(2)}) collective-permute-start(f32[8,512]{1,0:T(8,128)S(1)} %slice.46), channel_id=1, source_target_pairs={{0,1},{1,0},{2,3},{3,2},{4,5},{5,4},{6,7},{7,6},{8,9},{9,8},{10,11... | collective-permute-start | bytes 49160 | tf_op jit(solution)/shard_map/ppermute | solution.py:548
  86.4 30.6 %all-to-all-start.2 = ((bf16[32,32,512]{2,1,0:T(8,128)(2,1)}), bf16[32,32,512]{2,1,0:T(8,128)(2,1)S(1)}, u32[]{:S(2)}, u32[]{:S(2)}) async-start(bf16[32,32,512]{2,1,0:T(8,128)(2,1)} %bitcast.22), calls=%async_computation.2 | async-start | bytes 2097152 | tf_op jit(solution)/shard_map/all_to_all | solution.py:632
  90.9 8.2 %collective-permute-start.6 = (bf16[1024,512]{1,0:T(8,128)(2,1)}, bf16[1024,512]{1,0:T(8,128)(2,1)S(1)}, u32[]{:S(2)}, u32[]{:S(2)}) collective-permute-start(bf16[1024,512]{1,0:T(8,128)(2,1)} %collective-permute-done.2.refs_0_), channel_id=1, source_target_pairs={{0,2},{2,0},{4,6},{6,4},{8,10},{10,8},{12,14},{14,12},{16,18},{18,... | collective-permute-start | bytes 3145736 | tf_op jit(solution)/shard_map/ppermute | solution.py:614
  91.0 8.1 %collective-permute-start.7 = (bf16[1024,512]{1,0:T(8,128)(2,1)}, bf16[1024,512]{1,0:T(8,128)(2,1)S(1)}, u32[]{:S(2)}, u32[]{:S(2)}) collective-permute-start(bf16[1024,512]{1,0:T(8,128)(2,1)} %collective-permute-done.3.refs_1_), channel_id=1, source_target_pairs={{0,2},{2,0},{4,6},{6,4},{8,10},{10,8},{12,14},{14,12},{16,18},{18,... | collective-permute-start | bytes 3145736 | tf_op jit(solution)/shard_map/ppermute | solution.py:614
  93.6 22.1 %collective-permute-start.5 = (bf16[512,512]{1,0:T(8,128)(2,1)}, bf16[512,512]{1,0:T(8,128)(2,1)S(1)}, u32[]{:S(2)}, u32[]{:S(2)}) collective-permute-start(bf16[512,512]{1,0:T(8,128)(2,1)} %shard_map.77.gated_ref), channel_id=1, source_target_pairs={{0,1},{1,0},{2,3},{3,2},{4,5},{5,4},{6,7},{7,6},{8,9},{9,8},{10,11... | collective-permute-start | bytes 1572872 | tf_op jit(solution)/shard_map/ppermute | solution.py:548
  95.2 3.8 %copy-start.4 = (f32[8,1024]{1,0:T(8,128)S(1)}, f32[8,1024]{1,0:T(8,128)}, u32[]{:S(2)}) copy-start(f32[8,1024]{1,0:T(8,128)} %copy-done.3) | copy-start | bytes 98308
  99.1 1.0 copy-start
  100.1 1.0 copy-start.1

commit v6 on v5

--- a/solution.py
+++ b/solution.py
@@ -600,13 +600,13 @@
     taps = jnp.pad(taps.reshape(6, LANES), ((0, 2), (0, 0)))
     both = exchanged(deal(filters, streams, short_taps, count))
     cols = out_weight.shape[1] // groups
-    none = jnp.zeros((1, 2, chan), jnp.float32)
-    outer = outer_gate(streams, 2, none, short_taps[:, 2:], 2)
-    theirs = to_groups([outer[:, chan // 2 :]])[0]
-    theirs, skip, taps, out_weight = after((theirs, skip, taps, out_weight))
     wide = cols // 4
     columns = [(1 - here) * cols + (position % 2 * 2 + k) * wide for k in range(2)]
     near = [lax.dynamic_slice(out_weight, (0, c), (chan, wide)) for c in columns]
+    near, none = after((near, jnp.zeros((1, 2, chan), jnp.float32)))
+    outer = outer_gate(streams, 2, none, short_taps[:, 2:], 2)
+    theirs = to_groups([outer[:, chan // 2 :]])[0]
+    near, skip, taps = after((near, skip, taps))
     near, tail = after((near, streams[2, rows - 2 :]))
     near = [to_groups([n])[0] for n in near]
 

time: 125 us -> 125 us (level)
    ppermute x5, waiting for transfers between devices: 30.4 us -> 21.4 us  [to_groups(): lax.ppermute(value, 'ch', [(g, (g + s) % groups) for g in range(groups)])]
    all_to_all x2, waiting for transfers between devices: 16.4 us -> 25 us  [exchanged(): return lax.all_to_all(value, 'ctx', 0, 0, tiled=True)]
  transfers between devices with their start and end apart: 11 -> 11, of which waited for: 7 -> 5; matrix products, arithmetic and copies ran while one was open for 6% -> 6% of each run, Pallas kernels for 17% -> 18%
where the time goes in v6:
time: 125 us; the launch traced here: 124 us
  waiting for transfers between devices  47.6 us (38%)
  Pallas kernels  33.8 us (27%)
  starting transfers between devices  32.4 us (26%)
  local copies, waits for them, and re-layouts  9.64 us (8%)
    pallas_call x7, Pallas kernels, run(): return inner(*pinned)  33.8 us
    all_to_all x2, waiting for transfers between devices, exchanged(): return lax.all_to_all(value, 'ctx', 0, 0, tiled=True)  25 us
    ppermute x5, waiting for transfers between devices, to_groups(): lax.ppermute(value, 'ch', [(g, (g + s) % groups) for g in range(groups)])  21.4 us
    all_to_all x2, starting transfers between devices, exchanged(): return lax.all_to_all(value, 'ctx', 0, 0, tiled=True)  18.9 us
    ppermute x5, starting transfers between devices, to_groups(): lax.ppermute(value, 'ch', [(g, (g + s) % groups) for g in range(groups)])  6.81 us
    all_to_all x1, starting transfers between devices, local(): lax.all_to_all(late.reshape(count * groups, step, rows), ('ctx', 'ch'), 0...  4.19 us
    dynamic_slice x1, local copies, waits for them, and re-layouts, local(): lax.dynamic_slice(out_weight, (0, c), (chan, wide))  3.02 us
  transfers between devices with their start and end apart: 11, of which 5 were waited for; matrix products, arithmetic and copies ran while one was open for 6% of the time, Pallas kernels for 18%

profile of v6, /device:TPU:0, one launch (start us, length us, event | category | flops | bytes accessed | tf_op | source)
XLA Modules:
  0.0 124.1 jit_solution(12115244370985169173)
XLA Ops:
  0.0 4.8 %shard_map.73 = bf16[16,65,8,128]{3,2,1,0:T(8,128)(2,1)} custom-call(bf16[512,1024]{1,0:T(8,128)(2,1)} %f_ref.1, bf16[3,512,1024]{2,1,0:T(8,128)(2,1)} %bitcast.19, f32[3,3,1024]{2,1,0:T(4,128)} %t_ref.1), custom_call_target="tpu_custom_call" | custom-call | bytes 5242880 | tf_op jit(solution)/shard_map/pallas_call | solution.py:72
  4.8 7.5 %all-to-all-start = ((bf16[16,65,8,128]{3,2,1,0:T(8,128)(2,1)}), bf16[16,65,8,128]{3,2,1,0:T(8,128)(2,1)S(1)}, u32[]{:S(2)}, u32[]{:S(2)}) async-start(bf16[16,65,8,128]{3,2,1,0:T(8,128)(2,1)} %shard_map.73), calls=%async_computation | async-start | bytes 4259840 | tf_op jit(solution)/shard_map/all_to_all | solution.py:542
  12.4 0.6 slice.34.t_ref
  13.0 3.0 %constant_dynamic-slice_fusion.1 = (bf16[1024,512]{1,0:T(8,128)(2,1)}, bf16[1024,512]{1,0:T(8,128)(2,1)}) fusion(bf16[1024,4096]{1,0:T(8,128)(2,1)} %refs_4_.1, s32[]{:T(128)S(6)} %select_n.32, s32[]{:T(128)S(6)} %select_n.31), kind=kLoop, calls=%fused_computation.11 | loop fusion | bytes 4194312 | tf_op jit(solution)/shard_map/dynamic_slice | solution.py:605
  16.0 0.6 broadcast_in_dim.12.e_ref
  16.6 2.6 %shard_map.74.outer_ref.mine_ref = bf16[512,1024]{1,0:T(8,128)(2,1)} custom-call(bf16[3,512,1024]{2,1,0:T(8,128)(2,1)} %bitcast.20, f32[1,2,1024]{2,1,0:T(2,128)} %broadcast_in_dim.12.e_ref, f32[3,1,1024]{2,1,0:T(1,128)} %slice.34.t_ref), custom_call_target="tpu_custom_call" | custom-call | bytes 2097152 | tf_op jit(solution)/shard_map/pallas_call | solution.py:72
  19.2 1.1 slice.43
  20.3 1.6 %collective-permute-start.1 = (bf16[512,512]{1,0:T(8,128)(2,1)S(1)}, bf16[512,512]{1,0:T(8,128)(2,1)S(1)}, u32[]{:S(2)}, u32[]{:S(2)}) collective-permute-start(bf16[512,512]{1,0:T(8,128)(2,1)S(1)} %slice.43), channel_id=1, source_target_pairs={{0,1},{1,0},{2,3},{3,2},{4,5},{5,4},{6,7},{7,6},{8,9},{9,8},{10,11... | collective-permute-start | bytes 1572872 | tf_op jit(solution)/shard_map/ppermute | solution.py:548
  22.3 0.6 pad.8.taps_ref
  22.9 0.7 broadcast_in_dim.14.skip_ref
  23.6 0.7 slice_bitcast_fusion.1
  24.3 2.0 %collective-permute-start = (bf16[2,1024]{1,0:T(2,128)(2,1)S(1)}, bf16[2,1024]{1,0:T(2,128)(2,1)S(1)}, u32[]{:S(2)}, u32[]{:S(2)}) collective-permute-start(bf16[2,1024]{1,0:T(2,128)(2,1)S(1)} %slice_bitcast_fusion.1), channel_id=1, source_target_pairs={{0,2},{2,4},{4,6},{6,8},{8,10},{10,12},{12,14},{14,16},{16,18},{18... | collective-permute-start | bytes 12296 | tf_op jit(solution)/shard_map/ppermute | solution.py:18
  26.3 0.6 collective-permute-start.2
  26.9 1.5 %collective-permute-start.3 = (bf16[1024,512]{1,0:T(8,128)(2,1)}, bf16[1024,512]{1,0:T(8,128)(2,1)}, u32[]{:S(2)}, u32[]{:S(2)}) collective-permute-start(bf16[1024,512]{1,0:T(8,128)(2,1)} %get-tuple-element.40), channel_id=1, source_target_pairs={{0,1},{1,0},{2,3},{3,2},{4,5},{5,4},{6,7},{7,6},{8,9},{9,8},{10,11... | collective-permute-start | bytes 3145736 | tf_op jit(solution)/shard_map/ppermute | solution.py:548
  28.4 6.8 %collective-permute-done.1.theirs_ref = bf16[512,512]{1,0:T(8,128)(2,1)S(1)} collective-permute-done((bf16[512,512]{1,0:T(8,128)(2,1)S(1)}, bf16[512,512]{1,0:T(8,128)(2,1)S(1)}, u32[]{:S(2)}, u32[]{:S(2)}) %collective-permute-start.1) | collective-permute-done | bytes 524320 | tf_op jit(solution)/shard_map/ppermute | solution.py:548
  35.1 18.9 %all-to-all-done.both_ref = bf16[16,65,8,128]{3,2,1,0:T(8,128)(2,1)S(1)} async-done(((bf16[16,65,8,128]{3,2,1,0:T(8,128)(2,1)}), bf16[16,65,8,128]{3,2,1,0:T(8,128)(2,1)S(1)}, u32[]{:S(2)}, u32[]{:S(2)}) %all-to-all-start) | async-done | bytes 2129952 | tf_op jit(solution)/shard_map/all_to_all | solution.py:542
  54.0 6.5 %shard_map.75 = bf16[16,1,32,512]{3,2,1,0:T(8,128)(2,1)} custom-call(s32[1]{0:T(128)} %bitcast.1.place_ref, bf16[16,65,8,128]{3,2,1,0:T(8,128)(2,1)S(1)} %all-to-all-done.both_ref, bf16[512,1024]{1,0:T(8,128)(2,1)} %constant.62.clone.head_ref, bf16[1024,512]{1,0:T(8,128)(2,1)} %constant.63.clone.back_ref, f32[64,128]{1,0:T(8,128)} %broadcast_in_dim.14.skip_ref, ...), custom_call_target="tpu_custom_call" | custom-call | flops 1610612736 | bytes 2097152 | tf_op jit(solution)/shard_map/pallas_call | solution.py:72
  60.6 11.4 %all-to-all-start.1 = ((bf16[16,32,512]{2,1,0:T(8,128)(2,1)}), bf16[16,32,512]{2,1,0:T(8,128)(2,1)S(1)}, u32[]{:S(2)}, u32[]{:S(2)}) async-start(bf16[16,32,512]{2,1,0:T(8,128)(2,1)} %bitcast.23), calls=%async_computation.1 | async-start | bytes 1048576 | tf_op jit(solution)/shard_map/all_to_all | solution.py:542
  72.0 1.6 %collective-permute-start.4 = (f32[8,512]{1,0:T(8,128)S(1)}, f32[8,512]{1,0:T(8,128)S(1)}, u32[]{:S(2)}, u32[]{:S(2)}) collective-permute-start(f32[8,512]{1,0:T(8,128)S(1)} %slice.46), channel_id=1, source_target_pairs={{0,1},{1,0},{2,3},{3,2},{4,5},{5,4},{6,7},{7,6},{8,9},{9,8},{10,11... | collective-permute-start | bytes 49160 | tf_op jit(solution)/shard_map/ppermute | solution.py:548
  73.6 6.7 %shard_map.76 = bf16[16,2,32,512]{3,2,1,0:T(8,128)(2,1)} custom-call(s32[1]{0:T(128)} %bitcast.1.place_ref, bf16[16,65,8,128]{3,2,1,0:T(8,128)(2,1)S(1)} %all-to-all-done.both_ref, bf16[512,1024]{1,0:T(8,128)(2,1)} %constant.62.clone.head_ref, bf16[1024,512]{1,0:T(8,128)(2,1)} %constant.63.clone.back_ref, f32[64,128]{1,0:T(8,128)} %broadcast_in_dim.14.skip_ref, ...), custom_call_target="tpu_custom_call" | custom-call | flops 1610612736 | bytes 2097152 | tf_op jit(solution)/shard_map/pallas_call | solution.py:72
  80.3 6.1 %all-to-all-done.1.long_ref = bf16[16,32,512]{2,1,0:T(8,128)(2,1)S(1)} async-done(((bf16[16,32,512]{2,1,0:T(8,128)(2,1)}), bf16[16,32,512]{2,1,0:T(8,128)(2,1)S(1)}, u32[]{:S(2)}, u32[]{:S(2)}) %all-to-all-start.1) | async-done | bytes 524320 | tf_op jit(solution)/shard_map/all_to_all | solution.py:542
  86.4 4.2 %all-to-all-start.2 = ((bf16[32,32,512]{2,1,0:T(8,128)(2,1)}), bf16[32,32,512]{2,1,0:T(8,128)(2,1)S(1)}, u32[]{:S(2)}, u32[]{:S(2)}) async-start(bf16[32,32,512]{2,1,0:T(8,128)(2,1)} %bitcast.22), calls=%async_computation.2 | async-start | bytes 2097152 | tf_op jit(solution)/shard_map/all_to_all | solution.py:632
  90.6 0.1 collective-permute-start.6
  90.7 0.4 collective-permute-start.7
  91.2 2.1 %shard_map.77.gated_ref = bf16[512,512]{1,0:T(8,128)(2,1)} custom-call(bf16[16,32,512]{2,1,0:T(8,128)(2,1)S(1)} %all-to-all-done.1.long_ref, bf16[512,1024]{1,0:T(8,128)(2,1)} %shard_map.74.outer_ref.mine_ref, f32[8,1024]{1,0:T(8,128)} %copy-done.3), custom_call_target="tpu_custom_call" | custom-call | bytes 1572864 | tf_op jit(solution)/shard_map/pallas_call | solution.py:72
  93.3 1.6 %collective-permute-start.5 = (bf16[512,512]{1,0:T(8,128)(2,1)}, bf16[512,512]{1,0:T(8,128)(2,1)S(1)}, u32[]{:S(2)}, u32[]{:S(2)}) collective-permute-start(bf16[512,512]{1,0:T(8,128)(2,1)} %shard_map.77.gated_ref), channel_id=1, source_target_pairs={{0,1},{1,0},{2,3},{3,2},{4,5},{5,4},{6,7},{7,6},{8,9},{9,8},{10,11... | collective-permute-start | bytes 1572872 | tf_op jit(solution)/shard_map/ppermute | solution.py:548
  94.9 3.9 %shard_map.78.sum_ref = bf16[512,2048]{1,0:T(8,128)(2,1)} custom-call(s32[1]{0:T(128)} %bitcast.here_ref, bf16[512,512]{1,0:T(8,128)(2,1)} %shard_map.77.gated_ref, bf16[1024,4096]{1,0:T(8,128)(2,1)} %refs_4_.1), custom_call_target="tpu_custom_call" | custom-call | flops 1073741824 | bytes 4194304 | tf_op jit(solution)/shard_map/pallas_call | solution.py:72
  98.9 1.0 copy-done
  99.8 1.0 copy-done.1
  100.8 14.6 %collective-permute-done.5.sent_ref = bf16[512,512]{1,0:T(8,128)(2,1)S(1)} collective-permute-done((bf16[512,512]{1,0:T(8,128)(2,1)}, bf16[512,512]{1,0:T(8,128)(2,1)S(1)}, u32[]{:S(2)}, u32[]{:S(2)}) %collective-permute-start.5) | collective-permute-done | bytes 524320 | tf_op jit(solution)/shard_map/ppermute | solution.py:548
  115.4 1.3 %all-to-all-done.2 = bf16[32,32,512]{2,1,0:T(8,128)(2,1)S(1)} async-done(((bf16[32,32,512]{2,1,0:T(8,128)(2,1)}), bf16[32,32,512]{2,1,0:T(8,128)(2,1)S(1)}, u32[]{:S(2)}, u32[]{:S(2)}) %all-to-all-start.2) | async-done | bytes 1048608 | tf_op jit(solution)/shard_map/all_to_all | solution.py:632
  116.6 7.3 %shard_map.79 = bf16[512,2048]{1,0:T(8,128)(2,1)} custom-call(s32[2]{0:T(128)S(1)} %pad_add_fusion.place_ref, bf16[512,512]{1,0:T(8,128)(2,1)S(1)} %collective-permute-done.5.sent_ref, bf16[16,2,32,512]{3,2,1,0:T(8,128)(2,1)S(1)} %bitcast.18, f32[2,8,512]{2,1,0:T(8,128)S(1)} %pad_maximum_fusion.first_ref, bf16[512,2048]{1,0:T(8,128)(2,1)} %shard_map.78.sum_ref, ...), custom_call_target="tpu_custom_call" | custom-call | flops 3221225472 | bytes 10485760 | tf_op jit(solution)/shard_map/pallas_call | solution.py:72
  (33 shorter events, 0.5 us)
Async XLA Ops:
  4.8 7.6 %copy-start.5 = (f32[3,3,1024]{2,1,0:T(4,128)S(1)}, f32[3,3,1024]{2,1,0:T(4,128)}, u32[]{:S(2)}) copy-start(f32[3,3,1024]{2,1,0:T(4,128)} %t_ref.1) | copy-start | bytes 110596
  4.8 49.2 %all-to-all-start = ((bf16[16,65,8,128]{3,2,1,0:T(8,128)(2,1)}), bf16[16,65,8,128]{3,2,1,0:T(8,128)(2,1)S(1)}, u32[]{:S(2)}, u32[]{:S(2)}) async-start(bf16[16,65,8,128]{3,2,1,0:T(8,128)(2,1)} %shard_map.73), calls=%async_computation | async-start | bytes 4259840 | tf_op jit(solution)/shard_map/all_to_all | solution.py:542
  16.0 5.9 %copy-start.6 = (f32[1024]{0:T(1024)S(1)}, f32[1024]{0:T(1024)}, u32[]{:S(2)}) copy-start(f32[1024]{0:T(1024)} %param.10) | copy-start | bytes 12292
  16.0 6.1 %slice-start = ((f32[3,3,1024]{2,1,0:T(4,128)}), f32[3,2,1024]{2,1,0:T(2,128)S(1)}, s32[]{:S(2)}) async-start(f32[3,3,1024]{2,1,0:T(4,128)} %t_ref.1), calls=%async_computation.3 | async-start | bytes 49152 | tf_op jit(solution)/shard_map/slice | solution.py:598
  20.3 14.8 %collective-permute-start.1 = (bf16[512,512]{1,0:T(8,128)(2,1)S(1)}, bf16[512,512]{1,0:T(8,128)(2,1)S(1)}, u32[]{:S(2)}, u32[]{:S(2)}) collective-permute-start(bf16[512,512]{1,0:T(8,128)(2,1)S(1)} %slice.43), channel_id=1, source_target_pairs={{0,1},{1,0},{2,3},{3,2},{4,5},{5,4},{6,7},{7,6},{8,9},{9,8},{10,11... | collective-permute-start | bytes 1572872 | tf_op jit(solution)/shard_map/ppermute | solution.py:548
  24.3 36.3 %collective-permute-start = (bf16[2,1024]{1,0:T(2,128)(2,1)S(1)}, bf16[2,1024]{1,0:T(2,128)(2,1)S(1)}, u32[]{:S(2)}, u32[]{:S(2)}) collective-permute-start(bf16[2,1024]{1,0:T(2,128)(2,1)S(1)} %slice_bitcast_fusion.1), channel_id=1, source_target_pairs={{0,2},{2,4},{4,6},{6,8},{8,10},{10,12},{12,14},{14,16},{16,18},{18... | collective-permute-start | bytes 12296 | tf_op jit(solution)/shard_map/ppermute | solution.py:18
  26.3 54.0 %collective-permute-start.2 = (bf16[1024,512]{1,0:T(8,128)(2,1)}, bf16[1024,512]{1,0:T(8,128)(2,1)}, u32[]{:S(2)}, u32[]{:S(2)}) collective-permute-start(bf16[1024,512]{1,0:T(8,128)(2,1)} %get-tuple-element.39), channel_id=1, source_target_pairs={{0,1},{1,0},{2,3},{3,2},{4,5},{5,4},{6,7},{7,6},{8,9},{9,8},{10,11... | collective-permute-start | bytes 3145736 | tf_op jit(solution)/shard_map/ppermute | solution.py:548
  26.9 53.4 %collective-permute-start.3 = (bf16[1024,512]{1,0:T(8,128)(2,1)}, bf16[1024,512]{1,0:T(8,128)(2,1)}, u32[]{:S(2)}, u32[]{:S(2)}) collective-permute-start(bf16[1024,512]{1,0:T(8,128)(2,1)} %get-tuple-element.40), channel_id=1, source_target_pairs={{0,1},{1,0},{2,3},{3,2},{4,5},{5,4},{6,7},{7,6},{8,9},{9,8},{10,11... | collective-permute-start | bytes 3145736 | tf_op jit(solution)/shard_map/ppermute | solution.py:548
  35.1 25.4 %copy-start.2 = (bf16[512,512]{1,0:T(8,128)(2,1)}, bf16[512,512]{1,0:T(8,128)(2,1)S(1)}, u32[]{:S(2)}) copy-start(bf16[512,512]{1,0:T(8,128)(2,1)S(1)} %collective-permute-done.1.theirs_ref) | copy-start | bytes 1572868
  60.6 25.8 %all-to-all-start.1 = ((bf16[16,32,512]{2,1,0:T(8,128)(2,1)}), bf16[16,32,512]{2,1,0:T(8,128)(2,1)S(1)}, u32[]{:S(2)}, u32[]{:S(2)}) async-start(bf16[16,32,512]{2,1,0:T(8,128)(2,1)} %bitcast.23), calls=%async_computation.1 | async-start | bytes 1048576 | tf_op jit(solution)/shard_map/all_to_all | solution.py:542
  72.0 14.4 %copy-start.3 = (f32[8,1024]{1,0:T(8,128)}, f32[8,1024]{1,0:T(8,128)S(1)}, u32[]{:S(2)}) copy-start(f32[8,1024]{1,0:T(8,128)S(1)} %select_maximum_fusion.first_ref) | copy-start | bytes 98308
  72.0 8.3 %collective-permute-start.4 = (f32[8,512]{1,0:T(8,128)S(1)}, f32[8,512]{1,0:T(8,128)S(1)}, u32[]{:S(2)}, u32[]{:S(2)}) collective-permute-start(f32[8,512]{1,0:T(8,128)S(1)} %slice.46), channel_id=1, source_target_pairs={{0,1},{1,0},{2,3},{3,2},{4,5},{5,4},{6,7},{7,6},{8,9},{9,8},{10,11... | collective-permute-start | bytes 49160 | tf_op jit(solution)/shard_map/ppermute | solution.py:548
  86.4 30.3 %all-to-all-start.2 = ((bf16[32,32,512]{2,1,0:T(8,128)(2,1)}), bf16[32,32,512]{2,1,0:T(8,128)(2,1)S(1)}, u32[]{:S(2)}, u32[]{:S(2)}) async-start(bf16[32,32,512]{2,1,0:T(8,128)(2,1)} %bitcast.22), calls=%async_computation.2 | async-start | bytes 2097152 | tf_op jit(solution)/shard_map/all_to_all | solution.py:632
  90.6 8.2 %collective-permute-start.6 = (bf16[1024,512]{1,0:T(8,128)(2,1)}, bf16[1024,512]{1,0:T(8,128)(2,1)S(1)}, u32[]{:S(2)}, u32[]{:S(2)}) collective-permute-start(bf16[1024,512]{1,0:T(8,128)(2,1)} %collective-permute-done.2.refs_0_), channel_id=1, source_target_pairs={{0,2},{2,0},{4,6},{6,4},{8,10},{10,8},{12,14},{14,12},{16,18},{18,... | collective-permute-start | bytes 3145736 | tf_op jit(solution)/shard_map/ppermute | solution.py:614
  90.7 8.1 %collective-permute-start.7 = (bf16[1024,512]{1,0:T(8,128)(2,1)}, bf16[1024,512]{1,0:T(8,128)(2,1)S(1)}, u32[]{:S(2)}, u32[]{:S(2)}) collective-permute-start(bf16[1024,512]{1,0:T(8,128)(2,1)} %collective-permute-done.3.refs_1_), channel_id=1, source_target_pairs={{0,2},{2,0},{4,6},{6,4},{8,10},{10,8},{12,14},{14,12},{16,18},{18,... | collective-permute-start | bytes 3145736 | tf_op jit(solution)/shard_map/ppermute | solution.py:614
  93.3 22.1 %collective-permute-start.5 = (bf16[512,512]{1,0:T(8,128)(2,1)}, bf16[512,512]{1,0:T(8,128)(2,1)S(1)}, u32[]{:S(2)}, u32[]{:S(2)}) collective-permute-start(bf16[512,512]{1,0:T(8,128)(2,1)} %shard_map.77.gated_ref), channel_id=1, source_target_pairs={{0,1},{1,0},{2,3},{3,2},{4,5},{5,4},{6,7},{7,6},{8,9},{9,8},{10,11... | collective-permute-start | bytes 1572872 | tf_op jit(solution)/shard_map/ppermute | solution.py:548
  94.9 3.9 %copy-start.4 = (f32[8,1024]{1,0:T(8,128)S(1)}, f32[8,1024]{1,0:T(8,128)}, u32[]{:S(2)}) copy-start(f32[8,1024]{1,0:T(8,128)} %copy-done.3) | copy-start | bytes 98308
  98.8 1.0 copy-start
  99.8 1.0 copy-start.1

commit v7 on v6

--- a/solution.py
+++ b/solution.py
@@ -298,11 +298,11 @@
         first = split * (LANES // 2) + place_ref[0] * part
         mine = fix_ref[pl.ds(pl.multiple_of(first, part), part), :]
         lane = lax.broadcasted_iota(jnp.int32, (part, LANES), 1)
+        later = pltpu.roll(mine, LANES - count + 1, 1)
         for block in range(count):
-            one = pltpu.roll(mine, (LANES - block) % LANES, 1)
-            two = pltpu.roll(mine, (LANES - block - count + 1) % LANES, 1)
+            tokens = pltpu.roll(jnp.where(lane == block, mine, later), (LANES - block) % LANES, 1)
             value = x_buf[block, :, :LANES].astype(jnp.float32)
-            value = jnp.where(lane == 0, one, jnp.where(lane == 1, two, value))
+            value = jnp.where(lane < 2, tokens, value)
             x_buf[block, :, :LANES] = value.astype(x_buf.dtype)
     filters = arrived(0)
     odd = lax.broadcasted_iota(jnp.int32, (height, 2 * LANES), 1) % 2 == 1
@@ -495,8 +495,9 @@
         gated_ref[g] = gated_part(long, outer_buf[g], first_ref[g])
     outputs = []
     for k in range(4):
-        for copy in inputs[k]:
-            copy.wait()
+        if k < 3:
+            for copy in inputs[k] + (inputs[3] if k == 2 else []):
+                copy.wait()
         value = sum_buf[k].astype(jnp.float32)
         for left, right in (
             (sent_ref[...], block_buf[k, :used]),

time: 125 us -> 125 us (level)
  no operation moved by 1% of the time
where the time goes in v7:
time: 125 us; the launch traced here: 124 us
  waiting for transfers between devices  47.7 us (38%)
  Pallas kernels  33.6 us (27%)
  starting transfers between devices  32.4 us (26%)
  local copies, waits for them, and re-layouts  9.64 us (8%)
    pallas_call x7, Pallas kernels, run(): return inner(*pinned)  33.6 us
    all_to_all x2, waiting for transfers between devices, exchanged(): return lax.all_to_all(value, 'ctx', 0, 0, tiled=True)  25 us
    ppermute x5, waiting for transfers between devices, to_groups(): lax.ppermute(value, 'ch', [(g, (g + s) % groups) for g in range(groups)])  21.4 us
    all_to_all x2, starting transfers between devices, exchanged(): return lax.all_to_all(value, 'ctx', 0, 0, tiled=True)  18.9 us
    ppermute x5, starting transfers between devices, to_groups(): lax.ppermute(value, 'ch', [(g, (g + s) % groups) for g in range(groups)])  6.81 us
    all_to_all x1, starting transfers between devices, local(): lax.all_to_all(late.reshape(count * groups, step, rows), ('ctx', 'ch'), 0...  4.19 us
    dynamic_slice x1, local copies, waits for them, and re-layouts, local(): lax.dynamic_slice(out_weight, (0, c), (chan, wide))  3.02 us
  transfers between devices with their start and end apart: 11, of which 5 were waited for; matrix products, arithmetic and copies ran while one was open for 6% of the time, Pallas kernels for 18%

profile of v7, /device:TPU:0, one launch (start us, length us, event | category | flops | bytes accessed | tf_op | source)
XLA Modules:
  0.0 123.9 jit_solution(9339592266193324475)
XLA Ops:
  0.0 4.8 %shard_map.73 = bf16[16,65,8,128]{3,2,1,0:T(8,128)(2,1)} custom-call(bf16[512,1024]{1,0:T(8,128)(2,1)} %f_ref.1, bf16[3,512,1024]{2,1,0:T(8,128)(2,1)} %bitcast.19, f32[3,3,1024]{2,1,0:T(4,128)} %t_ref.1), custom_call_target="tpu_custom_call" | custom-call | bytes 5242880 | tf_op jit(solution)/shard_map/pallas_call | solution.py:72
  4.8 7.5 %all-to-all-start = ((bf16[16,65,8,128]{3,2,1,0:T(8,128)(2,1)}), bf16[16,65,8,128]{3,2,1,0:T(8,128)(2,1)S(1)}, u32[]{:S(2)}, u32[]{:S(2)}) async-start(bf16[16,65,8,128]{3,2,1,0:T(8,128)(2,1)} %shard_map.73), calls=%async_computation | async-start | bytes 4259840 | tf_op jit(solution)/shard_map/all_to_all | solution.py:543
  12.4 0.6 slice.34.t_ref
  13.0 3.0 %constant_dynamic-slice_fusion.1 = (bf16[1024,512]{1,0:T(8,128)(2,1)}, bf16[1024,512]{1,0:T(8,128)(2,1)}) fusion(bf16[1024,4096]{1,0:T(8,128)(2,1)} %refs_4_.1, s32[]{:T(128)S(6)} %select_n.32, s32[]{:T(128)S(6)} %select_n.31), kind=kLoop, calls=%fused_computation.11 | loop fusion | bytes 4194312 | tf_op jit(solution)/shard_map/dynamic_slice | solution.py:606
  16.0 0.6 broadcast_in_dim.12.e_ref
  16.6 2.6 %shard_map.74.outer_ref.mine_ref = bf16[512,1024]{1,0:T(8,128)(2,1)} custom-call(bf16[3,512,1024]{2,1,0:T(8,128)(2,1)} %bitcast.20, f32[1,2,1024]{2,1,0:T(2,128)} %broadcast_in_dim.12.e_ref, f32[3,1,1024]{2,1,0:T(1,128)} %slice.34.t_ref), custom_call_target="tpu_custom_call" | custom-call | bytes 2097152 | tf_op jit(solution)/shard_map/pallas_call | solution.py:72
  19.2 1.1 slice.43
  20.3 1.6 %collective-permute-start.1 = (bf16[512,512]{1,0:T(8,128)(2,1)S(1)}, bf16[512,512]{1,0:T(8,128)(2,1)S(1)}, u32[]{:S(2)}, u32[]{:S(2)}) collective-permute-start(bf16[512,512]{1,0:T(8,128)(2,1)S(1)} %slice.43), channel_id=1, source_target_pairs={{0,1},{1,0},{2,3},{3,2},{4,5},{5,4},{6,7},{7,6},{8,9},{9,8},{10,11... | collective-permute-start | bytes 1572872 | tf_op jit(solution)/shard_map/ppermute | solution.py:549
  22.3 0.6 pad.8.taps_ref
  22.9 0.7 broadcast_in_dim.14.skip_ref
  23.6 0.7 slice_bitcast_fusion.1
  24.3 2.0 %collective-permute-start = (bf16[2,1024]{1,0:T(2,128)(2,1)S(1)}, bf16[2,1024]{1,0:T(2,128)(2,1)S(1)}, u32[]{:S(2)}, u32[]{:S(2)}) collective-permute-start(bf16[2,1024]{1,0:T(2,128)(2,1)S(1)} %slice_bitcast_fusion.1), channel_id=1, source_target_pairs={{0,2},{2,4},{4,6},{6,8},{8,10},{10,12},{12,14},{14,16},{16,18},{18... | collective-permute-start | bytes 12296 | tf_op jit(solution)/shard_map/ppermute | solution.py:18
  26.3 0.6 collective-permute-start.2
  26.9 1.5 %collective-permute-start.3 = (bf16[1024,512]{1,0:T(8,128)(2,1)}, bf16[1024,512]{1,0:T(8,128)(2,1)}, u32[]{:S(2)}, u32[]{:S(2)}) collective-permute-start(bf16[1024,512]{1,0:T(8,128)(2,1)} %get-tuple-element.40), channel_id=1, source_target_pairs={{0,1},{1,0},{2,3},{3,2},{4,5},{5,4},{6,7},{7,6},{8,9},{9,8},{10,11... | collective-permute-start | bytes 3145736 | tf_op jit(solution)/shard_map/ppermute | solution.py:549
  28.4 6.8 %collective-permute-done.1.theirs_ref = bf16[512,512]{1,0:T(8,128)(2,1)S(1)} collective-permute-done((bf16[512,512]{1,0:T(8,128)(2,1)S(1)}, bf16[512,512]{1,0:T(8,128)(2,1)S(1)}, u32[]{:S(2)}, u32[]{:S(2)}) %collective-permute-start.1) | collective-permute-done | bytes 524320 | tf_op jit(solution)/shard_map/ppermute | solution.py:549
  35.1 18.9 %all-to-all-done.both_ref = bf16[16,65,8,128]{3,2,1,0:T(8,128)(2,1)S(1)} async-done(((bf16[16,65,8,128]{3,2,1,0:T(8,128)(2,1)}), bf16[16,65,8,128]{3,2,1,0:T(8,128)(2,1)S(1)}, u32[]{:S(2)}, u32[]{:S(2)}) %all-to-all-start) | async-done | bytes 2129952 | tf_op jit(solution)/shard_map/all_to_all | solution.py:543
  54.0 6.5 %shard_map.75 = bf16[16,1,32,512]{3,2,1,0:T(8,128)(2,1)} custom-call(s32[1]{0:T(128)} %bitcast.1.place_ref, bf16[16,65,8,128]{3,2,1,0:T(8,128)(2,1)S(1)} %all-to-all-done.both_ref, bf16[512,1024]{1,0:T(8,128)(2,1)} %constant.62.clone.head_ref, bf16[1024,512]{1,0:T(8,128)(2,1)} %constant.63.clone.back_ref, f32[64,128]{1,0:T(8,128)} %broadcast_in_dim.14.skip_ref, ...), custom_call_target="tpu_custom_call" | custom-call | flops 1610612736 | bytes 2097152 | tf_op jit(solution)/shard_map/pallas_call | solution.py:72
  60.5 11.4 %all-to-all-start.1 = ((bf16[16,32,512]{2,1,0:T(8,128)(2,1)}), bf16[16,32,512]{2,1,0:T(8,128)(2,1)S(1)}, u32[]{:S(2)}, u32[]{:S(2)}) async-start(bf16[16,32,512]{2,1,0:T(8,128)(2,1)} %bitcast.23), calls=%async_computation.1 | async-start | bytes 1048576 | tf_op jit(solution)/shard_map/all_to_all | solution.py:543
  72.0 1.6 %collective-permute-start.4 = (f32[8,512]{1,0:T(8,128)S(1)}, f32[8,512]{1,0:T(8,128)S(1)}, u32[]{:S(2)}, u32[]{:S(2)}) collective-permute-start(f32[8,512]{1,0:T(8,128)S(1)} %slice.46), channel_id=1, source_target_pairs={{0,1},{1,0},{2,3},{3,2},{4,5},{5,4},{6,7},{7,6},{8,9},{9,8},{10,11... | collective-permute-start | bytes 49160 | tf_op jit(solution)/shard_map/ppermute | solution.py:549
  73.5 6.6 %shard_map.76 = bf16[16,2,32,512]{3,2,1,0:T(8,128)(2,1)} custom-call(s32[1]{0:T(128)} %bitcast.1.place_ref, bf16[16,65,8,128]{3,2,1,0:T(8,128)(2,1)S(1)} %all-to-all-done.both_ref, bf16[512,1024]{1,0:T(8,128)(2,1)} %constant.62.clone.head_ref, bf16[1024,512]{1,0:T(8,128)(2,1)} %constant.63.clone.back_ref, f32[64,128]{1,0:T(8,128)} %broadcast_in_dim.14.skip_ref, ...), custom_call_target="tpu_custom_call" | custom-call | flops 1610612736 | bytes 2097152 | tf_op jit(solution)/shard_map/pallas_call | solution.py:72
  80.2 6.1 %all-to-all-done.1.long_ref = bf16[16,32,512]{2,1,0:T(8,128)(2,1)S(1)} async-done(((bf16[16,32,512]{2,1,0:T(8,128)(2,1)}), bf16[16,32,512]{2,1,0:T(8,128)(2,1)S(1)}, u32[]{:S(2)}, u32[]{:S(2)}) %all-to-all-start.1) | async-done | bytes 524320 | tf_op jit(solution)/shard_map/all_to_all | solution.py:543
  86.4 4.2 %all-to-all-start.2 = ((bf16[32,32,512]{2,1,0:T(8,128)(2,1)}), bf16[32,32,512]{2,1,0:T(8,128)(2,1)S(1)}, u32[]{:S(2)}, u32[]{:S(2)}) async-start(bf16[32,32,512]{2,1,0:T(8,128)(2,1)} %bitcast.22), calls=%async_computation.2 | async-start | bytes 2097152 | tf_op jit(solution)/shard_map/all_to_all | solution.py:633
  90.6 0.1 collective-permute-start.6
  90.7 0.4 collective-permute-start.7
  91.1 2.1 %shard_map.77.gated_ref = bf16[512,512]{1,0:T(8,128)(2,1)} custom-call(bf16[16,32,512]{2,1,0:T(8,128)(2,1)S(1)} %all-to-all-done.1.long_ref, bf16[512,1024]{1,0:T(8,128)(2,1)} %shard_map.74.outer_ref.mine_ref, f32[8,1024]{1,0:T(8,128)} %copy-done.3), custom_call_target="tpu_custom_call" | custom-call | bytes 1572864 | tf_op jit(solution)/shard_map/pallas_call | solution.py:72
  93.2 1.6 %collective-permute-start.5 = (bf16[512,512]{1,0:T(8,128)(2,1)}, bf16[512,512]{1,0:T(8,128)(2,1)S(1)}, u32[]{:S(2)}, u32[]{:S(2)}) collective-permute-start(bf16[512,512]{1,0:T(8,128)(2,1)} %shard_map.77.gated_ref), channel_id=1, source_target_pairs={{0,1},{1,0},{2,3},{3,2},{4,5},{5,4},{6,7},{7,6},{8,9},{9,8},{10,11... | collective-permute-start | bytes 1572872 | tf_op jit(solution)/shard_map/ppermute | solution.py:549
  94.9 3.9 %shard_map.78.sum_ref = bf16[512,2048]{1,0:T(8,128)(2,1)} custom-call(s32[1]{0:T(128)} %bitcast.here_ref, bf16[512,512]{1,0:T(8,128)(2,1)} %shard_map.77.gated_ref, bf16[1024,4096]{1,0:T(8,128)(2,1)} %refs_4_.1), custom_call_target="tpu_custom_call" | custom-call | flops 1073741824 | bytes 4194304 | tf_op jit(solution)/shard_map/pallas_call | solution.py:72
  98.8 1.0 copy-done
  99.8 1.0 copy-done.1
  100.8 14.6 %collective-permute-done.5.sent_ref = bf16[512,512]{1,0:T(8,128)(2,1)S(1)} collective-permute-done((bf16[512,512]{1,0:T(8,128)(2,1)}, bf16[512,512]{1,0:T(8,128)(2,1)S(1)}, u32[]{:S(2)}, u32[]{:S(2)}) %collective-permute-start.5) | collective-permute-done | bytes 524320 | tf_op jit(solution)/shard_map/ppermute | solution.py:549
  115.4 1.3 %all-to-all-done.2 = bf16[32,32,512]{2,1,0:T(8,128)(2,1)S(1)} async-done(((bf16[32,32,512]{2,1,0:T(8,128)(2,1)}), bf16[32,32,512]{2,1,0:T(8,128)(2,1)S(1)}, u32[]{:S(2)}, u32[]{:S(2)}) %all-to-all-start.2) | async-done | bytes 1048608 | tf_op jit(solution)/shard_map/all_to_all | solution.py:633
  116.6 7.1 %shard_map.79 = bf16[512,2048]{1,0:T(8,128)(2,1)} custom-call(s32[2]{0:T(128)S(1)} %pad_add_fusion.place_ref, bf16[512,512]{1,0:T(8,128)(2,1)S(1)} %collective-permute-done.5.sent_ref, bf16[16,2,32,512]{3,2,1,0:T(8,128)(2,1)S(1)} %bitcast.18, f32[2,8,512]{2,1,0:T(8,128)S(1)} %pad_maximum_fusion.first_ref, bf16[512,2048]{1,0:T(8,128)(2,1)} %shard_map.78.sum_ref, ...), custom_call_target="tpu_custom_call" | custom-call | flops 3221225472 | bytes 10485760 | tf_op jit(solution)/shard_map/pallas_call | solution.py:72
  (33 shorter events, 0.5 us)
Async XLA Ops:
  4.8 7.6 %copy-start.5 = (f32[3,3,1024]{2,1,0:T(4,128)S(1)}, f32[3,3,1024]{2,1,0:T(4,128)}, u32[]{:S(2)}) copy-start(f32[3,3,1024]{2,1,0:T(4,128)} %t_ref.1) | copy-start | bytes 110596
  4.8 49.2 %all-to-all-start = ((bf16[16,65,8,128]{3,2,1,0:T(8,128)(2,1)}), bf16[16,65,8,128]{3,2,1,0:T(8,128)(2,1)S(1)}, u32[]{:S(2)}, u32[]{:S(2)}) async-start(bf16[16,65,8,128]{3,2,1,0:T(8,128)(2,1)} %shard_map.73), calls=%async_computation | async-start | bytes 4259840 | tf_op jit(solution)/shard_map/all_to_all | solution.py:543
  16.0 5.9 %copy-start.6 = (f32[1024]{0:T(1024)S(1)}, f32[1024]{0:T(1024)}, u32[]{:S(2)}) copy-start(f32[1024]{0:T(1024)} %param.10) | copy-start | bytes 12292
  16.0 6.1 %slice-start = ((f32[3,3,1024]{2,1,0:T(4,128)}), f32[3,2,1024]{2,1,0:T(2,128)S(1)}, s32[]{:S(2)}) async-start(f32[3,3,1024]{2,1,0:T(4,128)} %t_ref.1), calls=%async_computation.3 | async-start | bytes 49152 | tf_op jit(solution)/shard_map/slice | solution.py:599
  20.3 14.8 %collective-permute-start.1 = (bf16[512,512]{1,0:T(8,128)(2,1)S(1)}, bf16[512,512]{1,0:T(8,128)(2,1)S(1)}, u32[]{:S(2)}, u32[]{:S(2)}) collective-permute-start(bf16[512,512]{1,0:T(8,128)(2,1)S(1)} %slice.43), channel_id=1, source_target_pairs={{0,1},{1,0},{2,3},{3,2},{4,5},{5,4},{6,7},{7,6},{8,9},{9,8},{10,11... | collective-permute-start | bytes 1572872 | tf_op jit(solution)/shard_map/ppermute | solution.py:549
  24.3 36.2 %collective-permute-start = (bf16[2,1024]{1,0:T(2,128)(2,1)S(1)}, bf16[2,1024]{1,0:T(2,128)(2,1)S(1)}, u32[]{:S(2)}, u32[]{:S(2)}) collective-permute-start(bf16[2,1024]{1,0:T(2,128)(2,1)S(1)} %slice_bitcast_fusion.1), channel_id=1, source_target_pairs={{0,2},{2,4},{4,6},{6,8},{8,10},{10,12},{12,14},{14,16},{16,18},{18... | collective-permute-start | bytes 12296 | tf_op jit(solution)/shard_map/ppermute | solution.py:18
  26.3 53.9 %collective-permute-start.2 = (bf16[1024,512]{1,0:T(8,128)(2,1)}, bf16[1024,512]{1,0:T(8,128)(2,1)}, u32[]{:S(2)}, u32[]{:S(2)}) collective-permute-start(bf16[1024,512]{1,0:T(8,128)(2,1)} %get-tuple-element.39), channel_id=1, source_target_pairs={{0,1},{1,0},{2,3},{3,2},{4,5},{5,4},{6,7},{7,6},{8,9},{9,8},{10,11... | collective-permute-start | bytes 3145736 | tf_op jit(solution)/shard_map/ppermute | solution.py:549
  26.9 53.3 %collective-permute-start.3 = (bf16[1024,512]{1,0:T(8,128)(2,1)}, bf16[1024,512]{1,0:T(8,128)(2,1)}, u32[]{:S(2)}, u32[]{:S(2)}) collective-permute-start(bf16[1024,512]{1,0:T(8,128)(2,1)} %get-tuple-element.40), channel_id=1, source_target_pairs={{0,1},{1,0},{2,3},{3,2},{4,5},{5,4},{6,7},{7,6},{8,9},{9,8},{10,11... | collective-permute-start | bytes 3145736 | tf_op jit(solution)/shard_map/ppermute | solution.py:549
  35.1 25.4 %copy-start.2 = (bf16[512,512]{1,0:T(8,128)(2,1)}, bf16[512,512]{1,0:T(8,128)(2,1)S(1)}, u32[]{:S(2)}) copy-start(bf16[512,512]{1,0:T(8,128)(2,1)S(1)} %collective-permute-done.1.theirs_ref) | copy-start | bytes 1572868
  60.5 25.8 %all-to-all-start.1 = ((bf16[16,32,512]{2,1,0:T(8,128)(2,1)}), bf16[16,32,512]{2,1,0:T(8,128)(2,1)S(1)}, u32[]{:S(2)}, u32[]{:S(2)}) async-start(bf16[16,32,512]{2,1,0:T(8,128)(2,1)} %bitcast.23), calls=%async_computation.1 | async-start | bytes 1048576 | tf_op jit(solution)/shard_map/all_to_all | solution.py:543
  71.9 14.4 %copy-start.3 = (f32[8,1024]{1,0:T(8,128)}, f32[8,1024]{1,0:T(8,128)S(1)}, u32[]{:S(2)}) copy-start(f32[8,1024]{1,0:T(8,128)S(1)} %select_maximum_fusion.first_ref) | copy-start | bytes 98308
  72.0 8.2 %collective-permute-start.4 = (f32[8,512]{1,0:T(8,128)S(1)}, f32[8,512]{1,0:T(8,128)S(1)}, u32[]{:S(2)}, u32[]{:S(2)}) collective-permute-start(f32[8,512]{1,0:T(8,128)S(1)} %slice.46), channel_id=1, source_target_pairs={{0,1},{1,0},{2,3},{3,2},{4,5},{5,4},{6,7},{7,6},{8,9},{9,8},{10,11... | collective-permute-start | bytes 49160 | tf_op jit(solution)/shard_map/ppermute | solution.py:549
  86.4 30.3 %all-to-all-start.2 = ((bf16[32,32,512]{2,1,0:T(8,128)(2,1)}), bf16[32,32,512]{2,1,0:T(8,128)(2,1)S(1)}, u32[]{:S(2)}, u32[]{:S(2)}) async-start(bf16[32,32,512]{2,1,0:T(8,128)(2,1)} %bitcast.22), calls=%async_computation.2 | async-start | bytes 2097152 | tf_op jit(solution)/shard_map/all_to_all | solution.py:633
  90.6 8.2 %collective-permute-start.6 = (bf16[1024,512]{1,0:T(8,128)(2,1)}, bf16[1024,512]{1,0:T(8,128)(2,1)S(1)}, u32[]{:S(2)}, u32[]{:S(2)}) collective-permute-start(bf16[1024,512]{1,0:T(8,128)(2,1)} %collective-permute-done.2.refs_0_), channel_id=1, source_target_pairs={{0,2},{2,0},{4,6},{6,4},{8,10},{10,8},{12,14},{14,12},{16,18},{18,... | collective-permute-start | bytes 3145736 | tf_op jit(solution)/shard_map/ppermute | solution.py:615
  90.7 8.1 %collective-permute-start.7 = (bf16[1024,512]{1,0:T(8,128)(2,1)}, bf16[1024,512]{1,0:T(8,128)(2,1)S(1)}, u32[]{:S(2)}, u32[]{:S(2)}) collective-permute-start(bf16[1024,512]{1,0:T(8,128)(2,1)} %collective-permute-done.3.refs_1_), channel_id=1, source_target_pairs={{0,2},{2,0},{4,6},{6,4},{8,10},{10,8},{12,14},{14,12},{16,18},{18,... | collective-permute-start | bytes 3145736 | tf_op jit(solution)/shard_map/ppermute | solution.py:615
  93.2 22.1 %collective-permute-start.5 = (bf16[512,512]{1,0:T(8,128)(2,1)}, bf16[512,512]{1,0:T(8,128)(2,1)S(1)}, u32[]{:S(2)}, u32[]{:S(2)}) collective-permute-start(bf16[512,512]{1,0:T(8,128)(2,1)} %shard_map.77.gated_ref), channel_id=1, source_target_pairs={{0,1},{1,0},{2,3},{3,2},{4,5},{5,4},{6,7},{7,6},{8,9},{9,8},{10,11... | collective-permute-start | bytes 1572872 | tf_op jit(solution)/shard_map/ppermute | solution.py:549
  94.9 3.9 %copy-start.4 = (f32[8,1024]{1,0:T(8,128)S(1)}, f32[8,1024]{1,0:T(8,128)}, u32[]{:S(2)}) copy-start(f32[8,1024]{1,0:T(8,128)} %copy-done.3) | copy-start | bytes 98308
  98.8 1.0 copy-start
  99.8 1.0 copy-start.1

commit v8 on v6

--- a/solution.py
+++ b/solution.py
@@ -495,8 +495,9 @@
         gated_ref[g] = gated_part(long, outer_buf[g], first_ref[g])
     outputs = []
     for k in range(4):
-        for copy in inputs[k]:
-            copy.wait()
+        if k < 3:
+            for copy in inputs[k] + (inputs[3] if k == 2 else []):
+                copy.wait()
         value = sum_buf[k].astype(jnp.float32)
         for left, right in (
             (sent_ref[...], block_buf[k, :used]),

time: 125 us -> 125 us (level)
  no operation moved by 1% of the time
where the time goes in v8:
time: 125 us; the launch traced here: 124 us
  waiting for transfers between devices  47.6 us (38%)
  Pallas kernels  33.7 us (27%)
  starting transfers between devices  32.4 us (26%)
  local copies, waits for them, and re-layouts  9.64 us (8%)
    pallas_call x7, Pallas kernels, run(): return inner(*pinned)  33.7 us
    all_to_all x2, waiting for transfers between devices, exchanged(): return lax.all_to_all(value, 'ctx', 0, 0, tiled=True)  25 us
    ppermute x5, waiting for transfers between devices, to_groups(): lax.ppermute(value, 'ch', [(g, (g + s) % groups) for g in range(groups)])  21.4 us
    all_to_all x2, starting transfers between devices, exchanged(): return lax.all_to_all(value, 'ctx', 0, 0, tiled=True)  18.9 us
    ppermute x5, starting transfers between devices, to_groups(): lax.ppermute(value, 'ch', [(g, (g + s) % groups) for g in range(groups)])  6.81 us
    all_to_all x1, starting transfers between devices, local(): lax.all_to_all(late.reshape(count * groups, step, rows), ('ctx', 'ch'), 0...  4.19 us
    dynamic_slice x1, local copies, waits for them, and re-layouts, local(): lax.dynamic_slice(out_weight, (0, c), (chan, wide))  3.02 us
  transfers between devices with their start and end apart: 11, of which 5 were waited for; matrix products, arithmetic and copies ran while one was open for 6% of the time, Pallas kernels for 18%

profile of v8, /device:TPU:0, one launch (start us, length us, event | category | flops | bytes accessed | tf_op | source)
XLA Modules:
  0.0 123.9 jit_solution(1616221437584033788)
XLA Ops:
  0.0 4.8 %shard_map.73 = bf16[16,65,8,128]{3,2,1,0:T(8,128)(2,1)} custom-call(bf16[512,1024]{1,0:T(8,128)(2,1)} %f_ref.1, bf16[3,512,1024]{2,1,0:T(8,128)(2,1)} %bitcast.19, f32[3,3,1024]{2,1,0:T(4,128)} %t_ref.1), custom_call_target="tpu_custom_call" | custom-call | bytes 5242880 | tf_op jit(solution)/shard_map/pallas_call | solution.py:72
  4.8 7.5 %all-to-all-start = ((bf16[16,65,8,128]{3,2,1,0:T(8,128)(2,1)}), bf16[16,65,8,128]{3,2,1,0:T(8,128)(2,1)S(1)}, u32[]{:S(2)}, u32[]{:S(2)}) async-start(bf16[16,65,8,128]{3,2,1,0:T(8,128)(2,1)} %shard_map.73), calls=%async_computation | async-start | bytes 4259840 | tf_op jit(solution)/shard_map/all_to_all | solution.py:543
  12.4 0.6 slice.34.t_ref
  13.0 3.0 %constant_dynamic-slice_fusion.1 = (bf16[1024,512]{1,0:T(8,128)(2,1)}, bf16[1024,512]{1,0:T(8,128)(2,1)}) fusion(bf16[1024,4096]{1,0:T(8,128)(2,1)} %refs_4_.1, s32[]{:T(128)S(6)} %select_n.32, s32[]{:T(128)S(6)} %select_n.31), kind=kLoop, calls=%fused_computation.11 | loop fusion | bytes 4194312 | tf_op jit(solution)/shard_map/dynamic_slice | solution.py:606
  16.0 0.6 broadcast_in_dim.12.e_ref
  16.6 2.6 %shard_map.74.outer_ref.mine_ref = bf16[512,1024]{1,0:T(8,128)(2,1)} custom-call(bf16[3,512,1024]{2,1,0:T(8,128)(2,1)} %bitcast.20, f32[1,2,1024]{2,1,0:T(2,128)} %broadcast_in_dim.12.e_ref, f32[3,1,1024]{2,1,0:T(1,128)} %slice.34.t_ref), custom_call_target="tpu_custom_call" | custom-call | bytes 2097152 | tf_op jit(solution)/shard_map/pallas_call | solution.py:72
  19.2 1.1 slice.43
  20.3 1.6 %collective-permute-start.1 = (bf16[512,512]{1,0:T(8,128)(2,1)S(1)}, bf16[512,512]{1,0:T(8,128)(2,1)S(1)}, u32[]{:S(2)}, u32[]{:S(2)}) collective-permute-start(bf16[512,512]{1,0:T(8,128)(2,1)S(1)} %slice.43), channel_id=1, source_target_pairs={{0,1},{1,0},{2,3},{3,2},{4,5},{5,4},{6,7},{7,6},{8,9},{9,8},{10,11... | collective-permute-start | bytes 1572872 | tf_op jit(solution)/shard_map/ppermute | solution.py:549
  22.3 0.6 pad.8.taps_ref
  22.9 0.7 broadcast_in_dim.14.skip_ref
  23.6 0.7 slice_bitcast_fusion.1
  24.3 2.0 %collective-permute-start = (bf16[2,1024]{1,0:T(2,128)(2,1)S(1)}, bf16[2,1024]{1,0:T(2,128)(2,1)S(1)}, u32[]{:S(2)}, u32[]{:S(2)}) collective-permute-start(bf16[2,1024]{1,0:T(2,128)(2,1)S(1)} %slice_bitcast_fusion.1), channel_id=1, source_target_pairs={{0,2},{2,4},{4,6},{6,8},{8,10},{10,12},{12,14},{14,16},{16,18},{18... | collective-permute-start | bytes 12296 | tf_op jit(solution)/shard_map/ppermute | solution.py:18
  26.3 0.6 collective-permute-start.2
  26.9 1.5 %collective-permute-start.3 = (bf16[1024,512]{1,0:T(8,128)(2,1)}, bf16[1024,512]{1,0:T(8,128)(2,1)}, u32[]{:S(2)}, u32[]{:S(2)}) collective-permute-start(bf16[1024,512]{1,0:T(8,128)(2,1)} %get-tuple-element.40), channel_id=1, source_target_pairs={{0,1},{1,0},{2,3},{3,2},{4,5},{5,4},{6,7},{7,6},{8,9},{9,8},{10,11... | collective-permute-start | bytes 3145736 | tf_op jit(solution)/shard_map/ppermute | solution.py:549
  28.4 6.8 %collective-permute-done.1.theirs_ref = bf16[512,512]{1,0:T(8,128)(2,1)S(1)} collective-permute-done((bf16[512,512]{1,0:T(8,128)(2,1)S(1)}, bf16[512,512]{1,0:T(8,128)(2,1)S(1)}, u32[]{:S(2)}, u32[]{:S(2)}) %collective-permute-start.1) | collective-permute-done | bytes 524320 | tf_op jit(solution)/shard_map/ppermute | solution.py:549
  35.1 18.9 %all-to-all-done.both_ref = bf16[16,65,8,128]{3,2,1,0:T(8,128)(2,1)S(1)} async-done(((bf16[16,65,8,128]{3,2,1,0:T(8,128)(2,1)}), bf16[16,65,8,128]{3,2,1,0:T(8,128)(2,1)S(1)}, u32[]{:S(2)}, u32[]{:S(2)}) %all-to-all-start) | async-done | bytes 2129952 | tf_op jit(solution)/shard_map/all_to_all | solution.py:543
  54.0 6.5 %shard_map.75 = bf16[16,1,32,512]{3,2,1,0:T(8,128)(2,1)} custom-call(s32[1]{0:T(128)} %bitcast.1.place_ref, bf16[16,65,8,128]{3,2,1,0:T(8,128)(2,1)S(1)} %all-to-all-done.both_ref, bf16[512,1024]{1,0:T(8,128)(2,1)} %constant.62.clone.head_ref, bf16[1024,512]{1,0:T(8,128)(2,1)} %constant.63.clone.back_ref, f32[64,128]{1,0:T(8,128)} %broadcast_in_dim.14.skip_ref, ...), custom_call_target="tpu_custom_call" | custom-call | flops 1610612736 | bytes 2097152 | tf_op jit(solution)/shard_map/pallas_call | solution.py:72
  60.6 11.4 %all-to-all-start.1 = ((bf16[16,32,512]{2,1,0:T(8,128)(2,1)}), bf16[16,32,512]{2,1,0:T(8,128)(2,1)S(1)}, u32[]{:S(2)}, u32[]{:S(2)}) async-start(bf16[16,32,512]{2,1,0:T(8,128)(2,1)} %bitcast.23), calls=%async_computation.1 | async-start | bytes 1048576 | tf_op jit(solution)/shard_map/all_to_all | solution.py:543
  72.0 1.6 %collective-permute-start.4 = (f32[8,512]{1,0:T(8,128)S(1)}, f32[8,512]{1,0:T(8,128)S(1)}, u32[]{:S(2)}, u32[]{:S(2)}) collective-permute-start(f32[8,512]{1,0:T(8,128)S(1)} %slice.46), channel_id=1, source_target_pairs={{0,1},{1,0},{2,3},{3,2},{4,5},{5,4},{6,7},{7,6},{8,9},{9,8},{10,11... | collective-permute-start | bytes 49160 | tf_op jit(solution)/shard_map/ppermute | solution.py:549
  73.6 6.7 %shard_map.76 = bf16[16,2,32,512]{3,2,1,0:T(8,128)(2,1)} custom-call(s32[1]{0:T(128)} %bitcast.1.place_ref, bf16[16,65,8,128]{3,2,1,0:T(8,128)(2,1)S(1)} %all-to-all-done.both_ref, bf16[512,1024]{1,0:T(8,128)(2,1)} %constant.62.clone.head_ref, bf16[1024,512]{1,0:T(8,128)(2,1)} %constant.63.clone.back_ref, f32[64,128]{1,0:T(8,128)} %broadcast_in_dim.14.skip_ref, ...), custom_call_target="tpu_custom_call" | custom-call | flops 1610612736 | bytes 2097152 | tf_op jit(solution)/shard_map/pallas_call | solution.py:72
  80.3 6.1 %all-to-all-done.1.long_ref = bf16[16,32,512]{2,1,0:T(8,128)(2,1)S(1)} async-done(((bf16[16,32,512]{2,1,0:T(8,128)(2,1)}), bf16[16,32,512]{2,1,0:T(8,128)(2,1)S(1)}, u32[]{:S(2)}, u32[]{:S(2)}) %all-to-all-start.1) | async-done | bytes 524320 | tf_op jit(solution)/shard_map/all_to_all | solution.py:543
  86.4 4.2 %all-to-all-start.2 = ((bf16[32,32,512]{2,1,0:T(8,128)(2,1)}), bf16[32,32,512]{2,1,0:T(8,128)(2,1)S(1)}, u32[]{:S(2)}, u32[]{:S(2)}) async-start(bf16[32,32,512]{2,1,0:T(8,128)(2,1)} %bitcast.22), calls=%async_computation.2 | async-start | bytes 2097152 | tf_op jit(solution)/shard_map/all_to_all | solution.py:633
  90.6 0.1 collective-permute-start.6
  90.7 0.4 collective-permute-start.7
  91.2 2.1 %shard_map.77.gated_ref = bf16[512,512]{1,0:T(8,128)(2,1)} custom-call(bf16[16,32,512]{2,1,0:T(8,128)(2,1)S(1)} %all-to-all-done.1.long_ref, bf16[512,1024]{1,0:T(8,128)(2,1)} %shard_map.74.outer_ref.mine_ref, f32[8,1024]{1,0:T(8,128)} %copy-done.3), custom_call_target="tpu_custom_call" | custom-call | bytes 1572864 | tf_op jit(solution)/shard_map/pallas_call | solution.py:72
  93.3 1.6 %collective-permute-start.5 = (bf16[512,512]{1,0:T(8,128)(2,1)}, bf16[512,512]{1,0:T(8,128)(2,1)S(1)}, u32[]{:S(2)}, u32[]{:S(2)}) collective-permute-start(bf16[512,512]{1,0:T(8,128)(2,1)} %shard_map.77.gated_ref), channel_id=1, source_target_pairs={{0,1},{1,0},{2,3},{3,2},{4,5},{5,4},{6,7},{7,6},{8,9},{9,8},{10,11... | collective-permute-start | bytes 1572872 | tf_op jit(solution)/shard_map/ppermute | solution.py:549
  94.9 3.9 %shard_map.78.sum_ref = bf16[512,2048]{1,0:T(8,128)(2,1)} custom-call(s32[1]{0:T(128)} %bitcast.here_ref, bf16[512,512]{1,0:T(8,128)(2,1)} %shard_map.77.gated_ref, bf16[1024,4096]{1,0:T(8,128)(2,1)} %refs_4_.1), custom_call_target="tpu_custom_call" | custom-call | flops 1073741824 | bytes 4194304 | tf_op jit(solution)/shard_map/pallas_call | solution.py:72
  98.9 1.0 copy-done
  99.8 1.0 copy-done.1
  100.8 14.6 %collective-permute-done.5.sent_ref = bf16[512,512]{1,0:T(8,128)(2,1)S(1)} collective-permute-done((bf16[512,512]{1,0:T(8,128)(2,1)}, bf16[512,512]{1,0:T(8,128)(2,1)S(1)}, u32[]{:S(2)}, u32[]{:S(2)}) %collective-permute-start.5) | collective-permute-done | bytes 524320 | tf_op jit(solution)/shard_map/ppermute | solution.py:549
  115.4 1.3 %all-to-all-done.2 = bf16[32,32,512]{2,1,0:T(8,128)(2,1)S(1)} async-done(((bf16[32,32,512]{2,1,0:T(8,128)(2,1)}), bf16[32,32,512]{2,1,0:T(8,128)(2,1)S(1)}, u32[]{:S(2)}, u32[]{:S(2)}) %all-to-all-start.2) | async-done | bytes 1048608 | tf_op jit(solution)/shard_map/all_to_all | solution.py:633
  116.6 7.1 %shard_map.79 = bf16[512,2048]{1,0:T(8,128)(2,1)} custom-call(s32[2]{0:T(128)S(1)} %pad_add_fusion.place_ref, bf16[512,512]{1,0:T(8,128)(2,1)S(1)} %collective-permute-done.5.sent_ref, bf16[16,2,32,512]{3,2,1,0:T(8,128)(2,1)S(1)} %bitcast.18, f32[2,8,512]{2,1,0:T(8,128)S(1)} %pad_maximum_fusion.first_ref, bf16[512,2048]{1,0:T(8,128)(2,1)} %shard_map.78.sum_ref, ...), custom_call_target="tpu_custom_call" | custom-call | flops 3221225472 | bytes 10485760 | tf_op jit(solution)/shard_map/pallas_call | solution.py:72
  (33 shorter events, 0.5 us)
Async XLA Ops:
  4.8 7.6 %copy-start.5 = (f32[3,3,1024]{2,1,0:T(4,128)S(1)}, f32[3,3,1024]{2,1,0:T(4,128)}, u32[]{:S(2)}) copy-start(f32[3,3,1024]{2,1,0:T(4,128)} %t_ref.1) | copy-start | bytes 110596
  4.8 49.2 %all-to-all-start = ((bf16[16,65,8,128]{3,2,1,0:T(8,128)(2,1)}), bf16[16,65,8,128]{3,2,1,0:T(8,128)(2,1)S(1)}, u32[]{:S(2)}, u32[]{:S(2)}) async-start(bf16[16,65,8,128]{3,2,1,0:T(8,128)(2,1)} %shard_map.73), calls=%async_computation | async-start | bytes 4259840 | tf_op jit(solution)/shard_map/all_to_all | solution.py:543
  16.0 5.9 %copy-start.6 = (f32[1024]{0:T(1024)S(1)}, f32[1024]{0:T(1024)}, u32[]{:S(2)}) copy-start(f32[1024]{0:T(1024)} %param.10) | copy-start | bytes 12292
  16.0 6.1 %slice-start = ((f32[3,3,1024]{2,1,0:T(4,128)}), f32[3,2,1024]{2,1,0:T(2,128)S(1)}, s32[]{:S(2)}) async-start(f32[3,3,1024]{2,1,0:T(4,128)} %t_ref.1), calls=%async_computation.3 | async-start | bytes 49152 | tf_op jit(solution)/shard_map/slice | solution.py:599
  20.3 14.8 %collective-permute-start.1 = (bf16[512,512]{1,0:T(8,128)(2,1)S(1)}, bf16[512,512]{1,0:T(8,128)(2,1)S(1)}, u32[]{:S(2)}, u32[]{:S(2)}) collective-permute-start(bf16[512,512]{1,0:T(8,128)(2,1)S(1)} %slice.43), channel_id=1, source_target_pairs={{0,1},{1,0},{2,3},{3,2},{4,5},{5,4},{6,7},{7,6},{8,9},{9,8},{10,11... | collective-permute-start | bytes 1572872 | tf_op jit(solution)/shard_map/ppermute | solution.py:549
  24.3 36.3 %collective-permute-start = (bf16[2,1024]{1,0:T(2,128)(2,1)S(1)}, bf16[2,1024]{1,0:T(2,128)(2,1)S(1)}, u32[]{:S(2)}, u32[]{:S(2)}) collective-permute-start(bf16[2,1024]{1,0:T(2,128)(2,1)S(1)} %slice_bitcast_fusion.1), channel_id=1, source_target_pairs={{0,2},{2,4},{4,6},{6,8},{8,10},{10,12},{12,14},{14,16},{16,18},{18... | collective-permute-start | bytes 12296 | tf_op jit(solution)/shard_map/ppermute | solution.py:18
  26.3 54.0 %collective-permute-start.2 = (bf16[1024,512]{1,0:T(8,128)(2,1)}, bf16[1024,512]{1,0:T(8,128)(2,1)}, u32[]{:S(2)}, u32[]{:S(2)}) collective-permute-start(bf16[1024,512]{1,0:T(8,128)(2,1)} %get-tuple-element.39), channel_id=1, source_target_pairs={{0,1},{1,0},{2,3},{3,2},{4,5},{5,4},{6,7},{7,6},{8,9},{9,8},{10,11... | collective-permute-start | bytes 3145736 | tf_op jit(solution)/shard_map/ppermute | solution.py:549
  26.9 53.4 %collective-permute-start.3 = (bf16[1024,512]{1,0:T(8,128)(2,1)}, bf16[1024,512]{1,0:T(8,128)(2,1)}, u32[]{:S(2)}, u32[]{:S(2)}) collective-permute-start(bf16[1024,512]{1,0:T(8,128)(2,1)} %get-tuple-element.40), channel_id=1, source_target_pairs={{0,1},{1,0},{2,3},{3,2},{4,5},{5,4},{6,7},{7,6},{8,9},{9,8},{10,11... | collective-permute-start | bytes 3145736 | tf_op jit(solution)/shard_map/ppermute | solution.py:549
  35.1 25.4 %copy-start.2 = (bf16[512,512]{1,0:T(8,128)(2,1)}, bf16[512,512]{1,0:T(8,128)(2,1)S(1)}, u32[]{:S(2)}) copy-start(bf16[512,512]{1,0:T(8,128)(2,1)S(1)} %collective-permute-done.1.theirs_ref) | copy-start | bytes 1572868
  60.6 25.8 %all-to-all-start.1 = ((bf16[16,32,512]{2,1,0:T(8,128)(2,1)}), bf16[16,32,512]{2,1,0:T(8,128)(2,1)S(1)}, u32[]{:S(2)}, u32[]{:S(2)}) async-start(bf16[16,32,512]{2,1,0:T(8,128)(2,1)} %bitcast.23), calls=%async_computation.1 | async-start | bytes 1048576 | tf_op jit(solution)/shard_map/all_to_all | solution.py:543
  72.0 14.4 %copy-start.3 = (f32[8,1024]{1,0:T(8,128)}, f32[8,1024]{1,0:T(8,128)S(1)}, u32[]{:S(2)}) copy-start(f32[8,1024]{1,0:T(8,128)S(1)} %select_maximum_fusion.first_ref) | copy-start | bytes 98308
  72.0 8.3 %collective-permute-start.4 = (f32[8,512]{1,0:T(8,128)S(1)}, f32[8,512]{1,0:T(8,128)S(1)}, u32[]{:S(2)}, u32[]{:S(2)}) collective-permute-start(f32[8,512]{1,0:T(8,128)S(1)} %slice.46), channel_id=1, source_target_pairs={{0,1},{1,0},{2,3},{3,2},{4,5},{5,4},{6,7},{7,6},{8,9},{9,8},{10,11... | collective-permute-start | bytes 49160 | tf_op jit(solution)/shard_map/ppermute | solution.py:549
  86.4 30.3 %all-to-all-start.2 = ((bf16[32,32,512]{2,1,0:T(8,128)(2,1)}), bf16[32,32,512]{2,1,0:T(8,128)(2,1)S(1)}, u32[]{:S(2)}, u32[]{:S(2)}) async-start(bf16[32,32,512]{2,1,0:T(8,128)(2,1)} %bitcast.22), calls=%async_computation.2 | async-start | bytes 2097152 | tf_op jit(solution)/shard_map/all_to_all | solution.py:633
  90.6 8.2 %collective-permute-start.6 = (bf16[1024,512]{1,0:T(8,128)(2,1)}, bf16[1024,512]{1,0:T(8,128)(2,1)S(1)}, u32[]{:S(2)}, u32[]{:S(2)}) collective-permute-start(bf16[1024,512]{1,0:T(8,128)(2,1)} %collective-permute-done.2.refs_0_), channel_id=1, source_target_pairs={{0,2},{2,0},{4,6},{6,4},{8,10},{10,8},{12,14},{14,12},{16,18},{18,... | collective-permute-start | bytes 3145736 | tf_op jit(solution)/shard_map/ppermute | solution.py:615
  90.7 8.1 %collective-permute-start.7 = (bf16[1024,512]{1,0:T(8,128)(2,1)}, bf16[1024,512]{1,0:T(8,128)(2,1)S(1)}, u32[]{:S(2)}, u32[]{:S(2)}) collective-permute-start(bf16[1024,512]{1,0:T(8,128)(2,1)} %collective-permute-done.3.refs_1_), channel_id=1, source_target_pairs={{0,2},{2,0},{4,6},{6,4},{8,10},{10,8},{12,14},{14,12},{16,18},{18,... | collective-permute-start | bytes 3145736 | tf_op jit(solution)/shard_map/ppermute | solution.py:615
  93.3 22.1 %collective-permute-start.5 = (bf16[512,512]{1,0:T(8,128)(2,1)}, bf16[512,512]{1,0:T(8,128)(2,1)S(1)}, u32[]{:S(2)}, u32[]{:S(2)}) collective-permute-start(bf16[512,512]{1,0:T(8,128)(2,1)} %shard_map.77.gated_ref), channel_id=1, source_target_pairs={{0,1},{1,0},{2,3},{3,2},{4,5},{5,4},{6,7},{7,6},{8,9},{9,8},{10,11... | collective-permute-start | bytes 1572872 | tf_op jit(solution)/shard_map/ppermute | solution.py:549
  94.9 3.9 %copy-start.4 = (f32[8,1024]{1,0:T(8,128)S(1)}, f32[8,1024]{1,0:T(8,128)}, u32[]{:S(2)}) copy-start(f32[8,1024]{1,0:T(8,128)} %copy-done.3) | copy-start | bytes 98308
  98.8 1.0 copy-start
  99.8 1.0 copy-start.1
